TPU v7x, 512 devices: a whole 4x8x8 slice. The times are simulated.
512 devices in a mesh: space: 32 (over z, y_hi), field: 16 (over y_lo, x, core).
Axes of the slice: x: 4, y: 8 (y_hi: 4, y_lo: 2; y = y_hi * 2 + y_lo), z: 8, core: 2. Of those that a mesh axis runs over, the one named last changes fastest.
Arguments:
- phi: float32 [16, 8, 96, 48, 128], P('field', None, 'space'), may hold values from -6 to 6
- velocity: float32 [3, 96, 48, 128], P(None, 'space'), may hold values from -1 to 1
- wiener: float32 [16, 3, 96, 48, 128], P('field', None, 'space'), may hold values from -3 to 3
- diffusivity: float32 [96, 48, 128], P('space'), may hold values from 0.02 to 0.1
- stoich: float32 [8], replicated, may hold values from -1 to 1
Outputs:
- phi_next: float32 [16, 8, 96, 48, 128], P('field', None, 'space')
All inputs are finite; a program needn't handle non-finite values.
Results may differ from a plain program's by a relative error of at most 0.00002.
Values sent between devices are 32-bit elements; how exact they have to be, the bound alone decides.
No kernel may reach another device: no remote copies, remote signals or barrier semaphores. Data moves between devices by JAX's collectives and lax.ppermute only.
A program may use at most 64 MiB of HBM per device.

v0:
```python
import jax
import jax.numpy as jnp
from jax import lax
from jax.sharding import PartitionSpec as P

time_step = 0.3
mix_const = 5.0
pre_factor = 2.0
activation = 2.0


def with_halo(cells, sides, width):
    for axis, dim in sides:
        count = lax.axis_size(axis)
        ends = count - 1
        head = lax.slice_in_dim(cells, 0, width, axis=dim)
        tail = lax.slice_in_dim(cells, cells.shape[dim] - width, cells.shape[dim], axis=dim)
        cells = jnp.concatenate(
            [
                lax.ppermute(tail, axis, [(i, (i + 1) % count) for i in range(ends)]),
                cells,
                lax.ppermute(head, axis, [((i + 1) % count, i) for i in range(ends)]),
            ],
            axis=dim,
        )
    return cells


def stencil(padded, num_cells):

    def along_x(k):
        return padded[:, 3 + k : 3 + k + num_cells]

    centre = along_x(0)

    def along_y(k):
        return jnp.roll(centre, -k, axis=2)

    def along_z(k):
        return jnp.roll(centre, -k, axis=3)

    def derivative(g):
        return (45.0 * (g(1) - g(-1)) - 9.0 * (g(2) - g(-2)) + (g(3) - g(-3))) / 60.0

    laplace = (
        along_x(1)
        + along_x(-1)
        + along_y(1)
        + along_y(-1)
        + along_z(1)
        + along_z(-1)
        - 6.0 * centre
    )
    return (centre, derivative(along_x), derivative(along_y), derivative(along_z), laplace)


def increment(padded, velocity, wiener, diffusion, field_mean, amplitude, stoich):
    centre, grad_x, grad_y, grad_z, laplace = stencil(padded, velocity.shape[1])
    advect = -(velocity[0] * grad_x + velocity[1] * grad_y + velocity[2] * grad_z)
    noise_term = amplitude * (wiener[0] * grad_x + wiener[1] * grad_y + wiener[2] * grad_z)
    mixing = -mix_const * diffusion * (centre - field_mean)
    theta_cell = 1.0 + 3.0 * jax.nn.sigmoid(centre[7])
    arrhenius = pre_factor * centre[0] * centre[1] * jnp.exp(-activation / theta_cell)
    reaction = stoich[:, None, None, None] * arrhenius
    return centre + time_step * (advect + diffusion * laplace + mixing + reaction) + noise_term


def local(phi, velocity, wiener, diffusivity, stoich):
    fields_total = phi.shape[0] * lax.axis_size("field")

    def mean_parts(state):
        local_total = jnp.sum(state, axis=0)
        summed = lax.psum(local_total, "field")
        field_mean = summed / fields_total
        amplitude = jnp.sqrt(2.0 * diffusivity * (1.0 + 3.0 * jax.nn.sigmoid(field_mean[7])))
        return (field_mean, amplitude)

    def advance(state):
        field_mean, amplitude = mean_parts(state)
        padded = with_halo(state, (("space", 2),), 3)
        return jax.vmap(
            lambda p, w: increment(p, velocity, w, diffusivity, field_mean, amplitude, stoich)
        )(padded, wiener)

    first = advance(phi)
    second = advance(first)
    return 0.5 * phi + 0.5 * second


def solution(mesh):
    return jax.shard_map(
        local,
        mesh=mesh,
        in_specs=(
            P("field", None, "space", None, None),
            P(None, "space", None, None),
            P("field", None, "space", None, None),
            P("space", None, None),
            P(),
        ),
        out_specs=P("field", None, "space", None, None),
        check_vma=False,
    )
```

profile of v0, /device:TPU:7, one launch (start us, length us, event | category | flops | bytes accessed | tf_op | source)
XLA Modules:
  0.0 339.3 jit_solution(7242187162504446687)
XLA Ops:
  6.5 0.0 all-reduce.3.cloned.1.call-start
  6.5 4.4 %collective-permute-start.1 = (f32[1,8,3,48,128]{4,3,2,1,0:T(8,128)}, f32[1,8,3,48,128]{4,3,2,1,0:T(8,128)S(1)}, u32[]{:S(2)}, u32[]{:S(2)}) collective-permute-start(f32[1,8,3,48,128]{4,3,2,1,0:T(8,128)} %param.5), channel_id=1, source_target_pairs={{0,16},{16,32},{32,48},{48,64},{64,80},{80,96},{96,112},{112,128},... | collective-permute-start | bytes 1769480 | tf_op jit(solution)/shard_map/ppermute | solution.py:20
  10.9 1.3 collective-permute-start
  12.2 0.0 all-reduce.3.cloned.1.call-update
  12.2 0.0 all-reduce.5.cloned.1.call-start
  12.3 1.6 fusion.77
  13.9 0.0 copy-done
  13.9 1.2 fusion.78
  15.1 1.2 fusion.83
  16.3 1.2 fusion.81
  17.5 1.1 fusion.76
  18.6 1.2 fusion.80
  19.8 1.2 fusion.82
  20.9 1.2 fusion.74
  22.1 1.2 fusion.79
  23.3 0.0 copy-done.15
  23.3 0.7 multiply_bitcast_fusion.6
  24.0 0.0 copy-done.16
  24.0 0.7 multiply_bitcast_fusion.2
  24.7 0.6 fusion.75
  25.4 0.6 fusion.73
  26.0 1.1 fusion.72
  27.1 0.6 collective-permute-done.1
  27.8 0.1 constant_dynamic-update-slice_fusion.1
  27.9 0.0 copy-start.21
  27.9 129.0 %all-reduce.3.cloned.1.call-done = f32[8,3,48,128]{3,2,1,0:T(8,128)} async-done(((f32[8,3,48,128]{3,2,1,0:T(8,128)}), f32[8,3,48,128]{3,2,1,0:T(8,128)}) %all-reduce.3.cloned.1.call-update) | async-done | bytes 589840 | tf_op jit(solution)/shard_map/psum | solution.py:73
  156.9 0.0 copy-start.9
  156.9 0.0 copy-start.11
  156.9 0.0 copy-start.13
  156.9 0.0 copy-start.17
  156.9 0.0 copy-start.20
  156.9 1.3 broadcast_multiply_fusion.1
  158.2 0.9 broadcast_multiply_fusion.2
  159.1 0.0 copy-start.14
  159.1 0.0 collective-permute-done
  159.1 1.1 constant_dynamic-update-slice_fusion
  160.3 0.0 copy-done.21
  160.3 0.0 copy-done.3
  160.3 0.0 copy-done.4
  160.3 0.0 copy-done.5
  160.3 0.0 copy-done.6
  160.4 5.6 %fusion.34 = f32[1,8,3,48,128]{4,3,2,1,0:T(8,128)} fusion(f32[1,8,3,48,128]{4,3,2,1,0:T(8,128)S(1)} %copy-done, f32[1,8,3,48,125]{4,3,2,1,0:T(8,128)} %get-tuple-element.52, f32[1,8,3,48,3]{4,3,2,1,0:T(8,128)} %get-tuple-element.54, f32[1,8,3,48,3]{4,3,2,1,0:T(8,128)S(1)} %copy-done.6, f32[1,8,3,48,125]{4,3,2,1,0:T(8,128)} %get-tuple-element.51, ...), kind=kLoop, calls=%fused_computation.59 | loop fusion | flops 9289728 | bytes 13123616 | tf_op jit(solution)/shard_map/vmap()/add | solution.py:65
  166.1 1.6 fusion.63
  167.6 1.6 fusion.59
  169.3 4.8 %collective-permute-start.3 = (f32[1,8,3,48,128]{4,3,2,1,0:T(8,128)}, f32[1,8,3,48,128]{4,3,2,1,0:T(8,128)}, u32[]{:S(2)}, u32[]{:S(2)}) collective-permute-start(f32[1,8,3,48,128]{4,3,2,1,0:T(8,128)} %fusion.34), channel_id=1, source_target_pairs={{0,16},{16,32},{32,48},{48,64},{64,80},{80,96},{96,112},{112,128},... | collective-permute-start | bytes 1769480 | tf_op jit(solution)/shard_map/ppermute | solution.py:20
  174.1 1.3 collective-permute-start.2
  175.4 1.5 fusion.66
  176.9 1.5 fusion.71
  178.3 2.3 fusion.69
  180.6 2.4 fusion.64
  183.0 2.5 fusion.68
  185.5 2.5 fusion.70
  187.9 2.4 fusion.62
  190.3 2.4 fusion.67
  192.8 0.0 all-reduce.5.cloned.1.call-update
  192.8 1.6 fusion.65
  194.4 2.4 fusion.60
  196.8 1.6 fusion.61
  198.3 125.5 %all-reduce.5.cloned.1.call-done = f32[8,3,48,128]{3,2,1,0:T(8,128)} async-done(((f32[8,3,48,128]{3,2,1,0:T(8,128)}), f32[8,3,48,128]{3,2,1,0:T(8,128)}) %all-reduce.5.cloned.1.call-update) | async-done | bytes 589840 | tf_op jit(solution)/shard_map/psum | solution.py:73
  323.8 1.2 broadcast_multiply_fusion
  325.0 0.9 fusion.58
  326.0 0.0 collective-permute-done.3
  326.0 0.0 collective-permute-done.2
  326.1 6.4 %fusion.28 = f32[1,8,3,48,128]{4,3,2,1,0:T(8,128)} fusion(f32[1,8,3,48,128]{4,3,2,1,0:T(8,128)S(1)} %copy-done, f32[1,8,3,48,128]{4,3,2,1,0:T(8,128)} %fusion.34, f32[1,8,3,48,125]{4,3,2,1,0:T(8,128)} %get-tuple-element.26, f32[1,8,3,48,3]{4,3,2,1,0:T(8,128)S(1)} %get-tuple-element.28, f32[1,8,3,48,3]{4,3,2,1,0:T(8,128)S(1)} %get-tuple-element.27, ...), kind=kLoop, calls=%fused_computation.52 | loop fusion | flops 10174464 | bytes 11354144 | tf_op jit(solution)/shard_map/add | solution.py:87
  (30 shorter events, 0.1 us)
Async XLA Ops:
  6.5 7.4 %copy-start = (f32[1,8,3,48,128]{4,3,2,1,0:T(8,128)S(1)}, f32[1,8,3,48,128]{4,3,2,1,0:T(8,128)}, u32[]{:S(2)}) copy-start(f32[1,8,3,48,128]{4,3,2,1,0:T(8,128)} %param.5) | copy-start | bytes 1769476
  6.5 150.3 %all-reduce.3.cloned.1.call-start = ((), (), s32[]{:S(2)}) async-start(), calls=%async_computation | async-start | bytes 1179648 | tf_op jit(solution)/shard_map/psum | solution.py:73
  6.5 21.2 %collective-permute-start.1 = (f32[1,8,3,48,128]{4,3,2,1,0:T(8,128)}, f32[1,8,3,48,128]{4,3,2,1,0:T(8,128)S(1)}, u32[]{:S(2)}, u32[]{:S(2)}) collective-permute-start(f32[1,8,3,48,128]{4,3,2,1,0:T(8,128)} %param.5), channel_id=1, source_target_pairs={{0,16},{16,32},{32,48},{48,64},{64,80},{80,96},{96,112},{112,128},... | collective-permute-start | bytes 1769480 | tf_op jit(solution)/shard_map/ppermute | solution.py:20
  10.9 148.2 %collective-permute-start = (f32[1,8,3,48,128]{4,3,2,1,0:T(8,128)}, f32[1,8,3,48,128]{4,3,2,1,0:T(8,128)}, u32[]{:S(2)}, u32[]{:S(2)}) collective-permute-start(f32[1,8,3,48,128]{4,3,2,1,0:T(8,128)} %param.5), channel_id=1, source_target_pairs={{16,0},{32,16},{48,32},{64,48},{80,64},{96,80},{112,96},{128,112},... | collective-permute-start | bytes 1769480 | tf_op jit(solution)/shard_map/ppermute | solution.py:22
  12.2 311.5 %all-reduce.5.cloned.1.call-start = ((), (), s32[]{:S(2)}) async-start(), calls=%async_computation.1 | async-start | bytes 1179648 | tf_op jit(solution)/shard_map/psum | solution.py:73
  22.1 1.2 copy-start.15
  22.1 1.9 copy-start.16
  27.9 132.4 %copy-start.21 = (f32[8]{0:T(128)S(1)}, f32[8]{0:T(128)}, u32[]{:S(2)}) copy-start(f32[8]{0:T(128)} %param.9) | copy-start | bytes 100
  156.9 3.4 %copy-start.3 = (f32[8,3,48,128]{3,2,1,0:T(8,128)S(1)}, f32[8,3,48,128]{3,2,1,0:T(8,128)}, u32[]{:S(2)}) copy-start(f32[8,3,48,128]{3,2,1,0:T(8,128)} %all-reduce.3.cloned.1.call-done) | copy-start | bytes 1769476
  156.9 3.5 %copy-start.4 = (f32[1,8,3,48,127]{4,3,2,1,0:T(8,128)S(1)}, f32[1,8,3,48,127]{4,3,2,1,0:T(8,128)}, u32[]{:S(2)}) copy-start(f32[1,8,3,48,127]{4,3,2,1,0:T(8,128)} %get-tuple-element.43) | copy-start | bytes 1755652
  156.9 3.5 %copy-start.5 = (f32[1,8,3,48,127]{4,3,2,1,0:T(8,128)S(1)}, f32[1,8,3,48,127]{4,3,2,1,0:T(8,128)}, u32[]{:S(2)}) copy-start(f32[1,8,3,48,127]{4,3,2,1,0:T(8,128)} %get-tuple-element.44) | copy-start | bytes 1755652
  156.9 3.5 %copy-start.6 = (f32[1,8,3,48,3]{4,3,2,1,0:T(8,128)S(1)}, f32[1,8,3,48,3]{4,3,2,1,0:T(8,128)}, u32[]{:S(2)}) copy-start(f32[1,8,3,48,3]{4,3,2,1,0:T(8,128)} %get-tuple-element.53) | copy-start | bytes 41476
  156.9 3.5 %copy-start.7 = (f32[3,48,128]{2,1,0:T(8,128)S(1)}, f32[3,48,128]{2,1,0:T(8,128)}, u32[]{:S(2)}) copy-start(f32[3,48,128]{2,1,0:T(8,128)} %param.8) | copy-start | bytes 221188
  156.9 3.5 %copy-start.9 = (f32[3,48,128]{2,1,0:T(8,128)S(1)}, f32[3,48,128]{2,1,0:T(8,128)}, u32[]{:S(2)}) copy-start(f32[3,48,128]{2,1,0:T(8,128)} %get-tuple-element.58) | copy-start | bytes 221188
  156.9 3.5 %copy-start.11 = (f32[3,48,128]{2,1,0:T(8,128)S(1)}, f32[3,48,128]{2,1,0:T(8,128)}, u32[]{:S(2)}) copy-start(f32[3,48,128]{2,1,0:T(8,128)} %get-tuple-element.59) | copy-start | bytes 221188
  156.9 3.5 %copy-start.13 = (f32[3,48,128]{2,1,0:T(8,128)S(1)}, f32[3,48,128]{2,1,0:T(8,128)}, u32[]{:S(2)}) copy-start(f32[3,48,128]{2,1,0:T(8,128)} %get-tuple-element.60) | copy-start | bytes 221188
  156.9 3.5 %copy-start.17 = (f32[1,8,3,3,128]{4,3,2,1,0:T(4,128)S(1)}, f32[1,8,3,3,128]{4,3,2,1,0:T(4,128)}, u32[]{:S(2)}) copy-start(f32[1,8,3,3,128]{4,3,2,1,0:T(4,128)} %get-tuple-element.41) | copy-start | bytes 110596
  156.9 3.5 %copy-start.20 = (f32[1,8,3,1,128]{4,3,2,1,0:T(1,128)S(1)}, f32[1,8,3,1,128]{4,3,2,1,0:T(1,128)}, u32[]{:S(2)}) copy-start(f32[1,8,3,1,128]{4,3,2,1,0:T(1,128)} %get-tuple-element.34) | copy-start | bytes 36868
  159.1 6.9 %copy-start.14 = (f32[3,48,128]{2,1,0:T(8,128)}, f32[3,48,128]{2,1,0:T(8,128)S(1)}, u32[]{:S(2)}) copy-start(f32[3,48,128]{2,1,0:T(8,128)S(1)} %get-tuple-element.61) | copy-start | bytes 221188
  169.3 156.7 %collective-permute-start.3 = (f32[1,8,3,48,128]{4,3,2,1,0:T(8,128)}, f32[1,8,3,48,128]{4,3,2,1,0:T(8,128)}, u32[]{:S(2)}, u32[]{:S(2)}) collective-permute-start(f32[1,8,3,48,128]{4,3,2,1,0:T(8,128)} %fusion.34), channel_id=1, source_target_pairs={{0,16},{16,32},{32,48},{48,64},{64,80},{80,96},{96,112},{112,128},... | collective-permute-start | bytes 1769480 | tf_op jit(solution)/shard_map/ppermute | solution.py:20
  174.1 151.9 %collective-permute-start.2 = (f32[1,8,3,48,128]{4,3,2,1,0:T(8,128)}, f32[1,8,3,48,128]{4,3,2,1,0:T(8,128)}, u32[]{:S(2)}, u32[]{:S(2)}) collective-permute-start(f32[1,8,3,48,128]{4,3,2,1,0:T(8,128)} %fusion.34), channel_id=1, source_target_pairs={{16,0},{32,16},{48,32},{64,48},{80,64},{96,80},{112,96},{128,112},... | collective-permute-start | bytes 1769480 | tf_op jit(solution)/shard_map/ppermute | solution.py:22
  323.8 2.2 copy-start.1
  323.8 2.2 copy-start.2
  323.8 2.2 copy-start.8
  323.8 2.2 copy-start.10
  323.8 2.2 copy-start.12
  323.8 2.2 copy-start.18
  323.8 2.2 copy-start.19
Sparse Core Ops, SparseCore 0:
  12.4 144.4 all-reduce.2
  192.9 130.8 all-reduce.4
where the time goes:
time: 340 us; the launch traced here: 339 us
  waiting for transfers between devices  255 us (75%)
  local copies, waits for them, and re-layouts  39.2 us (12%)
  other arithmetic  19.4 us (6%)
  between operations  13.8 us (4%)
  starting transfers between devices  11.8 us (3%)
    psum x2, waiting for transfers between devices, mean_parts(): summed = lax.psum(local_total, 'field')  254 us
    slice x12, local copies, waits for them, and re-layouts, along_z(): return jnp.roll(centre, -k, axis=3)  19.8 us
    slice x12, local copies, waits for them, and re-layouts, along_y(): return jnp.roll(centre, -k, axis=2)  18.1 us
    ppermute x2, starting transfers between devices, with_halo(): lax.ppermute(tail, axis, [(i, (i + 1) % count) for i in range(ends)])  9.2 us
  transfers between devices with their start and end apart: 6, of which 3 were waited for; matrix products, arithmetic and copies ran while one was open for 12% of the time, Pallas kernels for 0%

commit v1 on v0

v1 whole, which is shorter than its diff:
```python
import functools

import jax
import jax.numpy as jnp
from jax import lax
from jax.experimental import pallas as pl
from jax.experimental.pallas import tpu as pltpu
from jax.sharding import PartitionSpec as P

time_step = 0.3
mix_const = 5.0
pre_factor = 2.0
activation = 2.0


def sigmoid(x):
    return 1.0 / (1.0 + jnp.exp(-x))


def section_kernel(fields, last, stoich_ref, q_ref, low_ref, high_ref, vel_ref, wie_ref, dif_ref, sum_ref, *rest):
    if last:
        base_ref, out_ref, coef, react = rest
    else:
        out_ref, coef, react = rest
    scalars, planes = q_ref.shape[:2]

    for i in range(planes):
        dif = dif_ref[i]
        theta_bar = 1.0 + 3.0 * sigmoid(sum_ref[scalars - 1, i] / fields)
        amplitude = jnp.sqrt(2.0 * dif * theta_bar)
        for d in range(3):
            coef[d, i] = amplitude * wie_ref[d, i] - time_step * vel_ref[d, i]
        theta = 1.0 + 3.0 * sigmoid(q_ref[scalars - 1, i])
        react[i] = (time_step * pre_factor) * q_ref[0, i] * q_ref[1, i] * jnp.exp(-activation / theta)

    def one(s, carry):
        for i in range(planes):

            def along_x(k):
                j = i + k
                if j < 0:
                    return low_ref[s, j + planes]
                if j >= planes:
                    return high_ref[s, j - planes]
                return q_ref[s, j]

            q = q_ref[s, i]
            rows, lanes = q.shape
            near = None
            grown = None
            for d in range(3):
                if d == 0:
                    at = along_x
                else:
                    size = (rows, lanes)[d - 1]
                    at = lambda k, d=d, size=size: pltpu.roll(q, (-k) % size, d - 1)
                up, down = at(1), at(-1)
                slope = 0.75 * (up - down) - 0.15 * (at(2) - at(-2)) + (1.0 / 60.0) * (at(3) - at(-3))
                term = coef[d, i] * slope
                pair = up + down
                near = pair if near is None else near + pair
                grown = term if grown is None else grown + term
            smooth = near - 6.0 * q - mix_const * (q - sum_ref[s, i] * (1.0 / fields))
            new = q + (grown + time_step * dif_ref[i] * smooth + stoich_ref[s] * react[i])
            if last:
                new = 0.5 * base_ref[s, i] + 0.5 * new
            out_ref[s, i] = new
        return carry

    lax.fori_loop(0, scalars, one, 0)


def section(fields, stoich, q, low, high, velocity, wiener, diffusivity, total, base=None):
    last = base is not None
    planes, rows, lanes = q.shape[1:]
    vmem = pl.BlockSpec(memory_space=pltpu.VMEM)
    args = (q, low, high, velocity, wiener, diffusivity, total) + ((base,) if last else ())
    return pl.pallas_call(
        functools.partial(section_kernel, fields, last),
        out_shape=jax.ShapeDtypeStruct(q.shape, q.dtype),
        in_specs=[pl.BlockSpec(memory_space=pltpu.SMEM)] + [vmem] * len(args),
        out_specs=vmem,
        scratch_shapes=[
            pltpu.VMEM((3, planes, rows, lanes), jnp.float32),
            pltpu.VMEM((planes, rows, lanes), jnp.float32),
        ],
        compiler_params=pltpu.CompilerParams(vmem_limit_bytes=16 * 2**20),
        cost_estimate=pl.CostEstimate(flops=80 * q.size, bytes_accessed=24 * q.size, transcendentals=q.size // 8),
        name="section_last" if last else "section_first",
    )(stoich, *args)


def field_sum(q):
    count = lax.axis_size("field")
    shares = q.reshape(count, -1, 8, q.shape[-1])
    share = jnp.sum(lax.all_to_all(shares, "field", 0, 0), axis=0)
    whole = lax.all_to_all(jnp.broadcast_to(share, shares.shape), "field", 0, 0)
    return whole.reshape(q.shape)


def neighbours(q):
    count = lax.axis_size("space")
    low = lax.ppermute(q, "space", [(i, i + 1) for i in range(count - 1)])
    high = lax.ppermute(q, "space", [(i + 1, i) for i in range(count - 1)])
    return low, high


def local(phi, velocity, wiener, diffusivity, stoich):
    fields = phi.shape[0] * lax.axis_size("field")
    phi, wiener = phi[0], wiener[0]
    low, high = neighbours(phi)
    first = section(fields, stoich, phi, low, high, velocity, wiener, diffusivity, field_sum(phi))
    low, high = neighbours(first)
    out = section(fields, stoich, first, low, high, velocity, wiener, diffusivity, field_sum(first), phi)
    return out[None]


def solution(mesh):
    return jax.shard_map(
        local,
        mesh=mesh,
        in_specs=(
            P("field", None, "space", None, None),
            P(None, "space", None, None),
            P("field", None, "space", None, None),
            P("space", None, None),
            P(),
        ),
        out_specs=P("field", None, "space", None, None),
        check_vma=False,
    )
```

time: 340 us -> 125 us (0.37)
  the two profiles are of different devices: /device:TPU:7 before, /device:TPU:267 now
where the time goes in v1:
time: 125 us
  waiting for transfers between devices  62.1 us (50%)
  blocking collectives  30.2 us (24%)
  starting transfers between devices  24.2 us (19%)
  Pallas kernels  5.45 us (4%)
  local copies, waits for them, and re-layouts  2.35 us (2%)
    ppermute x2, waiting for transfers between devices, neighbours(): high = lax.ppermute(q, 'space', [(i + 1, i) for i in range(count - 1)])  54.9 us
    all_to_all x2, blocking collectives, field_sum(): share = jnp.sum(lax.all_to_all(shares, 'field', 0, 0), axis=0)  30.2 us
    all_to_all x2, starting transfers between devices, field_sum(): whole = lax.all_to_all(jnp.broadcast_to(share, shares.shape), 'field', 0, 0)  11.9 us
    ppermute x2, waiting for transfers between devices, neighbours(): low = lax.ppermute(q, 'space', [(i, i + 1) for i in range(count - 1)])  7.19 us
    ppermute x2, starting transfers between devices, neighbours(): high = lax.ppermute(q, 'space', [(i + 1, i) for i in range(count - 1)])  6.57 us
    ppermute x2, starting transfers between devices, neighbours(): low = lax.ppermute(q, 'space', [(i, i + 1) for i in range(count - 1)])  5.78 us
    pallas_call x2, Pallas kernels, section(): pl.pallas_call(functools.partial(section_kernel, fields, last), out_shape...  5.45 us
  transfers between devices with their start and end apart: 6, of which 4 were waited for; matrix products, arithmetic and copies ran while one was open for 0% of the time, Pallas kernels for 0%

profile of v1, /device:TPU:267, one launch (start us, length us, event | category | flops | bytes accessed | tf_op | source)
XLA Modules:
  0.0 124.5 jit_solution(15055190220924040044)
XLA Ops:
  0.0 15.3 %all_to_all.20 = f32[16,9,8,128]{3,2,1,0:T(8,128)S(1)} all-to-all(f32[16,9,8,128]{3,2,1,0:T(8,128)} %bitcast.7), channel_id=1, replica_groups=mesh['space'=32,'field'=16] {'field'}, dimensions={0} | all-to-all | bytes 1179648 | tf_op jit(solution)/shard_map/all_to_all | solution.py:96
  15.3 0.9 broadcast_in_dim.9
  16.2 0.0 copy-start
  16.2 0.0 copy-start.1
  16.2 0.0 copy-start.2
  16.2 0.0 copy-start.3
  16.2 6.0 %all-to-all-start.1 = ((f32[16,9,8,128]{3,2,1,0:T(8,128)}), f32[16,9,8,128]{3,2,1,0:T(8,128)S(1)}, u32[]{:S(2)}, u32[]{:S(2)}) async-start(f32[16,9,8,128]{3,2,1,0:T(8,128)} %broadcast_in_dim.9), calls=%async_computation.1 | async-start | bytes 1179648 | tf_op jit(solution)/shard_map/all_to_all | solution.py:97
  22.2 0.0 copy-done
  22.2 4.1 %collective-permute-start.1 = (f32[8,3,48,128]{3,2,1,0:T(8,128)S(1)}, f32[8,3,48,128]{3,2,1,0:T(8,128)S(1)}, u32[]{:S(2)}, u32[]{:S(2)}) collective-permute-start(f32[8,3,48,128]{3,2,1,0:T(8,128)S(1)} %bitcast.8), channel_id=1, source_target_pairs={{16,0},{32,16},{48,32},{64,48},{80,64},{96,80},{112,96},{128,112},... | collective-permute-start | bytes 1769480 | tf_op jit(solution)/shard_map/ppermute | solution.py:104
  26.3 2.1 %collective-permute-start = (f32[8,3,48,128]{3,2,1,0:T(8,128)S(1)}, f32[8,3,48,128]{3,2,1,0:T(8,128)S(1)}, u32[]{:S(2)}, u32[]{:S(2)}) collective-permute-start(f32[8,3,48,128]{3,2,1,0:T(8,128)S(1)} %bitcast.9), channel_id=1, source_target_pairs={{0,16},{16,32},{32,48},{48,64},{64,80},{80,96},{96,112},{112,128},... | collective-permute-start | bytes 1769480 | tf_op jit(solution)/shard_map/ppermute | solution.py:103
  28.4 28.7 %collective-permute-done.1.high_ref = f32[8,3,48,128]{3,2,1,0:T(8,128)S(1)} collective-permute-done((f32[8,3,48,128]{3,2,1,0:T(8,128)S(1)}, f32[8,3,48,128]{3,2,1,0:T(8,128)S(1)}, u32[]{:S(2)}, u32[]{:S(2)}) %collective-permute-start.1) | collective-permute-done | bytes 589856 | tf_op jit(solution)/shard_map/ppermute | solution.py:104
  57.1 3.2 %collective-permute-done.low_ref = f32[8,3,48,128]{3,2,1,0:T(8,128)S(1)} collective-permute-done((f32[8,3,48,128]{3,2,1,0:T(8,128)S(1)}, f32[8,3,48,128]{3,2,1,0:T(8,128)S(1)}, u32[]{:S(2)}, u32[]{:S(2)}) %collective-permute-start) | collective-permute-done | bytes 589856 | tf_op jit(solution)/shard_map/ppermute | solution.py:103
  60.3 0.0 all-to-all-done.1
  60.3 0.0 copy-start.4
  60.3 0.0 copy-done.1
  60.3 0.0 copy-done.2
  60.3 0.0 copy-done.3
  60.3 0.6 copy-done.4
  60.9 2.3 %section_first.1.q_ref = f32[8,3,48,128]{3,2,1,0:T(8,128)S(1)} custom-call(f32[8]{0:T(128)S(1)} %copy-done.4, f32[8,3,48,128]{3,2,1,0:T(8,128)S(1)} %bitcast.10, f32[8,3,48,128]{3,2,1,0:T(8,128)S(1)} %collective-permute-done.low_ref, f32[8,3,48,128]{3,2,1,0:T(8,128)S(1)} %collective-permute-done.1.high_ref, f32[3,3,48,128]{3,2,1,0:T(8,128)S(1)} %copy-done.1, ...), custom_call_target="tpu_custom_call" | custom-call | flops 11796480 | bytes 3538944 | tf_op jit(solution)/shard_map/section_first/pallas_call | solution.py:78
  63.2 14.9 %all_to_all.21 = f32[16,9,8,128]{3,2,1,0:T(8,128)S(1)} all-to-all(f32[16,9,8,128]{3,2,1,0:T(8,128)S(1)} %bitcast.12), channel_id=1, replica_groups=mesh['space'=32,'field'=16] {'field'}, dimensions={0} | all-to-all | bytes 1179648 | tf_op jit(solution)/shard_map/all_to_all | solution.py:96
  78.2 0.9 broadcast_in_dim.10
  79.0 5.9 %all-to-all-start.3 = ((f32[16,9,8,128]{3,2,1,0:T(8,128)}), f32[16,9,8,128]{3,2,1,0:T(8,128)S(1)}, u32[]{:S(2)}, u32[]{:S(2)}) async-start(f32[16,9,8,128]{3,2,1,0:T(8,128)} %broadcast_in_dim.10), calls=%async_computation.3 | async-start | bytes 1179648 | tf_op jit(solution)/shard_map/all_to_all | solution.py:97
  84.9 2.5 %collective-permute-start.3 = (f32[8,3,48,128]{3,2,1,0:T(8,128)S(1)}, f32[8,3,48,128]{3,2,1,0:T(8,128)S(1)}, u32[]{:S(2)}, u32[]{:S(2)}) collective-permute-start(f32[8,3,48,128]{3,2,1,0:T(8,128)S(1)} %section_first.1.q_ref), channel_id=1, source_target_pairs={{16,0},{32,16},{48,32},{64,48},{80,64},{96,80},{112,96},{128,112},... | collective-permute-start | bytes 1769480 | tf_op jit(solution)/shard_map/ppermute | solution.py:104
  87.4 3.7 %collective-permute-start.2 = (f32[8,3,48,128]{3,2,1,0:T(8,128)S(1)}, f32[8,3,48,128]{3,2,1,0:T(8,128)S(1)}, u32[]{:S(2)}, u32[]{:S(2)}) collective-permute-start(f32[8,3,48,128]{3,2,1,0:T(8,128)S(1)} %section_first.1.q_ref), channel_id=1, source_target_pairs={{0,16},{16,32},{32,48},{48,64},{64,80},{80,96},{96,112},{112,128},... | collective-permute-start | bytes 1769480 | tf_op jit(solution)/shard_map/ppermute | solution.py:103
  91.1 26.2 %collective-permute-done.3.high_ref = f32[8,3,48,128]{3,2,1,0:T(8,128)S(1)} collective-permute-done((f32[8,3,48,128]{3,2,1,0:T(8,128)S(1)}, f32[8,3,48,128]{3,2,1,0:T(8,128)S(1)}, u32[]{:S(2)}, u32[]{:S(2)}) %collective-permute-start.3) | collective-permute-done | bytes 589856 | tf_op jit(solution)/shard_map/ppermute | solution.py:104
  117.3 4.0 %collective-permute-done.2.low_ref = f32[8,3,48,128]{3,2,1,0:T(8,128)S(1)} collective-permute-done((f32[8,3,48,128]{3,2,1,0:T(8,128)S(1)}, f32[8,3,48,128]{3,2,1,0:T(8,128)S(1)}, u32[]{:S(2)}, u32[]{:S(2)}) %collective-permute-start.2) | collective-permute-done | bytes 589856 | tf_op jit(solution)/shard_map/ppermute | solution.py:103
  121.4 0.0 all-to-all-done.3
  121.4 3.2 %section_last.1 = f32[8,3,48,128]{3,2,1,0:T(8,128)} custom-call(f32[8]{0:T(128)S(1)} %copy-done.4, f32[8,3,48,128]{3,2,1,0:T(8,128)S(1)} %section_first.1.q_ref, f32[8,3,48,128]{3,2,1,0:T(8,128)S(1)} %collective-permute-done.2.low_ref, f32[8,3,48,128]{3,2,1,0:T(8,128)S(1)} %collective-permute-done.3.high_ref, f32[3,3,48,128]{3,2,1,0:T(8,128)S(1)} %copy-done.1, ...), custom_call_target="tpu_custom_call" | custom-call | flops 11796480 | bytes 3538944 | tf_op jit(solution)/shard_map/section_last/pallas_call | solution.py:78
  (2 shorter events, 0.1 us)
Async XLA Ops:
  16.2 6.0 %copy-start = (f32[1,8,3,48,128]{4,3,2,1,0:T(8,128)S(1)}, f32[1,8,3,48,128]{4,3,2,1,0:T(8,128)}, u32[]{:S(2)}) copy-start(f32[1,8,3,48,128]{4,3,2,1,0:T(8,128)} %param.5) | copy-start | bytes 1769476
  16.2 44.1 %copy-start.1 = (f32[3,3,48,128]{3,2,1,0:T(8,128)S(1)}, f32[3,3,48,128]{3,2,1,0:T(8,128)}, u32[]{:S(2)}) copy-start(f32[3,3,48,128]{3,2,1,0:T(8,128)} %vel_ref.3) | copy-start | bytes 663556
  16.2 44.1 %copy-start.2 = (f32[1,3,3,48,128]{4,3,2,1,0:T(8,128)S(1)}, f32[1,3,3,48,128]{4,3,2,1,0:T(8,128)}, u32[]{:S(2)}) copy-start(f32[1,3,3,48,128]{4,3,2,1,0:T(8,128)} %param.7) | copy-start | bytes 663556
  16.2 44.1 %copy-start.3 = (f32[3,48,128]{2,1,0:T(8,128)S(1)}, f32[3,48,128]{2,1,0:T(8,128)}, u32[]{:S(2)}) copy-start(f32[3,48,128]{2,1,0:T(8,128)} %dif_ref.3) | copy-start | bytes 221188
  16.2 44.1 %all-to-all-start.1 = ((f32[16,9,8,128]{3,2,1,0:T(8,128)}), f32[16,9,8,128]{3,2,1,0:T(8,128)S(1)}, u32[]{:S(2)}, u32[]{:S(2)}) async-start(f32[16,9,8,128]{3,2,1,0:T(8,128)} %broadcast_in_dim.9), calls=%async_computation.1 | async-start | bytes 1179648 | tf_op jit(solution)/shard_map/all_to_all | solution.py:97
  22.2 34.9 %collective-permute-start.1 = (f32[8,3,48,128]{3,2,1,0:T(8,128)S(1)}, f32[8,3,48,128]{3,2,1,0:T(8,128)S(1)}, u32[]{:S(2)}, u32[]{:S(2)}) collective-permute-start(f32[8,3,48,128]{3,2,1,0:T(8,128)S(1)} %bitcast.8), channel_id=1, source_target_pairs={{16,0},{32,16},{48,32},{64,48},{80,64},{96,80},{112,96},{128,112},... | collective-permute-start | bytes 1769480 | tf_op jit(solution)/shard_map/ppermute | solution.py:104
  26.3 33.9 %collective-permute-start = (f32[8,3,48,128]{3,2,1,0:T(8,128)S(1)}, f32[8,3,48,128]{3,2,1,0:T(8,128)S(1)}, u32[]{:S(2)}, u32[]{:S(2)}) collective-permute-start(f32[8,3,48,128]{3,2,1,0:T(8,128)S(1)} %bitcast.9), channel_id=1, source_target_pairs={{0,16},{16,32},{32,48},{48,64},{64,80},{80,96},{96,112},{112,128},... | collective-permute-start | bytes 1769480 | tf_op jit(solution)/shard_map/ppermute | solution.py:103
  60.3 0.7 copy-start.4
  79.0 42.3 %all-to-all-start.3 = ((f32[16,9,8,128]{3,2,1,0:T(8,128)}), f32[16,9,8,128]{3,2,1,0:T(8,128)S(1)}, u32[]{:S(2)}, u32[]{:S(2)}) async-start(f32[16,9,8,128]{3,2,1,0:T(8,128)} %broadcast_in_dim.10), calls=%async_computation.3 | async-start | bytes 1179648 | tf_op jit(solution)/shard_map/all_to_all | solution.py:97
  84.9 32.4 %collective-permute-start.3 = (f32[8,3,48,128]{3,2,1,0:T(8,128)S(1)}, f32[8,3,48,128]{3,2,1,0:T(8,128)S(1)}, u32[]{:S(2)}, u32[]{:S(2)}) collective-permute-start(f32[8,3,48,128]{3,2,1,0:T(8,128)S(1)} %section_first.1.q_ref), channel_id=1, source_target_pairs={{16,0},{32,16},{48,32},{64,48},{80,64},{96,80},{112,96},{128,112},... | collective-permute-start | bytes 1769480 | tf_op jit(solution)/shard_map/ppermute | solution.py:104
  87.4 33.9 %collective-permute-start.2 = (f32[8,3,48,128]{3,2,1,0:T(8,128)S(1)}, f32[8,3,48,128]{3,2,1,0:T(8,128)S(1)}, u32[]{:S(2)}, u32[]{:S(2)}) collective-permute-start(f32[8,3,48,128]{3,2,1,0:T(8,128)S(1)} %section_first.1.q_ref), channel_id=1, source_target_pairs={{0,16},{16,32},{32,48},{48,64},{64,80},{80,96},{96,112},{112,128},... | collective-permute-start | bytes 1769480 | tf_op jit(solution)/shard_map/ppermute | solution.py:103

commit v2 on v1

--- a/solution.py
+++ b/solution.py
@@ -17,7 +17,7 @@
     return 1.0 / (1.0 + jnp.exp(-x))
 
 
-def section_kernel(fields, last, stoich_ref, q_ref, low_ref, high_ref, vel_ref, wie_ref, dif_ref, sum_ref, *rest):
+def section_kernel(fields, last, stoich_ref, q_ref, low_a, low_b, high_a, high_b, vel_ref, wie_ref, dif_ref, sum_ref, *rest):
     if last:
         base_ref, out_ref, coef, react = rest
     else:
@@ -33,15 +33,18 @@
         theta = 1.0 + 3.0 * sigmoid(q_ref[scalars - 1, i])
         react[i] = (time_step * pre_factor) * q_ref[0, i] * q_ref[1, i] * jnp.exp(-activation / theta)
 
-    def one(s, carry):
+    half = scalars // 2
+
+    def one(low_ref, high_ref, first, n, carry):
+        s = first + n
         for i in range(planes):
 
             def along_x(k):
                 j = i + k
                 if j < 0:
-                    return low_ref[s, j + planes]
+                    return low_ref[n, j + planes]
                 if j >= planes:
-                    return high_ref[s, j - planes]
+                    return high_ref[n, j - planes]
                 return q_ref[s, j]
 
             q = q_ref[s, i]
@@ -67,14 +70,15 @@
             out_ref[s, i] = new
         return carry
 
-    lax.fori_loop(0, scalars, one, 0)
+    lax.fori_loop(0, half, functools.partial(one, low_a, high_a, 0), 0)
+    lax.fori_loop(0, half, functools.partial(one, low_b, high_b, half), 0)
 
 
-def section(fields, stoich, q, low, high, velocity, wiener, diffusivity, total, base=None):
+def section(fields, stoich, q, halo, velocity, wiener, diffusivity, total, base=None):
     last = base is not None
     planes, rows, lanes = q.shape[1:]
     vmem = pl.BlockSpec(memory_space=pltpu.VMEM)
-    args = (q, low, high, velocity, wiener, diffusivity, total) + ((base,) if last else ())
+    args = (q, *halo, velocity, wiener, diffusivity, total) + ((base,) if last else ())
     return pl.pallas_call(
         functools.partial(section_kernel, fields, last),
         out_shape=jax.ShapeDtypeStruct(q.shape, q.dtype),
@@ -90,14 +94,6 @@
     )(stoich, *args)
 
 
-def field_sum(q):
-    count = lax.axis_size("field")
-    shares = q.reshape(count, -1, 8, q.shape[-1])
-    share = jnp.sum(lax.all_to_all(shares, "field", 0, 0), axis=0)
-    whole = lax.all_to_all(jnp.broadcast_to(share, shares.shape), "field", 0, 0)
-    return whole.reshape(q.shape)
-
-
 def neighbours(q):
     count = lax.axis_size("space")
     low = lax.ppermute(q, "space", [(i, i + 1) for i in range(count - 1)])
@@ -105,13 +101,25 @@
     return low, high
 
 
+def exchange(q):
+    count = lax.axis_size("field")
+    half = q.shape[0] // 2
+    shares = q.reshape(count, -1, 8, q.shape[-1])
+    low_a, high_a = neighbours(q[:half])
+    share = jnp.sum(lax.all_to_all(shares, "field", 0, 0), axis=0)
+    share, low_a, high_a, rest = lax.optimization_barrier((share, low_a, high_a, q[half:]))
+    low_b, high_b = neighbours(rest)
+    whole = lax.all_to_all(jnp.broadcast_to(share, shares.shape), "field", 0, 0)
+    return whole.reshape(q.shape), (low_a, low_b, high_a, high_b)
+
+
 def local(phi, velocity, wiener, diffusivity, stoich):
     fields = phi.shape[0] * lax.axis_size("field")
     phi, wiener = phi[0], wiener[0]
-    low, high = neighbours(phi)
-    first = section(fields, stoich, phi, low, high, velocity, wiener, diffusivity, field_sum(phi))
-    low, high = neighbours(first)
-    out = section(fields, stoich, first, low, high, velocity, wiener, diffusivity, field_sum(first), phi)
+    total, halo = exchange(phi)
+    first = section(fields, stoich, phi, halo, velocity, wiener, diffusivity, total)
+    total, halo = exchange(first)
+    out = section(fields, stoich, first, halo, velocity, wiener, diffusivity, total, phi)
     return out[None]
 
 

time: 125 us -> 131 us (1.048)
  the two profiles are of different devices: /device:TPU:267 before, /device:TPU:258 now
where the time goes in v2:
time: 131 us; the launch traced here: 130 us
  starting transfers between devices  61.6 us (47%)
  waiting for transfers between devices  58 us (44%)
  Pallas kernels  6.8 us (5%)
  local copies, waits for them, and re-layouts  3.47 us (3%)
    ppermute x4, waiting for transfers between devices, neighbours(): low = lax.ppermute(q, 'space', [(i, i + 1) for i in range(count - 1)])  50.9 us
    ppermute x4, starting transfers between devices, neighbours(): high = lax.ppermute(q, 'space', [(i + 1, i) for i in range(count - 1)])  27 us
    ppermute x4, starting transfers between devices, neighbours(): low = lax.ppermute(q, 'space', [(i, i + 1) for i in range(count - 1)])  14 us
    all_to_all x2, starting transfers between devices, exchange(): share = jnp.sum(lax.all_to_all(shares, 'field', 0, 0), axis=0)  10.8 us
    all_to_all x2, starting transfers between devices, exchange(): whole = lax.all_to_all(jnp.broadcast_to(share, shares.shape), 'field', 0, 0)  9.77 us
    pallas_call x2, Pallas kernels, section(): pl.pallas_call(functools.partial(section_kernel, fields, last), out_shape...  6.8 us
    all_to_all x2, waiting for transfers between devices, exchange(): share = jnp.sum(lax.all_to_all(shares, 'field', 0, 0), axis=0)  6.48 us
  transfers between devices with their start and end apart: 12, of which 8 were waited for; matrix products, arithmetic and copies ran while one was open for 1% of the time, Pallas kernels for 0%

profile of v2, /device:TPU:258, one launch (start us, length us, event | category | flops | bytes accessed | tf_op | source)
XLA Modules:
  0.0 130.0 jit_solution(242676098356199299)
XLA Ops:
  0.0 0.0 copy-start
  0.0 6.0 %all-to-all-start = ((f32[16,9,8,128]{3,2,1,0:T(8,128)}), f32[16,9,8,128]{3,2,1,0:T(8,128)S(1)}, u32[]{:S(2)}, u32[]{:S(2)}) async-start(f32[16,9,8,128]{3,2,1,0:T(8,128)} %bitcast.11), calls=%async_computation | async-start | bytes 1179648 | tf_op jit(solution)/shard_map/all_to_all | solution.py:109
  6.0 0.0 copy-done
  6.0 4.5 %collective-permute-start = (f32[4,3,48,128]{3,2,1,0:T(8,128)S(1)}, f32[4,3,48,128]{3,2,1,0:T(8,128)S(1)}, u32[]{:S(2)}, u32[]{:S(2)}) collective-permute-start(f32[4,3,48,128]{3,2,1,0:T(8,128)S(1)} %get-tuple-element.24), channel_id=1, source_target_pairs={{0,16},{16,32},{32,48},{48,64},{64,80},{80,96},{96,112},{112,128},... | collective-permute-start | bytes 884744 | tf_op jit(solution)/shard_map/ppermute | solution.py:99
  10.6 5.6 %collective-permute-start.1 = (f32[4,3,48,128]{3,2,1,0:T(8,128)S(1)}, f32[4,3,48,128]{3,2,1,0:T(8,128)S(1)}, u32[]{:S(2)}, u32[]{:S(2)}) collective-permute-start(f32[4,3,48,128]{3,2,1,0:T(8,128)S(1)} %get-tuple-element.24), channel_id=1, source_target_pairs={{16,0},{32,16},{48,32},{64,48},{80,64},{96,80},{112,96},{128,112},... | collective-permute-start | bytes 884744 | tf_op jit(solution)/shard_map/ppermute | solution.py:100
  16.1 3.7 %all-to-all-done = f32[16,9,8,128]{3,2,1,0:T(8,128)S(1)} async-done(((f32[16,9,8,128]{3,2,1,0:T(8,128)}), f32[16,9,8,128]{3,2,1,0:T(8,128)S(1)}, u32[]{:S(2)}, u32[]{:S(2)}) %all-to-all-start) | async-done | bytes 589856 | tf_op jit(solution)/shard_map/all_to_all | solution.py:109
  19.9 8.7 %collective-permute-done.low_a = f32[4,3,48,128]{3,2,1,0:T(8,128)S(1)} collective-permute-done((f32[4,3,48,128]{3,2,1,0:T(8,128)S(1)}, f32[4,3,48,128]{3,2,1,0:T(8,128)S(1)}, u32[]{:S(2)}, u32[]{:S(2)}) %collective-permute-start) | collective-permute-done | bytes 294944 | tf_op jit(solution)/shard_map/ppermute | solution.py:99
  28.6 0.3 collective-permute-done.1.high_a
  28.9 0.9 broadcast_in_dim.9
  29.8 0.0 copy-start.1
  29.8 0.0 copy-start.2
  29.8 0.0 copy-start.3
  29.8 5.0 %all-to-all-start.1 = ((f32[16,9,8,128]{3,2,1,0:T(8,128)}), f32[16,9,8,128]{3,2,1,0:T(8,128)S(1)}, u32[]{:S(2)}, u32[]{:S(2)}) async-start(f32[16,9,8,128]{3,2,1,0:T(8,128)} %broadcast_in_dim.9), calls=%async_computation.1 | async-start | bytes 1179648 | tf_op jit(solution)/shard_map/all_to_all | solution.py:112
  34.7 5.6 %collective-permute-start.2 = (f32[4,3,48,128]{3,2,1,0:T(8,128)S(1)}, f32[4,3,48,128]{3,2,1,0:T(8,128)S(1)}, u32[]{:S(2)}, u32[]{:S(2)}) collective-permute-start(f32[4,3,48,128]{3,2,1,0:T(8,128)S(1)} %get-tuple-element.14), channel_id=1, source_target_pairs={{0,16},{16,32},{32,48},{48,64},{64,80},{80,96},{96,112},{112,128},... | collective-permute-start | bytes 884744 | tf_op jit(solution)/shard_map/ppermute | solution.py:99
  40.4 4.7 %collective-permute-start.3 = (f32[4,3,48,128]{3,2,1,0:T(8,128)S(1)}, f32[4,3,48,128]{3,2,1,0:T(8,128)S(1)}, u32[]{:S(2)}, u32[]{:S(2)}) collective-permute-start(f32[4,3,48,128]{3,2,1,0:T(8,128)S(1)} %get-tuple-element.14), channel_id=1, source_target_pairs={{16,0},{32,16},{48,32},{64,48},{80,64},{96,80},{112,96},{128,112},... | collective-permute-start | bytes 884744 | tf_op jit(solution)/shard_map/ppermute | solution.py:100
  45.1 16.3 %collective-permute-done.2.low_b = f32[4,3,48,128]{3,2,1,0:T(8,128)S(1)} collective-permute-done((f32[4,3,48,128]{3,2,1,0:T(8,128)S(1)}, f32[4,3,48,128]{3,2,1,0:T(8,128)S(1)}, u32[]{:S(2)}, u32[]{:S(2)}) %collective-permute-start.2) | collective-permute-done | bytes 294944 | tf_op jit(solution)/shard_map/ppermute | solution.py:99
  61.4 0.0 collective-permute-done.3.high_b
  61.4 0.0 all-to-all-done.1
  61.4 0.0 copy-start.4
  61.4 0.0 copy-done.1
  61.4 0.0 copy-done.2
  61.4 0.0 copy-done.3
  61.4 0.6 copy-done.4
  62.1 3.1 %section_first.1.q_ref = f32[8,3,48,128]{3,2,1,0:T(8,128)} custom-call(f32[8]{0:T(128)S(1)} %copy-done.4, f32[8,3,48,128]{3,2,1,0:T(8,128)S(1)} %bitcast.12, f32[4,3,48,128]{3,2,1,0:T(8,128)S(1)} %collective-permute-done.low_a, f32[4,3,48,128]{3,2,1,0:T(8,128)S(1)} %collective-permute-done.2.low_b, f32[4,3,48,128]{3,2,1,0:T(8,128)S(1)} %collective-permute-done.1.high_a, ...), custom_call_target="tpu_custom_call" | custom-call | flops 11796480 | bytes 3538944 | tf_op jit(solution)/shard_map/section_first/pallas_call | solution.py:82
  65.2 4.8 %all-to-all-start.2 = ((f32[16,9,8,128]{3,2,1,0:T(8,128)}), f32[16,9,8,128]{3,2,1,0:T(8,128)S(1)}, u32[]{:S(2)}, u32[]{:S(2)}) async-start(f32[16,9,8,128]{3,2,1,0:T(8,128)} %bitcast.6), calls=%async_computation.2 | async-start | bytes 1179648 | tf_op jit(solution)/shard_map/all_to_all | solution.py:109
  70.0 1.1 fusion
  71.1 1.9 %collective-permute-start.4 = (f32[4,3,48,128]{3,2,1,0:T(8,128)S(1)}, f32[4,3,48,128]{3,2,1,0:T(8,128)S(1)}, u32[]{:S(2)}, u32[]{:S(2)}) collective-permute-start(f32[4,3,48,128]{3,2,1,0:T(8,128)S(1)} %get-tuple-element.22), channel_id=1, source_target_pairs={{0,16},{16,32},{32,48},{48,64},{64,80},{80,96},{96,112},{112,128},... | collective-permute-start | bytes 884744 | tf_op jit(solution)/shard_map/ppermute | solution.py:99
  73.0 8.1 %collective-permute-start.5 = (f32[4,3,48,128]{3,2,1,0:T(8,128)S(1)}, f32[4,3,48,128]{3,2,1,0:T(8,128)S(1)}, u32[]{:S(2)}, u32[]{:S(2)}) collective-permute-start(f32[4,3,48,128]{3,2,1,0:T(8,128)S(1)} %get-tuple-element.22), channel_id=1, source_target_pairs={{16,0},{32,16},{48,32},{64,48},{80,64},{96,80},{112,96},{128,112},... | collective-permute-start | bytes 884744 | tf_op jit(solution)/shard_map/ppermute | solution.py:100
  81.2 2.8 %all-to-all-done.2 = f32[16,9,8,128]{3,2,1,0:T(8,128)S(1)} async-done(((f32[16,9,8,128]{3,2,1,0:T(8,128)}), f32[16,9,8,128]{3,2,1,0:T(8,128)S(1)}, u32[]{:S(2)}, u32[]{:S(2)}) %all-to-all-start.2) | async-done | bytes 589856 | tf_op jit(solution)/shard_map/all_to_all | solution.py:109
  84.0 9.5 %collective-permute-done.4.low_a = f32[4,3,48,128]{3,2,1,0:T(8,128)S(1)} collective-permute-done((f32[4,3,48,128]{3,2,1,0:T(8,128)S(1)}, f32[4,3,48,128]{3,2,1,0:T(8,128)S(1)}, u32[]{:S(2)}, u32[]{:S(2)}) %collective-permute-start.4) | collective-permute-done | bytes 294944 | tf_op jit(solution)/shard_map/ppermute | solution.py:99
  93.5 0.3 collective-permute-done.5.high_a
  93.8 0.9 broadcast_in_dim.10
  94.6 4.8 %all-to-all-start.3 = ((f32[16,9,8,128]{3,2,1,0:T(8,128)}), f32[16,9,8,128]{3,2,1,0:T(8,128)S(1)}, u32[]{:S(2)}, u32[]{:S(2)}) async-start(f32[16,9,8,128]{3,2,1,0:T(8,128)} %broadcast_in_dim.10), calls=%async_computation.3 | async-start | bytes 1179648 | tf_op jit(solution)/shard_map/all_to_all | solution.py:112
  99.5 1.9 %collective-permute-start.6 = (f32[4,3,48,128]{3,2,1,0:T(8,128)S(1)}, f32[4,3,48,128]{3,2,1,0:T(8,128)S(1)}, u32[]{:S(2)}, u32[]{:S(2)}) collective-permute-start(f32[4,3,48,128]{3,2,1,0:T(8,128)S(1)} %get-tuple-element.18), channel_id=1, source_target_pairs={{0,16},{16,32},{32,48},{48,64},{64,80},{80,96},{96,112},{112,128},... | collective-permute-start | bytes 884744 | tf_op jit(solution)/shard_map/ppermute | solution.py:99
  101.4 8.6 %collective-permute-start.7 = (f32[4,3,48,128]{3,2,1,0:T(8,128)S(1)}, f32[4,3,48,128]{3,2,1,0:T(8,128)S(1)}, u32[]{:S(2)}, u32[]{:S(2)}) collective-permute-start(f32[4,3,48,128]{3,2,1,0:T(8,128)S(1)} %get-tuple-element.18), channel_id=1, source_target_pairs={{16,0},{32,16},{48,32},{64,48},{80,64},{96,80},{112,96},{128,112},... | collective-permute-start | bytes 884744 | tf_op jit(solution)/shard_map/ppermute | solution.py:100
  110.0 16.3 %collective-permute-done.6.low_b = f32[4,3,48,128]{3,2,1,0:T(8,128)S(1)} collective-permute-done((f32[4,3,48,128]{3,2,1,0:T(8,128)S(1)}, f32[4,3,48,128]{3,2,1,0:T(8,128)S(1)}, u32[]{:S(2)}, u32[]{:S(2)}) %collective-permute-start.6) | collective-permute-done | bytes 294944 | tf_op jit(solution)/shard_map/ppermute | solution.py:99
  126.3 0.0 collective-permute-done.7.high_b
  126.3 0.0 all-to-all-done.3
  126.3 3.7 %section_last.1 = f32[8,3,48,128]{3,2,1,0:T(8,128)} custom-call(f32[8]{0:T(128)S(1)} %copy-done.4, f32[8,3,48,128]{3,2,1,0:T(8,128)} %section_first.1.q_ref, f32[4,3,48,128]{3,2,1,0:T(8,128)S(1)} %collective-permute-done.4.low_a, f32[4,3,48,128]{3,2,1,0:T(8,128)S(1)} %collective-permute-done.6.low_b, f32[4,3,48,128]{3,2,1,0:T(8,128)S(1)} %collective-permute-done.5.high_a, ...), custom_call_target="tpu_custom_call" | custom-call | flops 11796480 | bytes 3538944 | tf_op jit(solution)/shard_map/section_last/pallas_call | solution.py:82
  (3 shorter events, 0.1 us)
Async XLA Ops:
  0.0 6.0 %copy-start = (f32[1,8,3,48,128]{4,3,2,1,0:T(8,128)S(1)}, f32[1,8,3,48,128]{4,3,2,1,0:T(8,128)}, u32[]{:S(2)}) copy-start(f32[1,8,3,48,128]{4,3,2,1,0:T(8,128)} %param.5) | copy-start | bytes 1769476
  0.0 19.8 %all-to-all-start = ((f32[16,9,8,128]{3,2,1,0:T(8,128)}), f32[16,9,8,128]{3,2,1,0:T(8,128)S(1)}, u32[]{:S(2)}, u32[]{:S(2)}) async-start(f32[16,9,8,128]{3,2,1,0:T(8,128)} %bitcast.11), calls=%async_computation | async-start | bytes 1179648 | tf_op jit(solution)/shard_map/all_to_all | solution.py:109
  6.0 22.6 %collective-permute-start = (f32[4,3,48,128]{3,2,1,0:T(8,128)S(1)}, f32[4,3,48,128]{3,2,1,0:T(8,128)S(1)}, u32[]{:S(2)}, u32[]{:S(2)}) collective-permute-start(f32[4,3,48,128]{3,2,1,0:T(8,128)S(1)} %get-tuple-element.24), channel_id=1, source_target_pairs={{0,16},{16,32},{32,48},{48,64},{64,80},{80,96},{96,112},{112,128},... | collective-permute-start | bytes 884744 | tf_op jit(solution)/shard_map/ppermute | solution.py:99
  10.6 18.3 %collective-permute-start.1 = (f32[4,3,48,128]{3,2,1,0:T(8,128)S(1)}, f32[4,3,48,128]{3,2,1,0:T(8,128)S(1)}, u32[]{:S(2)}, u32[]{:S(2)}) collective-permute-start(f32[4,3,48,128]{3,2,1,0:T(8,128)S(1)} %get-tuple-element.24), channel_id=1, source_target_pairs={{16,0},{32,16},{48,32},{64,48},{80,64},{96,80},{112,96},{128,112},... | collective-permute-start | bytes 884744 | tf_op jit(solution)/shard_map/ppermute | solution.py:100
  29.8 31.7 %copy-start.1 = (f32[3,3,48,128]{3,2,1,0:T(8,128)S(1)}, f32[3,3,48,128]{3,2,1,0:T(8,128)}, u32[]{:S(2)}) copy-start(f32[3,3,48,128]{3,2,1,0:T(8,128)} %vel_ref.3) | copy-start | bytes 663556
  29.8 31.7 %copy-start.2 = (f32[1,3,3,48,128]{4,3,2,1,0:T(8,128)S(1)}, f32[1,3,3,48,128]{4,3,2,1,0:T(8,128)}, u32[]{:S(2)}) copy-start(f32[1,3,3,48,128]{4,3,2,1,0:T(8,128)} %param.7) | copy-start | bytes 663556
  29.8 31.7 %copy-start.3 = (f32[3,48,128]{2,1,0:T(8,128)S(1)}, f32[3,48,128]{2,1,0:T(8,128)}, u32[]{:S(2)}) copy-start(f32[3,48,128]{2,1,0:T(8,128)} %dif_ref.3) | copy-start | bytes 221188
  29.8 31.6 %all-to-all-start.1 = ((f32[16,9,8,128]{3,2,1,0:T(8,128)}), f32[16,9,8,128]{3,2,1,0:T(8,128)S(1)}, u32[]{:S(2)}, u32[]{:S(2)}) async-start(f32[16,9,8,128]{3,2,1,0:T(8,128)} %broadcast_in_dim.9), calls=%async_computation.1 | async-start | bytes 1179648 | tf_op jit(solution)/shard_map/all_to_all | solution.py:112
  34.7 26.7 %collective-permute-start.2 = (f32[4,3,48,128]{3,2,1,0:T(8,128)S(1)}, f32[4,3,48,128]{3,2,1,0:T(8,128)S(1)}, u32[]{:S(2)}, u32[]{:S(2)}) collective-permute-start(f32[4,3,48,128]{3,2,1,0:T(8,128)S(1)} %get-tuple-element.14), channel_id=1, source_target_pairs={{0,16},{16,32},{32,48},{48,64},{64,80},{80,96},{96,112},{112,128},... | collective-permute-start | bytes 884744 | tf_op jit(solution)/shard_map/ppermute | solution.py:99
  40.4 21.0 %collective-permute-start.3 = (f32[4,3,48,128]{3,2,1,0:T(8,128)S(1)}, f32[4,3,48,128]{3,2,1,0:T(8,128)S(1)}, u32[]{:S(2)}, u32[]{:S(2)}) collective-permute-start(f32[4,3,48,128]{3,2,1,0:T(8,128)S(1)} %get-tuple-element.14), channel_id=1, source_target_pairs={{16,0},{32,16},{48,32},{64,48},{80,64},{96,80},{112,96},{128,112},... | collective-permute-start | bytes 884744 | tf_op jit(solution)/shard_map/ppermute | solution.py:100
  61.4 0.7 copy-start.4
  65.2 18.8 %all-to-all-start.2 = ((f32[16,9,8,128]{3,2,1,0:T(8,128)}), f32[16,9,8,128]{3,2,1,0:T(8,128)S(1)}, u32[]{:S(2)}, u32[]{:S(2)}) async-start(f32[16,9,8,128]{3,2,1,0:T(8,128)} %bitcast.6), calls=%async_computation.2 | async-start | bytes 1179648 | tf_op jit(solution)/shard_map/all_to_all | solution.py:109
  71.1 22.4 %collective-permute-start.4 = (f32[4,3,48,128]{3,2,1,0:T(8,128)S(1)}, f32[4,3,48,128]{3,2,1,0:T(8,128)S(1)}, u32[]{:S(2)}, u32[]{:S(2)}) collective-permute-start(f32[4,3,48,128]{3,2,1,0:T(8,128)S(1)} %get-tuple-element.22), channel_id=1, source_target_pairs={{0,16},{16,32},{32,48},{48,64},{64,80},{80,96},{96,112},{112,128},... | collective-permute-start | bytes 884744 | tf_op jit(solution)/shard_map/ppermute | solution.py:99
  73.0 20.7 %collective-permute-start.5 = (f32[4,3,48,128]{3,2,1,0:T(8,128)S(1)}, f32[4,3,48,128]{3,2,1,0:T(8,128)S(1)}, u32[]{:S(2)}, u32[]{:S(2)}) collective-permute-start(f32[4,3,48,128]{3,2,1,0:T(8,128)S(1)} %get-tuple-element.22), channel_id=1, source_target_pairs={{16,0},{32,16},{48,32},{64,48},{80,64},{96,80},{112,96},{128,112},... | collective-permute-start | bytes 884744 | tf_op jit(solution)/shard_map/ppermute | solution.py:100
  94.6 31.7 %all-to-all-start.3 = ((f32[16,9,8,128]{3,2,1,0:T(8,128)}), f32[16,9,8,128]{3,2,1,0:T(8,128)S(1)}, u32[]{:S(2)}, u32[]{:S(2)}) async-start(f32[16,9,8,128]{3,2,1,0:T(8,128)} %broadcast_in_dim.10), calls=%async_computation.3 | async-start | bytes 1179648 | tf_op jit(solution)/shard_map/all_to_all | solution.py:112
  99.5 26.9 %collective-permute-start.6 = (f32[4,3,48,128]{3,2,1,0:T(8,128)S(1)}, f32[4,3,48,128]{3,2,1,0:T(8,128)S(1)}, u32[]{:S(2)}, u32[]{:S(2)}) collective-permute-start(f32[4,3,48,128]{3,2,1,0:T(8,128)S(1)} %get-tuple-element.18), channel_id=1, source_target_pairs={{0,16},{16,32},{32,48},{48,64},{64,80},{80,96},{96,112},{112,128},... | collective-permute-start | bytes 884744 | tf_op jit(solution)/shard_map/ppermute | solution.py:99
  101.4 24.9 %collective-permute-start.7 = (f32[4,3,48,128]{3,2,1,0:T(8,128)S(1)}, f32[4,3,48,128]{3,2,1,0:T(8,128)S(1)}, u32[]{:S(2)}, u32[]{:S(2)}) collective-permute-start(f32[4,3,48,128]{3,2,1,0:T(8,128)S(1)} %get-tuple-element.18), channel_id=1, source_target_pairs={{16,0},{32,16},{48,32},{64,48},{80,64},{96,80},{112,96},{128,112},... | collective-permute-start | bytes 884744 | tf_op jit(solution)/shard_map/ppermute | solution.py:100

commit v3 on v1

v3 whole, which is shorter than its diff:
```python
import functools

import jax
import jax.numpy as jnp
from jax import lax
from jax.experimental import pallas as pl
from jax.experimental.pallas import tpu as pltpu
from jax.sharding import PartitionSpec as P

time_step = 0.3
mix_const = 5.0
pre_factor = 2.0
activation = 2.0

SMEM = pl.BlockSpec(memory_space=pltpu.SMEM)
VMEM = pl.BlockSpec(memory_space=pltpu.VMEM)


def call(kernel, out_shape, in_specs, scratch, flops, name):
    return pl.pallas_call(
        kernel,
        out_shape=out_shape,
        in_specs=in_specs,
        out_specs=jax.tree.map(lambda _: VMEM, out_shape),
        scratch_shapes=scratch,
        compiler_params=pltpu.CompilerParams(vmem_limit_bytes=16 * 2**20),
        cost_estimate=pl.CostEstimate(flops=flops, bytes_accessed=0, transcendentals=0),
        name=name,
    )


def sigmoid(x):
    return 1.0 / (1.0 + jnp.exp(-x))


def parts_kernel(stoich_ref, q_ref, low_ref, high_ref, vel_ref, wie_ref, dif_ref, base_ref, noise_ref, react):
    scalars, planes = q_ref.shape[:2]
    for i in range(planes):
        theta = 1.0 + 3.0 * sigmoid(q_ref[scalars - 1, i])
        react[i] = (time_step * pre_factor) * q_ref[0, i] * q_ref[1, i] * jnp.exp(-activation / theta)

    def one(s, carry):
        for i in range(planes):

            def along_x(k):
                j = i + k
                if j < 0:
                    return low_ref[s, j + planes]
                if j >= planes:
                    return high_ref[s, j - planes]
                return q_ref[s, j]

            q = q_ref[s, i]
            rows, lanes = q.shape
            near = None
            for d in range(3):
                if d == 0:
                    at = along_x
                else:
                    size = (rows, lanes)[d - 1]
                    at = lambda k, d=d, size=size: pltpu.roll(q, (-k) % size, d - 1)
                up, down = at(1), at(-1)
                slope = 0.75 * (up - down) - 0.15 * (at(2) - at(-2)) + (1.0 / 60.0) * (at(3) - at(-3))
                drift = vel_ref[d, i] * slope
                shake = wie_ref[d, i] * slope
                pair = up + down
                near, drifts, shakes = (pair, drift, shake) if near is None else (near + pair, drifts + drift, shakes + shake)
            smooth = dif_ref[i] * (near - (6.0 + mix_const) * q)
            base_ref[s, i] = q + (time_step * (smooth - drifts) + stoich_ref[s] * react[i])
            noise_ref[s, i] = shakes
        return carry

    lax.fori_loop(0, scalars, one, 0)


def join_kernel(fields, last, base_ref, noise_ref, dif_ref, total_ref, *rest):
    out_ref = rest[-1]
    scalars, planes = base_ref.shape[:2]
    for i in range(planes):
        dif = dif_ref[i]
        theta_bar = 1.0 + 3.0 * sigmoid(total_ref[scalars - 1, i] * (1.0 / fields))
        amplitude = jnp.sqrt(2.0 * dif * theta_bar)
        pull = (time_step * mix_const / fields) * dif
        for s in range(scalars):
            new = base_ref[s, i] + (amplitude * noise_ref[s, i] + pull * total_ref[s, i])
            out_ref[s, i] = 0.5 * rest[0][s, i] + 0.5 * new if last else new


def spread_kernel(parts_ref, out_ref):
    count = parts_ref.shape[0]
    total = parts_ref[0]
    for n in range(1, count):
        total = total + parts_ref[n]
    for n in range(count):
        out_ref[n] = total


def section(fields, stoich, q, velocity, wiener, diffusivity, base=None):
    last = base is not None
    field_count = lax.axis_size("field")
    like = jax.ShapeDtypeStruct(q.shape, q.dtype)
    shares = q.reshape(field_count, -1, 8, q.shape[-1])
    received = lax.all_to_all(shares, "field", 0, 0)
    low, high = neighbours(q)
    spread = call(spread_kernel, jax.ShapeDtypeStruct(shares.shape, q.dtype), [VMEM], [], 0, "spread")(received)
    total = lax.all_to_all(spread, "field", 0, 0).reshape(q.shape)
    drift, noise = call(
        parts_kernel, (like, like), [SMEM] + [VMEM] * 6, [pltpu.VMEM(q.shape[1:], jnp.float32)], 10**10, "parts"
    )(stoich, q, low, high, velocity, wiener, diffusivity)
    args = (drift, noise, diffusivity, total) + ((base,) if last else ())
    return call(functools.partial(join_kernel, fields, last), like, [VMEM] * len(args), [], 0, "join")(*args)


def neighbours(q):
    count = lax.axis_size("space")
    low = lax.ppermute(q, "space", [(i, i + 1) for i in range(count - 1)])
    high = lax.ppermute(q, "space", [(i + 1, i) for i in range(count - 1)])
    return low, high


def local(phi, velocity, wiener, diffusivity, stoich):
    fields = phi.shape[0] * lax.axis_size("field")
    phi, wiener = phi[0], wiener[0]
    first = section(fields, stoich, phi, velocity, wiener, diffusivity)
    return section(fields, stoich, first, velocity, wiener, diffusivity, phi)[None]


def solution(mesh):
    return jax.shard_map(
        local,
        mesh=mesh,
        in_specs=(
            P("field", None, "space", None, None),
            P(None, "space", None, None),
            P("field", None, "space", None, None),
            P("space", None, None),
            P(),
        ),
        out_specs=P("field", None, "space", None, None),
        check_vma=False,
    )
```

time: 125 us -> 102 us (0.82)
  the two profiles are of different devices: /device:TPU:267 before, /device:TPU:256 now
where the time goes in v3:
time: 102 us; the launch traced here: 101 us
  waiting for transfers between devices  45.8 us (45%)
  starting transfers between devices  42.6 us (42%)
  Pallas kernels  8.88 us (9%)
  local copies, waits for them, and re-layouts  3.8 us (4%)
    all_to_all x2, waiting for transfers between devices, section(): received = lax.all_to_all(shares, 'field', 0, 0)  20.4 us
    ppermute x2, waiting for transfers between devices, neighbours(): low = lax.ppermute(q, 'space', [(i, i + 1) for i in range(count - 1)])  16.8 us
    all_to_all x2, starting transfers between devices, section(): total = lax.all_to_all(spread, 'field', 0, 0).reshape(q.shape)  13.4 us
    ppermute x2, starting transfers between devices, neighbours(): high = lax.ppermute(q, 'space', [(i + 1, i) for i in range(count - 1)])  12.9 us
    all_to_all x2, starting transfers between devices, section(): received = lax.all_to_all(shares, 'field', 0, 0)  9.13 us
    all_to_all x2, waiting for transfers between devices, section(): total = lax.all_to_all(spread, 'field', 0, 0).reshape(q.shape)  8.59 us
    ppermute x2, starting transfers between devices, neighbours(): low = lax.ppermute(q, 'space', [(i, i + 1) for i in range(count - 1)])  7.26 us
    pallas_call x2, Pallas kernels, section(): call(parts_kernel, (like, like), [SMEM] + [VMEM] * 6, [pltpu.VMEM(q.shape...  5.15 us
  transfers between devices with their start and end apart: 8, of which 6 were waited for; matrix products, arithmetic and copies ran while one was open for 0% of the time, Pallas kernels for 7%

profile of v3, /device:TPU:256, one launch (start us, length us, event | category | flops | bytes accessed | tf_op | source)
XLA Modules:
  0.0 101.2 jit_solution(18173748466003811339)
XLA Ops:
  0.0 0.0 copy-start
  0.0 5.5 %all-to-all-start = ((f32[16,9,8,128]{3,2,1,0:T(8,128)}), f32[16,9,8,128]{3,2,1,0:T(8,128)S(1)}, u32[]{:S(2)}, u32[]{:S(2)}) async-start(f32[16,9,8,128]{3,2,1,0:T(8,128)} %bitcast.7), calls=%async_computation | async-start | bytes 1179648 | tf_op jit(solution)/shard_map/all_to_all | solution.py:103
  5.6 0.0 copy-done
  5.6 4.5 %collective-permute-start = (f32[8,3,48,128]{3,2,1,0:T(8,128)S(1)}, f32[8,3,48,128]{3,2,1,0:T(8,128)S(1)}, u32[]{:S(2)}, u32[]{:S(2)}) collective-permute-start(f32[8,3,48,128]{3,2,1,0:T(8,128)S(1)} %bitcast.8), channel_id=1, source_target_pairs={{0,16},{16,32},{32,48},{48,64},{64,80},{80,96},{96,112},{112,128},... | collective-permute-start | bytes 1769480 | tf_op jit(solution)/shard_map/ppermute | solution.py:116
  10.1 5.6 %collective-permute-start.1 = (f32[8,3,48,128]{3,2,1,0:T(8,128)S(1)}, f32[8,3,48,128]{3,2,1,0:T(8,128)S(1)}, u32[]{:S(2)}, u32[]{:S(2)}) collective-permute-start(f32[8,3,48,128]{3,2,1,0:T(8,128)S(1)} %bitcast.9), channel_id=1, source_target_pairs={{16,0},{32,16},{48,32},{64,48},{80,64},{96,80},{112,96},{128,112},... | collective-permute-start | bytes 1769480 | tf_op jit(solution)/shard_map/ppermute | solution.py:117
  15.6 10.1 %all-to-all-done.parts_ref = f32[16,9,8,128]{3,2,1,0:T(8,128)S(1)} async-done(((f32[16,9,8,128]{3,2,1,0:T(8,128)}), f32[16,9,8,128]{3,2,1,0:T(8,128)S(1)}, u32[]{:S(2)}, u32[]{:S(2)}) %all-to-all-start) | async-done | bytes 589856 | tf_op jit(solution)/shard_map/all_to_all | solution.py:103
  25.8 0.9 spread.2
  26.6 0.0 copy-start.1
  26.6 0.0 copy-start.6
  26.6 0.0 copy-start.7
  26.6 6.9 %all-to-all-start.1 = ((f32[16,9,8,128]{3,2,1,0:T(8,128)}), f32[16,9,8,128]{3,2,1,0:T(8,128)S(1)}, u32[]{:S(2)}, u32[]{:S(2)}) async-start(f32[16,9,8,128]{3,2,1,0:T(8,128)} %spread.2), calls=%async_computation.1 | async-start | bytes 1179648 | tf_op jit(solution)/shard_map/all_to_all | solution.py:106
  33.5 0.0 copy-start.8
  33.5 7.8 %collective-permute-done.low_ref = f32[8,3,48,128]{3,2,1,0:T(8,128)S(1)} collective-permute-done((f32[8,3,48,128]{3,2,1,0:T(8,128)S(1)}, f32[8,3,48,128]{3,2,1,0:T(8,128)S(1)}, u32[]{:S(2)}, u32[]{:S(2)}) %collective-permute-start) | collective-permute-done | bytes 589856 | tf_op jit(solution)/shard_map/ppermute | solution.py:116
  41.3 0.0 collective-permute-done.1.high_ref
  41.3 0.0 copy-start.4
  41.3 0.8 copy-done.4
  42.1 0.0 copy-done.1
  42.1 0.0 copy-done.6
  42.1 0.0 copy-done.7
  42.1 0.0 copy-done.8
  42.1 0.0 copy-start.5
  42.1 1.1 %copy-done.5 = f32[8,3,48,128]{3,2,1,0:T(8,128)S(1)} copy-done((f32[8,3,48,128]{3,2,1,0:T(8,128)S(1)}, f32[8,3,48,128]{3,2,1,0:T(8,128)}, u32[]{:S(2)}) %copy-start.5) | copy-done | bytes 589848
  43.2 2.3 %parts.2 = (f32[8,3,48,128]{3,2,1,0:T(8,128)S(1)}, f32[8,3,48,128]{3,2,1,0:T(8,128)S(1)}) custom-call(f32[8]{0:T(128)S(1)} %copy-done.8, f32[8,3,48,128]{3,2,1,0:T(8,128)S(1)} %bitcast.10, f32[8,3,48,128]{3,2,1,0:T(8,128)S(1)} %collective-permute-done.low_ref, f32[8,3,48,128]{3,2,1,0:T(8,128)S(1)} %copy-done.5, f32[3,3,48,128]{3,2,1,0:T(8,128)S(1)} %copy-done.6, ...), custom_call_target="tpu_custom_call" | custom-call | flops 10000000000 | tf_op jit(solution)/shard_map/parts/pallas_call | solution.py:107
  45.5 5.1 %all-to-all-done.1 = f32[16,9,8,128]{3,2,1,0:T(8,128)S(1)} async-done(((f32[16,9,8,128]{3,2,1,0:T(8,128)}), f32[16,9,8,128]{3,2,1,0:T(8,128)S(1)}, u32[]{:S(2)}, u32[]{:S(2)}) %all-to-all-start.1) | async-done | bytes 589856 | tf_op jit(solution)/shard_map/all_to_all | solution.py:106
  50.6 1.0 join.2.q_ref
  51.6 3.6 %all-to-all-start.2 = ((f32[16,9,8,128]{3,2,1,0:T(8,128)}), f32[16,9,8,128]{3,2,1,0:T(8,128)S(1)}, u32[]{:S(2)}, u32[]{:S(2)}) async-start(f32[16,9,8,128]{3,2,1,0:T(8,128)} %bitcast.4), calls=%async_computation.2 | async-start | bytes 1179648 | tf_op jit(solution)/shard_map/all_to_all | solution.py:103
  55.2 2.8 %collective-permute-start.2 = (f32[8,3,48,128]{3,2,1,0:T(8,128)}, f32[8,3,48,128]{3,2,1,0:T(8,128)S(1)}, u32[]{:S(2)}, u32[]{:S(2)}) collective-permute-start(f32[8,3,48,128]{3,2,1,0:T(8,128)} %join.2.q_ref), channel_id=1, source_target_pairs={{0,16},{16,32},{32,48},{48,64},{64,80},{80,96},{96,112},{112,128},... | collective-permute-start | bytes 1769480 | tf_op jit(solution)/shard_map/ppermute | solution.py:116
  57.9 7.3 %collective-permute-start.3 = (f32[8,3,48,128]{3,2,1,0:T(8,128)}, f32[8,3,48,128]{3,2,1,0:T(8,128)S(1)}, u32[]{:S(2)}, u32[]{:S(2)}) collective-permute-start(f32[8,3,48,128]{3,2,1,0:T(8,128)} %join.2.q_ref), channel_id=1, source_target_pairs={{16,0},{32,16},{48,32},{64,48},{80,64},{96,80},{112,96},{128,112},... | collective-permute-start | bytes 1769480 | tf_op jit(solution)/shard_map/ppermute | solution.py:117
  65.2 10.3 %all-to-all-done.2.parts_ref = f32[16,9,8,128]{3,2,1,0:T(8,128)S(1)} async-done(((f32[16,9,8,128]{3,2,1,0:T(8,128)}), f32[16,9,8,128]{3,2,1,0:T(8,128)S(1)}, u32[]{:S(2)}, u32[]{:S(2)}) %all-to-all-start.2) | async-done | bytes 589856 | tf_op jit(solution)/shard_map/all_to_all | solution.py:103
  75.5 0.9 spread.3
  76.4 6.5 %all-to-all-start.3 = ((f32[16,9,8,128]{3,2,1,0:T(8,128)}), f32[16,9,8,128]{3,2,1,0:T(8,128)S(1)}, u32[]{:S(2)}, u32[]{:S(2)}) async-start(f32[16,9,8,128]{3,2,1,0:T(8,128)} %spread.3), calls=%async_computation.3 | async-start | bytes 1179648 | tf_op jit(solution)/shard_map/all_to_all | solution.py:106
  82.9 9.0 %collective-permute-done.2.low_ref = f32[8,3,48,128]{3,2,1,0:T(8,128)S(1)} collective-permute-done((f32[8,3,48,128]{3,2,1,0:T(8,128)}, f32[8,3,48,128]{3,2,1,0:T(8,128)S(1)}, u32[]{:S(2)}, u32[]{:S(2)}) %collective-permute-start.2) | collective-permute-done | bytes 589856 | tf_op jit(solution)/shard_map/ppermute | solution.py:116
  91.9 0.0 collective-permute-done.3.high_ref
  91.9 0.0 copy-start.2
  91.9 0.8 copy-done.2
  92.7 0.0 copy-start.3
  92.7 1.1 %copy-done.3 = f32[8,3,48,128]{3,2,1,0:T(8,128)S(1)} copy-done((f32[8,3,48,128]{3,2,1,0:T(8,128)S(1)}, f32[8,3,48,128]{3,2,1,0:T(8,128)}, u32[]{:S(2)}) %copy-start.3) | copy-done | bytes 589848
  93.8 2.8 %parts.3 = (f32[8,3,48,128]{3,2,1,0:T(8,128)S(1)}, f32[8,3,48,128]{3,2,1,0:T(8,128)S(1)}) custom-call(f32[8]{0:T(128)S(1)} %copy-done.8, f32[8,3,48,128]{3,2,1,0:T(8,128)} %join.2.q_ref, f32[8,3,48,128]{3,2,1,0:T(8,128)S(1)} %collective-permute-done.2.low_ref, f32[8,3,48,128]{3,2,1,0:T(8,128)S(1)} %copy-done.3, f32[3,3,48,128]{3,2,1,0:T(8,128)S(1)} %copy-done.6, ...), custom_call_target="tpu_custom_call" | custom-call | flops 10000000000 | tf_op jit(solution)/shard_map/parts/pallas_call | solution.py:107
  96.6 3.5 %all-to-all-done.3 = f32[16,9,8,128]{3,2,1,0:T(8,128)S(1)} async-done(((f32[16,9,8,128]{3,2,1,0:T(8,128)}), f32[16,9,8,128]{3,2,1,0:T(8,128)S(1)}, u32[]{:S(2)}, u32[]{:S(2)}) %all-to-all-start.3) | async-done | bytes 589856 | tf_op jit(solution)/shard_map/all_to_all | solution.py:106
  100.1 1.0 %join.3 = f32[8,3,48,128]{3,2,1,0:T(8,128)} custom-call(f32[8,3,48,128]{3,2,1,0:T(8,128)S(1)} %get-tuple-element.11.base_ref, f32[8,3,48,128]{3,2,1,0:T(8,128)S(1)} %get-tuple-element.12.noise_ref, f32[3,48,128]{2,1,0:T(8,128)S(1)} %copy-done.1, f32[8,3,48,128]{3,2,1,0:T(8,128)S(1)} %bitcast.12, f32[8,3,48,128]{3,2,1,0:T(8,128)S(1)} %bitcast.11), custom_call_target="tpu_custom_call" | custom-call | tf_op jit(solution)/shard_map/join/pallas_call | solution.py:111
Async XLA Ops:
  0.0 5.6 %copy-start = (f32[1,8,3,48,128]{4,3,2,1,0:T(8,128)S(1)}, f32[1,8,3,48,128]{4,3,2,1,0:T(8,128)}, u32[]{:S(2)}) copy-start(f32[1,8,3,48,128]{4,3,2,1,0:T(8,128)} %param.5) | copy-start | bytes 1769476
  0.0 25.8 %all-to-all-start = ((f32[16,9,8,128]{3,2,1,0:T(8,128)}), f32[16,9,8,128]{3,2,1,0:T(8,128)S(1)}, u32[]{:S(2)}, u32[]{:S(2)}) async-start(f32[16,9,8,128]{3,2,1,0:T(8,128)} %bitcast.7), calls=%async_computation | async-start | bytes 1179648 | tf_op jit(solution)/shard_map/all_to_all | solution.py:103
  5.6 35.7 %collective-permute-start = (f32[8,3,48,128]{3,2,1,0:T(8,128)S(1)}, f32[8,3,48,128]{3,2,1,0:T(8,128)S(1)}, u32[]{:S(2)}, u32[]{:S(2)}) collective-permute-start(f32[8,3,48,128]{3,2,1,0:T(8,128)S(1)} %bitcast.8), channel_id=1, source_target_pairs={{0,16},{16,32},{32,48},{48,64},{64,80},{80,96},{96,112},{112,128},... | collective-permute-start | bytes 1769480 | tf_op jit(solution)/shard_map/ppermute | solution.py:116
  10.1 31.2 %collective-permute-start.1 = (f32[8,3,48,128]{3,2,1,0:T(8,128)S(1)}, f32[8,3,48,128]{3,2,1,0:T(8,128)S(1)}, u32[]{:S(2)}, u32[]{:S(2)}) collective-permute-start(f32[8,3,48,128]{3,2,1,0:T(8,128)S(1)} %bitcast.9), channel_id=1, source_target_pairs={{16,0},{32,16},{48,32},{64,48},{80,64},{96,80},{112,96},{128,112},... | collective-permute-start | bytes 1769480 | tf_op jit(solution)/shard_map/ppermute | solution.py:117
  26.6 15.5 %copy-start.1 = (f32[3,48,128]{2,1,0:T(8,128)S(1)}, f32[3,48,128]{2,1,0:T(8,128)}, u32[]{:S(2)}) copy-start(f32[3,48,128]{2,1,0:T(8,128)} %dif_ref.7) | copy-start | bytes 221188
  26.6 15.5 %copy-start.6 = (f32[3,3,48,128]{3,2,1,0:T(8,128)S(1)}, f32[3,3,48,128]{3,2,1,0:T(8,128)}, u32[]{:S(2)}) copy-start(f32[3,3,48,128]{3,2,1,0:T(8,128)} %vel_ref.3) | copy-start | bytes 663556
  26.6 15.5 %copy-start.7 = (f32[1,3,3,48,128]{4,3,2,1,0:T(8,128)S(1)}, f32[1,3,3,48,128]{4,3,2,1,0:T(8,128)}, u32[]{:S(2)}) copy-start(f32[1,3,3,48,128]{4,3,2,1,0:T(8,128)} %param.7) | copy-start | bytes 663556
  26.6 24.0 %all-to-all-start.1 = ((f32[16,9,8,128]{3,2,1,0:T(8,128)}), f32[16,9,8,128]{3,2,1,0:T(8,128)S(1)}, u32[]{:S(2)}, u32[]{:S(2)}) async-start(f32[16,9,8,128]{3,2,1,0:T(8,128)} %spread.2), calls=%async_computation.1 | async-start | bytes 1179648 | tf_op jit(solution)/shard_map/all_to_all | solution.py:106
  33.5 8.6 %copy-start.8 = (f32[8]{0:T(128)S(1)}, f32[8]{0:T(128)}, u32[]{:S(2)}) copy-start(f32[8]{0:T(128)} %stoich_ref.3) | copy-start | bytes 100
  41.3 0.8 copy-start.4
  42.1 1.1 %copy-start.5 = (f32[8,3,48,128]{3,2,1,0:T(8,128)S(1)}, f32[8,3,48,128]{3,2,1,0:T(8,128)}, u32[]{:S(2)}) copy-start(f32[8,3,48,128]{3,2,1,0:T(8,128)} %copy-done.4) | copy-start | bytes 1769476
  51.6 23.9 %all-to-all-start.2 = ((f32[16,9,8,128]{3,2,1,0:T(8,128)}), f32[16,9,8,128]{3,2,1,0:T(8,128)S(1)}, u32[]{:S(2)}, u32[]{:S(2)}) async-start(f32[16,9,8,128]{3,2,1,0:T(8,128)} %bitcast.4), calls=%async_computation.2 | async-start | bytes 1179648 | tf_op jit(solution)/shard_map/all_to_all | solution.py:103
  55.2 36.7 %collective-permute-start.2 = (f32[8,3,48,128]{3,2,1,0:T(8,128)}, f32[8,3,48,128]{3,2,1,0:T(8,128)S(1)}, u32[]{:S(2)}, u32[]{:S(2)}) collective-permute-start(f32[8,3,48,128]{3,2,1,0:T(8,128)} %join.2.q_ref), channel_id=1, source_target_pairs={{0,16},{16,32},{32,48},{48,64},{64,80},{80,96},{96,112},{112,128},... | collective-permute-start | bytes 1769480 | tf_op jit(solution)/shard_map/ppermute | solution.py:116
  57.9 34.0 %collective-permute-start.3 = (f32[8,3,48,128]{3,2,1,0:T(8,128)}, f32[8,3,48,128]{3,2,1,0:T(8,128)S(1)}, u32[]{:S(2)}, u32[]{:S(2)}) collective-permute-start(f32[8,3,48,128]{3,2,1,0:T(8,128)} %join.2.q_ref), channel_id=1, source_target_pairs={{16,0},{32,16},{48,32},{64,48},{80,64},{96,80},{112,96},{128,112},... | collective-permute-start | bytes 1769480 | tf_op jit(solution)/shard_map/ppermute | solution.py:117
  76.4 23.8 %all-to-all-start.3 = ((f32[16,9,8,128]{3,2,1,0:T(8,128)}), f32[16,9,8,128]{3,2,1,0:T(8,128)S(1)}, u32[]{:S(2)}, u32[]{:S(2)}) async-start(f32[16,9,8,128]{3,2,1,0:T(8,128)} %spread.3), calls=%async_computation.3 | async-start | bytes 1179648 | tf_op jit(solution)/shard_map/all_to_all | solution.py:106
  91.9 0.8 copy-start.2
  92.7 1.1 %copy-start.3 = (f32[8,3,48,128]{3,2,1,0:T(8,128)S(1)}, f32[8,3,48,128]{3,2,1,0:T(8,128)}, u32[]{:S(2)}) copy-start(f32[8,3,48,128]{3,2,1,0:T(8,128)} %copy-done.2) | copy-start | bytes 1769476

commit v4 on v3

v4 whole, which is shorter than its diff:
```python
import functools

import jax
import jax.numpy as jnp
from jax import lax
from jax.experimental import pallas as pl
from jax.experimental.pallas import tpu as pltpu
from jax.sharding import PartitionSpec as P

time_step = 0.3
mix_const = 5.0
pre_factor = 2.0
activation = 2.0

HBM = pl.BlockSpec(memory_space=pltpu.HBM)
SMEM = pl.BlockSpec(memory_space=pltpu.SMEM)
VMEM = pl.BlockSpec(memory_space=pltpu.VMEM)


FIELD_ROWS = [[(y * 4 + x) * 2 + c for x in range(4) for c in range(2)] for y in range(2)]


def call(kernel, out_shape, in_specs, scratch, flops, name, aliases={}):
    return pl.pallas_call(
        kernel,
        out_shape=out_shape,
        in_specs=in_specs,
        out_specs=jax.tree.map(lambda _: VMEM, out_shape),
        scratch_shapes=scratch,
        compiler_params=pltpu.CompilerParams(vmem_limit_bytes=16 * 2**20),
        cost_estimate=pl.CostEstimate(flops=flops, bytes_accessed=0, transcendentals=0),
        input_output_aliases=aliases,
        name=name,
    )


def sigmoid(x):
    return 1.0 / (1.0 + jnp.exp(-x))


def slope_of(at):
    up, down = at(1), at(-1)
    return 0.75 * (up - down) - 0.15 * (at(2) - at(-2)) + (1.0 / 60.0) * (at(3) - at(-3)), up + down


def inner_kernel(stoich_ref, q_ref, vel_ref, wie_ref, dif_ref, base_ref, noise_ref, react):
    scalars, planes = q_ref.shape[:2]
    for i in range(planes):
        theta = 1.0 + 3.0 * sigmoid(q_ref[scalars - 1, i])
        react[i] = (time_step * pre_factor) * q_ref[0, i] * q_ref[1, i] * jnp.exp(-activation / theta)

    def one(s, carry):
        for i in range(planes):
            q = q_ref[s, i]
            rows, lanes = q.shape
            slope_y, near_y = slope_of(lambda k: pltpu.roll(q, (-k) % rows, 0))
            slope_z, near_z = slope_of(lambda k: pltpu.roll(q, (-k) % lanes, 1))
            smooth = dif_ref[i] * (near_y + near_z - (6.0 + mix_const) * q)
            drift = vel_ref[1, i] * slope_y + vel_ref[2, i] * slope_z
            base_ref[s, i] = q + (time_step * (smooth - drift) + stoich_ref[s] * react[i])
            noise_ref[s, i] = wie_ref[1, i] * slope_y + wie_ref[2, i] * slope_z
        return carry

    lax.fori_loop(0, scalars, one, 0)


def outer_kernel(low_hbm, high_hbm, q_ref, base_ref, noise_ref, vel_ref, wie_ref, dif_ref, base_out, noise_out, low_ref, high_ref, sems):
    scalars, planes = q_ref.shape[:2]
    cuts = [pl.ds(0, scalars // 2), pl.ds(scalars // 2, scalars // 2)]
    pairs = ((low_hbm, low_ref), (high_hbm, high_ref))
    copies = [
        [pltpu.make_async_copy(a.at[cut], b.at[cut], sems.at[m, n]) for n, (a, b) in enumerate(pairs)]
        for m, cut in enumerate(cuts)
    ]
    for copy in copies[0] + copies[1]:
        copy.start()

    def one(s, carry):
        for i in range(planes):

            def along_x(k):
                j = i + k
                if j < 0:
                    return low_ref[s, j + planes]
                if j >= planes:
                    return high_ref[s, j - planes]
                return q_ref[s, j]

            slope, near = slope_of(along_x)
            base_out[s, i] = base_ref[s, i] + time_step * (dif_ref[i] * near - vel_ref[0, i] * slope)
            noise_out[s, i] = noise_ref[s, i] + wie_ref[0, i] * slope
        return carry

    for m in range(2):
        for copy in copies[m]:
            copy.wait()
        lax.fori_loop(m * (scalars // 2), (m + 1) * (scalars // 2), one, 0)


def join_kernel(fields, last, base_ref, noise_ref, dif_ref, own_ref, other_ref, *rest):
    out_ref = rest[-1]
    scalars, planes = base_ref.shape[:2]
    half = scalars // 2
    row = lax.axis_index("field") // 8

    def total(s, i):
        return jnp.where(row == s // half, own_ref[s % half, i], other_ref[s % half, i])

    for i in range(planes):
        dif = dif_ref[i]
        theta_bar = 1.0 + 3.0 * sigmoid(total(scalars - 1, i) * (1.0 / fields))
        amplitude = jnp.sqrt(2.0 * dif * theta_bar)
        pull = (time_step * mix_const / fields) * dif
        for s in range(scalars):
            new = base_ref[s, i] + (amplitude * noise_ref[s, i] + pull * total(s, i))
            out_ref[s, i] = 0.5 * rest[0][s, i] + 0.5 * new if last else new


def spread_kernel(parts_ref, out_ref):
    total = parts_ref[0]
    for n in range(1, parts_ref.shape[0]):
        total = total + parts_ref[n]
    for n in range(out_ref.shape[0]):
        out_ref[n] = total


def section(fields, stoich, q, velocity, wiener, diffusivity, phi=None):
    last = phi is not None
    like = jax.ShapeDtypeStruct(q.shape, q.dtype)
    low, high = neighbours(q)
    base, noise = call(
        inner_kernel, (like, like), [SMEM] + [VMEM] * 4, [pltpu.VMEM(q.shape[1:], jnp.float32)], 10**6, "inner"
    )(stoich, q, velocity, wiener, diffusivity)
    mark = q
    shares = mark.reshape(lax.axis_size("field"), -1, 8, q.shape[-1])
    received = lax.all_to_all(shares, "field", 0, 0)
    spread = call(spread_kernel, jax.ShapeDtypeStruct((8,) + shares.shape[1:], q.dtype), [VMEM], [], 0, "spread")(received)
    own = lax.all_to_all(spread, "field", 0, 0, axis_index_groups=FIELD_ROWS).reshape((-1,) + q.shape[1:])
    other = lax.ppermute(own, "field", [(i, i ^ 8) for i in range(16)])
    scratch = [pltpu.VMEM(q.shape, jnp.float32)] * 2 + [pltpu.SemaphoreType.DMA((2, 2))]
    base, noise = call(outer_kernel, (like, like), [HBM] * 2 + [VMEM] * 6, scratch, 10**10, "outer", {3: 0, 4: 1})(
        low, high, q, base, noise, velocity, wiener, diffusivity
    )
    args = (base, noise, diffusivity, own, other) + ((phi,) if last else ())
    return call(functools.partial(join_kernel, fields, last), like, [VMEM] * len(args), [], 0, "join")(*args)


def neighbours(q):
    count = lax.axis_size("space")
    low = lax.ppermute(q, "space", [(i, i + 1) for i in range(count - 1)])
    high = lax.ppermute(q, "space", [(i + 1, i) for i in range(count - 1)])
    return low, high


def local(phi, velocity, wiener, diffusivity, stoich):
    fields = phi.shape[0] * lax.axis_size("field")
    phi, wiener = phi[0], wiener[0]
    first = section(fields, stoich, phi, velocity, wiener, diffusivity)
    return section(fields, stoich, first, velocity, wiener, diffusivity, phi)[None]


def solution(mesh):
    return jax.shard_map(
        local,
        mesh=mesh,
        in_specs=(
            P("field", None, "space", None, None),
            P(None, "space", None, None),
            P("field", None, "space", None, None),
            P("space", None, None),
            P(),
        ),
        out_specs=P("field", None, "space", None, None),
        check_vma=False,
    )
```

time: 102 us -> 107 us (1.049)
  the two profiles are of different devices: /device:TPU:256 before, /device:TPU:8 now
where the time goes in v4:
time: 107 us
  waiting for transfers between devices  63.7 us (60%)
  starting transfers between devices  29.5 us (28%)
  Pallas kernels  12.6 us (12%)
    all_to_all x2, waiting for transfers between devices, section(): received = lax.all_to_all(shares, 'field', 0, 0)  41.2 us
    all_to_all x2, starting transfers between devices, section(): received = lax.all_to_all(shares, 'field', 0, 0)  13.3 us
    ppermute x2, waiting for transfers between devices, section(): other = lax.ppermute(own, 'field', [(i, i ^ 8) for i in range(16)])  12.6 us
    all_to_all x2, waiting for transfers between devices, section(): lax.all_to_all(spread, 'field', 0, 0, axis_index_groups=FIELD_ROWS)  9.98 us
    all_to_all x2, starting transfers between devices, section(): lax.all_to_all(spread, 'field', 0, 0, axis_index_groups=FIELD_ROWS)  6.98 us
    pallas_call x2, Pallas kernels, section(): call(inner_kernel, (like, like), [SMEM] + [VMEM] * 4, [pltpu.VMEM(q.shape...  4.96 us
    pallas_call x2, Pallas kernels, section(): call(outer_kernel, (like, like), [HBM] * 2 + [VMEM] * 6, scratch, 10 ** 1...  3.99 us
    ppermute x2, starting transfers between devices, section(): other = lax.ppermute(own, 'field', [(i, i ^ 8) for i in range(16)])  3.82 us
  transfers between devices with their start and end apart: 10, of which 6 were waited for; matrix products, arithmetic and copies ran while one was open for 0% of the time, Pallas kernels for 10%

profile of v4, /device:TPU:8, one launch (start us, length us, event | category | flops | bytes accessed | tf_op | source)
XLA Modules:
  0.0 106.5 jit_solution(6942539067591979191)
XLA Ops:
  0.0 0.0 copy-start
  0.0 9.4 %all-to-all-start = ((f32[16,9,8,128]{3,2,1,0:T(8,128)}), f32[16,9,8,128]{3,2,1,0:T(8,128)S(1)}, u32[]{:S(2)}, u32[]{:S(2)}) async-start(f32[16,9,8,128]{3,2,1,0:T(8,128)} %bitcast.7), calls=%async_computation | async-start | bytes 1179648 | tf_op jit(solution)/shard_map/all_to_all | solution.py:136
  9.4 0.0 copy-done
  9.4 1.3 %collective-permute-start = (f32[8,3,48,128]{3,2,1,0:T(8,128)S(1)}, f32[8,3,48,128]{3,2,1,0:T(8,128)S(1)}, u32[]{:S(2)}, u32[]{:S(2)}) collective-permute-start(f32[8,3,48,128]{3,2,1,0:T(8,128)S(1)} %bitcast.8), channel_id=1, source_target_pairs={{0,16},{16,32},{32,48},{48,64},{64,80},{80,96},{96,112},{112,128},... | collective-permute-start | bytes 1769480 | tf_op jit(solution)/shard_map/ppermute | solution.py:150
  10.7 1.3 %collective-permute-start.1 = (f32[8,3,48,128]{3,2,1,0:T(8,128)S(1)}, f32[8,3,48,128]{3,2,1,0:T(8,128)}, u32[]{:S(2)}, u32[]{:S(2)}) collective-permute-start(f32[8,3,48,128]{3,2,1,0:T(8,128)S(1)} %bitcast.9), channel_id=1, source_target_pairs={{16,0},{32,16},{48,32},{64,48},{80,64},{96,80},{112,96},{128,112},... | collective-permute-start | bytes 1769480 | tf_op jit(solution)/shard_map/ppermute | solution.py:151
  12.0 20.6 %all-to-all-done.parts_ref = f32[16,9,8,128]{3,2,1,0:T(8,128)S(1)} async-done(((f32[16,9,8,128]{3,2,1,0:T(8,128)}), f32[16,9,8,128]{3,2,1,0:T(8,128)S(1)}, u32[]{:S(2)}, u32[]{:S(2)}) %all-to-all-start) | async-done | bytes 589856 | tf_op jit(solution)/shard_map/all_to_all | solution.py:136
  32.7 0.8 spread.2
  33.4 0.0 copy-start.1
  33.4 0.0 copy-start.2
  33.4 0.0 copy-start.3
  33.4 3.6 %all-to-all-start.1 = ((f32[8,9,8,128]{3,2,1,0:T(8,128)}), f32[8,9,8,128]{3,2,1,0:T(8,128)S(1)}, u32[]{:S(2)}, u32[]{:S(2)}) async-start(f32[8,9,8,128]{3,2,1,0:T(8,128)} %spread.2), calls=%async_computation.1 | async-start | bytes 589824 | tf_op jit(solution)/shard_map/all_to_all | solution.py:138
  37.0 0.0 copy-start.4
  37.0 0.0 copy-done.1
  37.0 0.0 copy-done.2
  37.0 0.0 copy-done.3
  37.0 0.6 copy-done.4
  37.6 2.2 %inner.2 = (f32[8,3,48,128]{3,2,1,0:T(8,128)S(1)}, f32[8,3,48,128]{3,2,1,0:T(8,128)S(1)}) custom-call(f32[8]{0:T(128)S(1)} %copy-done.4, f32[8,3,48,128]{3,2,1,0:T(8,128)S(1)} %bitcast.10, f32[3,3,48,128]{3,2,1,0:T(8,128)S(1)} %copy-done.2, f32[3,3,48,128]{3,2,1,0:T(8,128)S(1)} %bitcast.17, f32[3,48,128]{2,1,0:T(8,128)S(1)} %copy-done.1), custom_call_target="tpu_custom_call" | custom-call | flops 1000000 | tf_op jit(solution)/shard_map/inner/pallas_call | solution.py:131
  39.9 4.9 %all-to-all-done.1 = f32[8,9,8,128]{3,2,1,0:T(8,128)S(1)} async-done(((f32[8,9,8,128]{3,2,1,0:T(8,128)}), f32[8,9,8,128]{3,2,1,0:T(8,128)S(1)}, u32[]{:S(2)}, u32[]{:S(2)}) %all-to-all-start.1) | async-done | bytes 294944 | tf_op jit(solution)/shard_map/all_to_all | solution.py:138
  44.8 1.9 %collective-permute-start.2 = (f32[4,3,48,128]{3,2,1,0:T(8,128)S(1)}, f32[4,3,48,128]{3,2,1,0:T(8,128)S(1)}, u32[]{:S(2)}, u32[]{:S(2)}) collective-permute-start(f32[4,3,48,128]{3,2,1,0:T(8,128)S(1)} %bitcast.15), channel_id=1, source_target_pairs={{0,8},{1,9},{2,10},{3,11},{4,12},{5,13},{6,14},{7,15},{8,0},{9,1},... | collective-permute-start | bytes 884744 | tf_op jit(solution)/shard_map/ppermute | solution.py:139
  46.7 0.0 collective-permute-done.low_hbm
  46.7 0.0 collective-permute-done.1.high_hbm
  46.7 1.5 %outer.2 = (f32[8,3,48,128]{3,2,1,0:T(8,128)S(1)}, f32[8,3,48,128]{3,2,1,0:T(8,128)S(1)}) custom-call(f32[8,3,48,128]{3,2,1,0:T(8,128)S(1)} %collective-permute-done.low_hbm, f32[8,3,48,128]{3,2,1,0:T(8,128)} %collective-permute-done.1.high_hbm, f32[8,3,48,128]{3,2,1,0:T(8,128)S(1)} %bitcast.11, ...), custom_call_target="tpu_custom_call", output_to_operand_aliasing={{0}: (3, {}), {1}: (4, {})} | custom-call | flops 10000000000 | tf_op jit(solution)/shard_map/outer/pallas_call | solution.py:141
  48.2 6.8 %collective-permute-done.2.other_ref = f32[4,3,48,128]{3,2,1,0:T(8,128)S(1)} collective-permute-done((f32[4,3,48,128]{3,2,1,0:T(8,128)S(1)}, f32[4,3,48,128]{3,2,1,0:T(8,128)S(1)}, u32[]{:S(2)}, u32[]{:S(2)}) %collective-permute-start.2) | collective-permute-done | bytes 294944 | tf_op jit(solution)/shard_map/ppermute | solution.py:139
  55.0 1.0 join.2.q_ref
  56.0 3.9 %all-to-all-start.2 = ((f32[16,9,8,128]{3,2,1,0:T(8,128)}), f32[16,9,8,128]{3,2,1,0:T(8,128)S(1)}, u32[]{:S(2)}, u32[]{:S(2)}) async-start(f32[16,9,8,128]{3,2,1,0:T(8,128)} %bitcast.4), calls=%async_computation.2 | async-start | bytes 1179648 | tf_op jit(solution)/shard_map/all_to_all | solution.py:136
  59.9 1.5 %collective-permute-start.3 = (f32[8,3,48,128]{3,2,1,0:T(8,128)}, f32[8,3,48,128]{3,2,1,0:T(8,128)S(1)}, u32[]{:S(2)}, u32[]{:S(2)}) collective-permute-start(f32[8,3,48,128]{3,2,1,0:T(8,128)} %join.2.q_ref), channel_id=1, source_target_pairs={{0,16},{16,32},{32,48},{48,64},{64,80},{80,96},{96,112},{112,128},... | collective-permute-start | bytes 1769480 | tf_op jit(solution)/shard_map/ppermute | solution.py:150
  61.4 1.3 %collective-permute-start.4 = (f32[8,3,48,128]{3,2,1,0:T(8,128)}, f32[8,3,48,128]{3,2,1,0:T(8,128)}, u32[]{:S(2)}, u32[]{:S(2)}) collective-permute-start(f32[8,3,48,128]{3,2,1,0:T(8,128)} %join.2.q_ref), channel_id=1, source_target_pairs={{16,0},{32,16},{48,32},{64,48},{80,64},{96,80},{112,96},{128,112},... | collective-permute-start | bytes 1769480 | tf_op jit(solution)/shard_map/ppermute | solution.py:151
  62.7 20.5 %all-to-all-done.2.parts_ref = f32[16,9,8,128]{3,2,1,0:T(8,128)S(1)} async-done(((f32[16,9,8,128]{3,2,1,0:T(8,128)}), f32[16,9,8,128]{3,2,1,0:T(8,128)S(1)}, u32[]{:S(2)}, u32[]{:S(2)}) %all-to-all-start.2) | async-done | bytes 589856 | tf_op jit(solution)/shard_map/all_to_all | solution.py:136
  83.2 0.8 spread.3
  84.0 3.4 %all-to-all-start.3 = ((f32[8,9,8,128]{3,2,1,0:T(8,128)}), f32[8,9,8,128]{3,2,1,0:T(8,128)S(1)}, u32[]{:S(2)}, u32[]{:S(2)}) async-start(f32[8,9,8,128]{3,2,1,0:T(8,128)} %spread.3), calls=%async_computation.3 | async-start | bytes 589824 | tf_op jit(solution)/shard_map/all_to_all | solution.py:138
  87.4 2.8 %inner.3 = (f32[8,3,48,128]{3,2,1,0:T(8,128)S(1)}, f32[8,3,48,128]{3,2,1,0:T(8,128)S(1)}) custom-call(f32[8]{0:T(128)S(1)} %copy-done.4, f32[8,3,48,128]{3,2,1,0:T(8,128)} %join.2.q_ref, f32[3,3,48,128]{3,2,1,0:T(8,128)S(1)} %copy-done.2, f32[3,3,48,128]{3,2,1,0:T(8,128)S(1)} %bitcast.19, f32[3,48,128]{2,1,0:T(8,128)S(1)} %copy-done.1), custom_call_target="tpu_custom_call" | custom-call | flops 1000000 | tf_op jit(solution)/shard_map/inner/pallas_call | solution.py:131
  90.2 5.1 %all-to-all-done.3 = f32[8,9,8,128]{3,2,1,0:T(8,128)S(1)} async-done(((f32[8,9,8,128]{3,2,1,0:T(8,128)}), f32[8,9,8,128]{3,2,1,0:T(8,128)S(1)}, u32[]{:S(2)}, u32[]{:S(2)}) %all-to-all-start.3) | async-done | bytes 294944 | tf_op jit(solution)/shard_map/all_to_all | solution.py:138
  95.2 1.9 %collective-permute-start.5 = (f32[4,3,48,128]{3,2,1,0:T(8,128)S(1)}, f32[4,3,48,128]{3,2,1,0:T(8,128)S(1)}, u32[]{:S(2)}, u32[]{:S(2)}) collective-permute-start(f32[4,3,48,128]{3,2,1,0:T(8,128)S(1)} %bitcast.13), channel_id=1, source_target_pairs={{0,8},{1,9},{2,10},{3,11},{4,12},{5,13},{6,14},{7,15},{8,0},{9,1},... | collective-permute-start | bytes 884744 | tf_op jit(solution)/shard_map/ppermute | solution.py:139
  97.1 0.0 collective-permute-done.3.low_hbm
  97.2 0.0 collective-permute-done.4.high_hbm
  97.2 2.5 %outer.3 = (f32[8,3,48,128]{3,2,1,0:T(8,128)S(1)}, f32[8,3,48,128]{3,2,1,0:T(8,128)S(1)}) custom-call(f32[8,3,48,128]{3,2,1,0:T(8,128)S(1)} %collective-permute-done.3.low_hbm, f32[8,3,48,128]{3,2,1,0:T(8,128)} %collective-permute-done.4.high_hbm, f32[8,3,48,128]{3,2,1,0:T(8,128)} %join.2.q_ref, ...), custom_call_target="tpu_custom_call", output_to_operand_aliasing={{0}: (3, {}), {1}: (4, {})} | custom-call | flops 10000000000 | tf_op jit(solution)/shard_map/outer/pallas_call | solution.py:141
  99.7 5.7 %collective-permute-done.5.other_ref = f32[4,3,48,128]{3,2,1,0:T(8,128)S(1)} collective-permute-done((f32[4,3,48,128]{3,2,1,0:T(8,128)S(1)}, f32[4,3,48,128]{3,2,1,0:T(8,128)S(1)}, u32[]{:S(2)}, u32[]{:S(2)}) %collective-permute-start.5) | collective-permute-done | bytes 294944 | tf_op jit(solution)/shard_map/ppermute | solution.py:139
  105.5 1.1 %join.3 = f32[8,3,48,128]{3,2,1,0:T(8,128)} custom-call(f32[8,3,48,128]{3,2,1,0:T(8,128)S(1)} %get-tuple-element.19.base_ref, f32[8,3,48,128]{3,2,1,0:T(8,128)S(1)} %get-tuple-element.20.noise_ref, f32[3,48,128]{2,1,0:T(8,128)S(1)} %copy-done.1, f32[4,3,48,128]{3,2,1,0:T(8,128)S(1)} %bitcast.14, f32[4,3,48,128]{3,2,1,0:T(8,128)S(1)} %collective-permute-done.5.other_ref, ...), custom_call_target="tpu_custom_call" | custom-call | tf_op jit(solution)/shard_map/join/pallas_call | solution.py:145
Async XLA Ops:
  0.0 9.4 %copy-start = (f32[1,8,3,48,128]{4,3,2,1,0:T(8,128)S(1)}, f32[1,8,3,48,128]{4,3,2,1,0:T(8,128)}, u32[]{:S(2)}) copy-start(f32[1,8,3,48,128]{4,3,2,1,0:T(8,128)} %param.5) | copy-start | bytes 1769476
  0.0 32.7 %all-to-all-start = ((f32[16,9,8,128]{3,2,1,0:T(8,128)}), f32[16,9,8,128]{3,2,1,0:T(8,128)S(1)}, u32[]{:S(2)}, u32[]{:S(2)}) async-start(f32[16,9,8,128]{3,2,1,0:T(8,128)} %bitcast.7), calls=%async_computation | async-start | bytes 1179648 | tf_op jit(solution)/shard_map/all_to_all | solution.py:136
  9.4 37.3 %collective-permute-start = (f32[8,3,48,128]{3,2,1,0:T(8,128)S(1)}, f32[8,3,48,128]{3,2,1,0:T(8,128)S(1)}, u32[]{:S(2)}, u32[]{:S(2)}) collective-permute-start(f32[8,3,48,128]{3,2,1,0:T(8,128)S(1)} %bitcast.8), channel_id=1, source_target_pairs={{0,16},{16,32},{32,48},{48,64},{64,80},{80,96},{96,112},{112,128},... | collective-permute-start | bytes 1769480 | tf_op jit(solution)/shard_map/ppermute | solution.py:150
  10.7 36.0 %collective-permute-start.1 = (f32[8,3,48,128]{3,2,1,0:T(8,128)S(1)}, f32[8,3,48,128]{3,2,1,0:T(8,128)}, u32[]{:S(2)}, u32[]{:S(2)}) collective-permute-start(f32[8,3,48,128]{3,2,1,0:T(8,128)S(1)} %bitcast.9), channel_id=1, source_target_pairs={{16,0},{32,16},{48,32},{64,48},{80,64},{96,80},{112,96},{128,112},... | collective-permute-start | bytes 1769480 | tf_op jit(solution)/shard_map/ppermute | solution.py:151
  33.4 3.6 %copy-start.1 = (f32[3,48,128]{2,1,0:T(8,128)S(1)}, f32[3,48,128]{2,1,0:T(8,128)}, u32[]{:S(2)}) copy-start(f32[3,48,128]{2,1,0:T(8,128)} %dif_ref.11) | copy-start | bytes 221188
  33.4 3.6 %copy-start.2 = (f32[3,3,48,128]{3,2,1,0:T(8,128)S(1)}, f32[3,3,48,128]{3,2,1,0:T(8,128)}, u32[]{:S(2)}) copy-start(f32[3,3,48,128]{3,2,1,0:T(8,128)} %vel_ref.7) | copy-start | bytes 663556
  33.4 3.6 %copy-start.3 = (f32[1,3,3,48,128]{4,3,2,1,0:T(8,128)S(1)}, f32[1,3,3,48,128]{4,3,2,1,0:T(8,128)}, u32[]{:S(2)}) copy-start(f32[1,3,3,48,128]{4,3,2,1,0:T(8,128)} %param.7) | copy-start | bytes 663556
  33.4 11.4 %all-to-all-start.1 = ((f32[8,9,8,128]{3,2,1,0:T(8,128)}), f32[8,9,8,128]{3,2,1,0:T(8,128)S(1)}, u32[]{:S(2)}, u32[]{:S(2)}) async-start(f32[8,9,8,128]{3,2,1,0:T(8,128)} %spread.2), calls=%async_computation.1 | async-start | bytes 589824 | tf_op jit(solution)/shard_map/all_to_all | solution.py:138
  37.0 0.7 copy-start.4
  44.8 10.2 %collective-permute-start.2 = (f32[4,3,48,128]{3,2,1,0:T(8,128)S(1)}, f32[4,3,48,128]{3,2,1,0:T(8,128)S(1)}, u32[]{:S(2)}, u32[]{:S(2)}) collective-permute-start(f32[4,3,48,128]{3,2,1,0:T(8,128)S(1)} %bitcast.15), channel_id=1, source_target_pairs={{0,8},{1,9},{2,10},{3,11},{4,12},{5,13},{6,14},{7,15},{8,0},{9,1},... | collective-permute-start | bytes 884744 | tf_op jit(solution)/shard_map/ppermute | solution.py:139
  56.0 27.2 %all-to-all-start.2 = ((f32[16,9,8,128]{3,2,1,0:T(8,128)}), f32[16,9,8,128]{3,2,1,0:T(8,128)S(1)}, u32[]{:S(2)}, u32[]{:S(2)}) async-start(f32[16,9,8,128]{3,2,1,0:T(8,128)} %bitcast.4), calls=%async_computation.2 | async-start | bytes 1179648 | tf_op jit(solution)/shard_map/all_to_all | solution.py:136
  59.9 37.2 %collective-permute-start.3 = (f32[8,3,48,128]{3,2,1,0:T(8,128)}, f32[8,3,48,128]{3,2,1,0:T(8,128)S(1)}, u32[]{:S(2)}, u32[]{:S(2)}) collective-permute-start(f32[8,3,48,128]{3,2,1,0:T(8,128)} %join.2.q_ref), channel_id=1, source_target_pairs={{0,16},{16,32},{32,48},{48,64},{64,80},{80,96},{96,112},{112,128},... | collective-permute-start | bytes 1769480 | tf_op jit(solution)/shard_map/ppermute | solution.py:150
  61.4 35.8 %collective-permute-start.4 = (f32[8,3,48,128]{3,2,1,0:T(8,128)}, f32[8,3,48,128]{3,2,1,0:T(8,128)}, u32[]{:S(2)}, u32[]{:S(2)}) collective-permute-start(f32[8,3,48,128]{3,2,1,0:T(8,128)} %join.2.q_ref), channel_id=1, source_target_pairs={{16,0},{32,16},{48,32},{64,48},{80,64},{96,80},{112,96},{128,112},... | collective-permute-start | bytes 1769480 | tf_op jit(solution)/shard_map/ppermute | solution.py:151
  84.0 11.2 %all-to-all-start.3 = ((f32[8,9,8,128]{3,2,1,0:T(8,128)}), f32[8,9,8,128]{3,2,1,0:T(8,128)S(1)}, u32[]{:S(2)}, u32[]{:S(2)}) async-start(f32[8,9,8,128]{3,2,1,0:T(8,128)} %spread.3), calls=%async_computation.3 | async-start | bytes 589824 | tf_op jit(solution)/shard_map/all_to_all | solution.py:138
  95.2 10.2 %collective-permute-start.5 = (f32[4,3,48,128]{3,2,1,0:T(8,128)S(1)}, f32[4,3,48,128]{3,2,1,0:T(8,128)S(1)}, u32[]{:S(2)}, u32[]{:S(2)}) collective-permute-start(f32[4,3,48,128]{3,2,1,0:T(8,128)S(1)} %bitcast.13), channel_id=1, source_target_pairs={{0,8},{1,9},{2,10},{3,11},{4,12},{5,13},{6,14},{7,15},{8,0},{9,1},... | collective-permute-start | bytes 884744 | tf_op jit(solution)/shard_map/ppermute | solution.py:139

commit v5 on v4

--- a/solution.py
+++ b/solution.py
@@ -12,12 +12,15 @@
 pre_factor = 2.0
 activation = 2.0
 
+EARLY = 6
+
 HBM = pl.BlockSpec(memory_space=pltpu.HBM)
 SMEM = pl.BlockSpec(memory_space=pltpu.SMEM)
 VMEM = pl.BlockSpec(memory_space=pltpu.VMEM)
 
 
 FIELD_ROWS = [[(y * 4 + x) * 2 + c for x in range(4) for c in range(2)] for y in range(2)]
+BY_X = [[(y * 4 + x) * 2 + c for x in range(4)] for y in range(2) for c in range(2)]
 
 
 def call(kernel, out_shape, in_specs, scratch, flops, name, aliases={}):
@@ -64,14 +67,16 @@
     lax.fori_loop(0, scalars, one, 0)
 
 
-def outer_kernel(low_hbm, high_hbm, q_ref, base_ref, noise_ref, vel_ref, wie_ref, dif_ref, base_out, noise_out, low_ref, high_ref, sems):
+def outer_kernel(count, *refs):
+    halo, (q_ref, base_ref, noise_ref, vel_ref, wie_ref, dif_ref, base_out, noise_out, low_ref, high_ref, sems) = refs[:count], refs[count:]
     scalars, planes = q_ref.shape[:2]
-    cuts = [pl.ds(0, scalars // 2), pl.ds(scalars // 2, scalars // 2)]
-    pairs = ((low_hbm, low_ref), (high_hbm, high_ref))
-    copies = [
-        [pltpu.make_async_copy(a.at[cut], b.at[cut], sems.at[m, n]) for n, (a, b) in enumerate(pairs)]
-        for m, cut in enumerate(cuts)
-    ]
+    edge = EARLY if count == 4 else scalars // 2
+    cuts = [(0, edge), (edge, scalars)]
+    copies = []
+    for m, (at, end) in enumerate(cuts):
+        lot = halo[2 * m : 2 * m + 2] if count == 4 else [ref.at[pl.ds(at, end - at)] for ref in halo]
+        whole = [ref.at[pl.ds(at, end - at)] for ref in (low_ref, high_ref)]
+        copies.append([pltpu.make_async_copy(a, b, sems.at[m, n]) for n, (a, b) in enumerate(zip(lot, whole))])
     for copy in copies[0] + copies[1]:
         copy.start()
 
@@ -94,17 +99,17 @@
     for m in range(2):
         for copy in copies[m]:
             copy.wait()
-        lax.fori_loop(m * (scalars // 2), (m + 1) * (scalars // 2), one, 0)
-
-
-def join_kernel(fields, last, base_ref, noise_ref, dif_ref, own_ref, other_ref, *rest):
-    out_ref = rest[-1]
+        lax.fori_loop(*cuts[m], one, 0)
+
+
+def join_kernel(fields, last, base_ref, noise_ref, dif_ref, *rest):
     scalars, planes = base_ref.shape[:2]
-    half = scalars // 2
-    row = lax.axis_index("field") // 8
+    core = lax.axis_index("field") % 2
 
     def total(s, i):
-        return jnp.where(row == s // half, own_ref[s % half, i], other_ref[s % half, i])
+        if last:
+            return rest[0][s, i]
+        return jnp.where(core == s % 2, rest[0][s // 2, i], rest[1][s // 2, i])
 
     for i in range(planes):
         dif = dif_ref[i]
@@ -113,7 +118,7 @@
         pull = (time_step * mix_const / fields) * dif
         for s in range(scalars):
             new = base_ref[s, i] + (amplitude * noise_ref[s, i] + pull * total(s, i))
-            out_ref[s, i] = 0.5 * rest[0][s, i] + 0.5 * new if last else new
+            rest[2][s, i] = 0.5 * rest[1][s, i] + 0.5 * new if last else new
 
 
 def spread_kernel(parts_ref, out_ref):
@@ -124,25 +129,49 @@
         out_ref[n] = total
 
 
+def add_kernel(a_ref, b_ref, out_ref):
+    for n in range(out_ref.shape[0]):
+        out_ref[n] = a_ref[n] + b_ref[n]
+
+
+def flip(a, bit):
+    return lax.ppermute(a, "field", [(i, i ^ bit) for i in range(16)])
+
+
 def section(fields, stoich, q, velocity, wiener, diffusivity, phi=None):
     last = phi is not None
-    like = jax.ShapeDtypeStruct(q.shape, q.dtype)
-    low, high = neighbours(q)
+    scalars = q.shape[0]
+    like = lambda *lead: jax.ShapeDtypeStruct(lead + q.shape[1:], q.dtype)
+    halo = neighbours(q if last else q[:EARLY])
     base, noise = call(
-        inner_kernel, (like, like), [SMEM] + [VMEM] * 4, [pltpu.VMEM(q.shape[1:], jnp.float32)], 10**6, "inner"
+        inner_kernel, (like(scalars),) * 2, [SMEM] + [VMEM] * 4, [pltpu.VMEM(q.shape[1:], jnp.float32)], 10**6, "inner"
     )(stoich, q, velocity, wiener, diffusivity)
-    mark = q
-    shares = mark.reshape(lax.axis_size("field"), -1, 8, q.shape[-1])
-    received = lax.all_to_all(shares, "field", 0, 0)
-    spread = call(spread_kernel, jax.ShapeDtypeStruct((8,) + shares.shape[1:], q.dtype), [VMEM], [], 0, "spread")(received)
-    own = lax.all_to_all(spread, "field", 0, 0, axis_index_groups=FIELD_ROWS).reshape((-1,) + q.shape[1:])
-    other = lax.ppermute(own, "field", [(i, i ^ 8) for i in range(16)])
+    if last:
+        shares = q.reshape(lax.axis_size("field"), -1, 8, q.shape[-1])
+        received = lax.all_to_all(shares, "field", 0, 0)
+        spread = call(spread_kernel, jax.ShapeDtypeStruct(shares.shape, q.dtype), [VMEM], [], 0, "spread")(received)
+        totals = (lax.all_to_all(spread, "field", 0, 0).reshape(q.shape),)
+    else:
+        received = lax.all_to_all(q, "field", 0, 0, axis_index_groups=FIELD_ROWS)
+        spread = call(spread_kernel, like(4), [VMEM], [], 0, "spread")(received)
+        part = lax.all_to_all(spread, "field", 0, 0, axis_index_groups=BY_X)
+        part, late = lax.optimization_barrier((part, q[EARLY:]))
+        own = call(add_kernel, like(4), [VMEM] * 2, [], 0, "add")(part, flip(part, 8))
+        halo += neighbours(late)
+        totals = (own, flip(own, 1))
     scratch = [pltpu.VMEM(q.shape, jnp.float32)] * 2 + [pltpu.SemaphoreType.DMA((2, 2))]
-    base, noise = call(outer_kernel, (like, like), [HBM] * 2 + [VMEM] * 6, scratch, 10**10, "outer", {3: 0, 4: 1})(
-        low, high, q, base, noise, velocity, wiener, diffusivity
-    )
-    args = (base, noise, diffusivity, own, other) + ((phi,) if last else ())
-    return call(functools.partial(join_kernel, fields, last), like, [VMEM] * len(args), [], 0, "join")(*args)
+    count = len(halo)
+    base, noise = call(
+        functools.partial(outer_kernel, count),
+        (like(scalars),) * 2,
+        [HBM] * count + [VMEM] * 6,
+        scratch,
+        10**10,
+        "outer",
+        {count + 1: 0, count + 2: 1},
+    )(*halo, q, base, noise, velocity, wiener, diffusivity)
+    args = (base, noise, diffusivity) + totals + ((phi,) if last else ())
+    return call(functools.partial(join_kernel, fields, last), like(scalars), [VMEM] * len(args), [], 0, "join")(*args)
 
 
 def neighbours(q):

time: 107 us -> 103 us (0.963)
  the two profiles are of different devices: /device:TPU:8 before, /device:TPU:240 now
where the time goes in v5:
time: 103 us; the launch traced here: 102 us
  starting transfers between devices  49.4 us (48%)
  waiting for transfers between devices  39.6 us (38%)
  Pallas kernels  12.5 us (12%)
    ppermute x3, starting transfers between devices, neighbours(): low = lax.ppermute(q, 'space', [(i, i + 1) for i in range(count - 1)])  14.4 us
    all_to_all x1, waiting for transfers between devices, section(): received = lax.all_to_all(shares, 'field', 0, 0)  12.4 us
    all_to_all x1, starting transfers between devices, section(): received = lax.all_to_all(shares, 'field', 0, 0)  8.47 us
    ppermute x3, waiting for transfers between devices, neighbours(): high = lax.ppermute(q, 'space', [(i + 1, i) for i in range(count - 1)])  7.45 us
    all_to_all x1, starting transfers between devices, section(): totals = (lax.all_to_all(spread, 'field', 0, 0).reshape(q.shape),)  7.14 us
    all_to_all x1, waiting for transfers between devices, section(): part = lax.all_to_all(spread, 'field', 0, 0, axis_index_groups=BY_X)  7.01 us
    ppermute x3, starting transfers between devices, neighbours(): high = lax.ppermute(q, 'space', [(i + 1, i) for i in range(count - 1)])  6.94 us
    pallas_call x2, Pallas kernels, section(): call(inner_kernel, (like(scalars),) * 2, [SMEM] + [VMEM] * 4, [pltpu.VMEM...  4.97 us
  transfers between devices with their start and end apart: 12, of which 8 were waited for; matrix products, arithmetic and copies ran while one was open for 0% of the time, Pallas kernels for 10%

profile of v5, /device:TPU:240, one launch (start us, length us, event | category | flops | bytes accessed | tf_op | source)
XLA Modules:
  0.0 101.9 jit_solution(17657512617441147546)
XLA Ops:
  0.0 0.0 copy-start
  0.0 4.4 %all-to-all-start = ((f32[8,3,48,128]{3,2,1,0:T(8,128)}), f32[8,3,48,128]{3,2,1,0:T(8,128)S(1)}, u32[]{:S(2)}, u32[]{:S(2)}) async-start(f32[8,3,48,128]{3,2,1,0:T(8,128)} %bitcast.9), calls=%async_computation | async-start | bytes 1179648 | tf_op jit(solution)/shard_map/all_to_all | solution.py:155
  4.4 0.0 copy-done
  4.5 4.8 %collective-permute-start = (f32[6,3,48,128]{3,2,1,0:T(8,128)S(1)}, f32[6,3,48,128]{3,2,1,0:T(8,128)S(1)}, u32[]{:S(2)}, u32[]{:S(2)}) collective-permute-start(f32[6,3,48,128]{3,2,1,0:T(8,128)S(1)} %slice_bitcast_fusion), channel_id=1, source_target_pairs={{0,16},{16,32},{32,48},{48,64},{64,80},{80,96},{96,112},{112,128},... | collective-permute-start | bytes 1327112 | tf_op jit(solution)/shard_map/ppermute | solution.py:179
  9.3 1.9 %collective-permute-start.1 = (f32[6,3,48,128]{3,2,1,0:T(8,128)S(1)}, f32[6,3,48,128]{3,2,1,0:T(8,128)S(1)}, u32[]{:S(2)}, u32[]{:S(2)}) collective-permute-start(f32[6,3,48,128]{3,2,1,0:T(8,128)S(1)} %slice_bitcast_fusion), channel_id=1, source_target_pairs={{16,0},{32,16},{48,32},{64,48},{80,64},{96,80},{112,96},{128,112},... | collective-permute-start | bytes 1327112 | tf_op jit(solution)/shard_map/ppermute | solution.py:180
  11.2 4.2 %all-to-all-done.parts_ref = f32[8,3,48,128]{3,2,1,0:T(8,128)S(1)} async-done(((f32[8,3,48,128]{3,2,1,0:T(8,128)}), f32[8,3,48,128]{3,2,1,0:T(8,128)S(1)}, u32[]{:S(2)}, u32[]{:S(2)}) %all-to-all-start) | async-done | bytes 589856 | tf_op jit(solution)/shard_map/all_to_all | solution.py:155
  15.5 0.7 spread.2
  16.2 0.0 copy-start.3
  16.2 3.6 %all-to-all-start.1 = ((f32[4,3,48,128]{3,2,1,0:T(8,128)}), f32[4,3,48,128]{3,2,1,0:T(8,128)S(1)}, u32[]{:S(2)}, u32[]{:S(2)}) async-start(f32[4,3,48,128]{3,2,1,0:T(8,128)} %spread.2), calls=%async_computation.1 | async-start | bytes 589824 | tf_op jit(solution)/shard_map/all_to_all | solution.py:157
  19.8 0.0 copy-start.1
  19.8 0.0 copy-start.2
  19.9 0.0 copy-start.4
  19.9 7.0 %all-to-all-done.1.a_ref = f32[4,3,48,128]{3,2,1,0:T(8,128)S(1)} async-done(((f32[4,3,48,128]{3,2,1,0:T(8,128)}), f32[4,3,48,128]{3,2,1,0:T(8,128)S(1)}, u32[]{:S(2)}, u32[]{:S(2)}) %all-to-all-start.1) | async-done | bytes 294944 | tf_op jit(solution)/shard_map/all_to_all | solution.py:157
  26.9 2.6 %collective-permute-start.4 = (f32[4,3,48,128]{3,2,1,0:T(8,128)S(1)}, f32[4,3,48,128]{3,2,1,0:T(8,128)S(1)}, u32[]{:S(2)}, u32[]{:S(2)}) collective-permute-start(f32[4,3,48,128]{3,2,1,0:T(8,128)S(1)} %all-to-all-done.1.a_ref), channel_id=1, source_target_pairs={{0,8},{1,9},{2,10},{3,11},{4,12},{5,13},{6,14},{7,15},{8,0},{9,1},... | collective-permute-start | bytes 884744 | tf_op jit(solution)/shard_map/ppermute | solution.py:138
  29.5 5.9 %collective-permute-start.2 = (f32[2,3,48,128]{3,2,1,0:T(8,128)S(1)}, f32[2,3,48,128]{3,2,1,0:T(8,128)S(1)}, u32[]{:S(2)}, u32[]{:S(2)}) collective-permute-start(f32[2,3,48,128]{3,2,1,0:T(8,128)S(1)} %slice_bitcast_fusion.1), channel_id=1, source_target_pairs={{0,16},{16,32},{32,48},{48,64},{64,80},{80,96},{96,112},{112,128},... | collective-permute-start | bytes 442376 | tf_op jit(solution)/shard_map/ppermute | solution.py:179
  35.4 1.9 %collective-permute-start.3 = (f32[2,3,48,128]{3,2,1,0:T(8,128)S(1)}, f32[2,3,48,128]{3,2,1,0:T(8,128)S(1)}, u32[]{:S(2)}, u32[]{:S(2)}) collective-permute-start(f32[2,3,48,128]{3,2,1,0:T(8,128)S(1)} %slice_bitcast_fusion.1), channel_id=1, source_target_pairs={{16,0},{32,16},{48,32},{64,48},{80,64},{96,80},{112,96},{128,112},... | collective-permute-start | bytes 442376 | tf_op jit(solution)/shard_map/ppermute | solution.py:180
  37.3 0.0 copy-done.3
  37.3 0.0 copy-done.1
  37.3 0.0 copy-done.2
  37.3 0.0 copy-done.4
  37.4 2.2 %inner.2 = (f32[8,3,48,128]{3,2,1,0:T(8,128)S(1)}, f32[8,3,48,128]{3,2,1,0:T(8,128)S(1)}) custom-call(f32[8]{0:T(128)S(1)} %copy-done.4, f32[8,3,48,128]{3,2,1,0:T(8,128)S(1)} %bitcast.10, f32[3,3,48,128]{3,2,1,0:T(8,128)S(1)} %copy-done.2, f32[3,3,48,128]{3,2,1,0:T(8,128)S(1)} %bitcast.14, f32[3,48,128]{2,1,0:T(8,128)S(1)} %copy-done.1), custom_call_target="tpu_custom_call" | custom-call | flops 1000000 | tf_op jit(solution)/shard_map/inner/pallas_call | solution.py:146
  39.6 2.9 %collective-permute-done.4.b_ref = f32[4,3,48,128]{3,2,1,0:T(8,128)S(1)} collective-permute-done((f32[4,3,48,128]{3,2,1,0:T(8,128)S(1)}, f32[4,3,48,128]{3,2,1,0:T(8,128)S(1)}, u32[]{:S(2)}, u32[]{:S(2)}) %collective-permute-start.4) | collective-permute-done | bytes 294944 | tf_op jit(solution)/shard_map/ppermute | solution.py:138
  42.6 1.9 %collective-permute-start.5 = (f32[4,3,48,128]{3,2,1,0:T(8,128)S(1)}, f32[4,3,48,128]{3,2,1,0:T(8,128)S(1)}, u32[]{:S(2)}, u32[]{:S(2)}) collective-permute-start(f32[4,3,48,128]{3,2,1,0:T(8,128)S(1)} %add.1.rest_0_), channel_id=1, source_target_pairs={{0,1},{1,0},{2,3},{3,2},{4,5},{5,4},{6,7},{7,6},{8,9},{9,8},{10,11... | collective-permute-start | bytes 884744 | tf_op jit(solution)/shard_map/ppermute | solution.py:138
  44.5 0.0 collective-permute-done.refs_0_
  44.5 0.0 collective-permute-done.1.refs_1_
  44.5 0.0 collective-permute-done.2.refs_2_
  44.5 2.2 %collective-permute-done.3.refs_3_ = f32[2,3,48,128]{3,2,1,0:T(8,128)S(1)} collective-permute-done((f32[2,3,48,128]{3,2,1,0:T(8,128)S(1)}, f32[2,3,48,128]{3,2,1,0:T(8,128)S(1)}, u32[]{:S(2)}, u32[]{:S(2)}) %collective-permute-start.3) | collective-permute-done | bytes 147488 | tf_op jit(solution)/shard_map/ppermute | solution.py:180
  46.7 1.3 %outer.2 = (f32[8,3,48,128]{3,2,1,0:T(8,128)S(1)}, f32[8,3,48,128]{3,2,1,0:T(8,128)S(1)}) custom-call(f32[6,3,48,128]{3,2,1,0:T(8,128)S(1)} %collective-permute-done.refs_0_, f32[6,3,48,128]{3,2,1,0:T(8,128)S(1)} %collective-permute-done.1.refs_1_, ...), custom_call_target="tpu_custom_call", output_to_operand_aliasing={{0}: (5, {}), {1}: (6, {})} | custom-call | flops 10000000000 | tf_op jit(solution)/shard_map/outer/pallas_call | solution.py:164
  48.1 0.0 collective-permute-done.5.rest_1_
  48.1 1.0 join.2.q_ref.refs_2_
  49.1 8.5 %all-to-all-start.2 = ((f32[16,9,8,128]{3,2,1,0:T(8,128)}), f32[16,9,8,128]{3,2,1,0:T(8,128)S(1)}, u32[]{:S(2)}, u32[]{:S(2)}) async-start(f32[16,9,8,128]{3,2,1,0:T(8,128)} %bitcast.4), calls=%async_computation.2 | async-start | bytes 1179648 | tf_op jit(solution)/shard_map/all_to_all | solution.py:151
  57.6 3.7 %collective-permute-start.6 = (f32[8,3,48,128]{3,2,1,0:T(8,128)}, f32[8,3,48,128]{3,2,1,0:T(8,128)S(1)}, u32[]{:S(2)}, u32[]{:S(2)}) collective-permute-start(f32[8,3,48,128]{3,2,1,0:T(8,128)} %join.2.q_ref.refs_2_), channel_id=1, source_target_pairs={{0,16},{16,32},{32,48},{48,64},{64,80},{80,96},{96,112},{112,128},... | collective-permute-start | bytes 1769480 | tf_op jit(solution)/shard_map/ppermute | solution.py:179
  61.2 3.1 %collective-permute-start.7 = (f32[8,3,48,128]{3,2,1,0:T(8,128)}, f32[8,3,48,128]{3,2,1,0:T(8,128)}, u32[]{:S(2)}, u32[]{:S(2)}) collective-permute-start(f32[8,3,48,128]{3,2,1,0:T(8,128)} %join.2.q_ref.refs_2_), channel_id=1, source_target_pairs={{16,0},{32,16},{48,32},{64,48},{80,64},{96,80},{112,96},{128,112},... | collective-permute-start | bytes 1769480 | tf_op jit(solution)/shard_map/ppermute | solution.py:180
  64.3 12.4 %all-to-all-done.2.parts_ref = f32[16,9,8,128]{3,2,1,0:T(8,128)S(1)} async-done(((f32[16,9,8,128]{3,2,1,0:T(8,128)}), f32[16,9,8,128]{3,2,1,0:T(8,128)S(1)}, u32[]{:S(2)}, u32[]{:S(2)}) %all-to-all-start.2) | async-done | bytes 589856 | tf_op jit(solution)/shard_map/all_to_all | solution.py:151
  76.7 0.9 spread.3
  77.6 7.1 %all-to-all-start.3 = ((f32[16,9,8,128]{3,2,1,0:T(8,128)}), f32[16,9,8,128]{3,2,1,0:T(8,128)S(1)}, u32[]{:S(2)}, u32[]{:S(2)}) async-start(f32[16,9,8,128]{3,2,1,0:T(8,128)} %spread.3), calls=%async_computation.3 | async-start | bytes 1179648 | tf_op jit(solution)/shard_map/all_to_all | solution.py:153
  84.8 2.8 %inner.3 = (f32[8,3,48,128]{3,2,1,0:T(8,128)S(1)}, f32[8,3,48,128]{3,2,1,0:T(8,128)S(1)}) custom-call(f32[8]{0:T(128)S(1)} %copy-done.4, f32[8,3,48,128]{3,2,1,0:T(8,128)} %join.2.q_ref.refs_2_, f32[3,3,48,128]{3,2,1,0:T(8,128)S(1)} %copy-done.2, f32[3,3,48,128]{3,2,1,0:T(8,128)S(1)} %bitcast.16, f32[3,48,128]{2,1,0:T(8,128)S(1)} %copy-done.1), custom_call_target="tpu_custom_call" | custom-call | flops 1000000 | tf_op jit(solution)/shard_map/inner/pallas_call | solution.py:146
  87.5 3.0 %collective-permute-done.6.refs_0_ = f32[8,3,48,128]{3,2,1,0:T(8,128)S(1)} collective-permute-done((f32[8,3,48,128]{3,2,1,0:T(8,128)}, f32[8,3,48,128]{3,2,1,0:T(8,128)S(1)}, u32[]{:S(2)}, u32[]{:S(2)}) %collective-permute-start.6) | collective-permute-done | bytes 589856 | tf_op jit(solution)/shard_map/ppermute | solution.py:179
  90.5 5.2 %collective-permute-done.7.refs_1_ = f32[8,3,48,128]{3,2,1,0:T(8,128)} collective-permute-done((f32[8,3,48,128]{3,2,1,0:T(8,128)}, f32[8,3,48,128]{3,2,1,0:T(8,128)}, u32[]{:S(2)}, u32[]{:S(2)}) %collective-permute-start.7) | collective-permute-done | bytes 589856 | tf_op jit(solution)/shard_map/ppermute | solution.py:180
  95.7 2.5 %outer.3 = (f32[8,3,48,128]{3,2,1,0:T(8,128)S(1)}, f32[8,3,48,128]{3,2,1,0:T(8,128)S(1)}) custom-call(f32[8,3,48,128]{3,2,1,0:T(8,128)S(1)} %collective-permute-done.6.refs_0_, f32[8,3,48,128]{3,2,1,0:T(8,128)} %collective-permute-done.7.refs_1_, f32[8,3,48,128]{3,2,1,0:T(8,128)} %join.2.q_ref.refs_2_, ...), custom_call_target="tpu_custom_call", output_to_operand_aliasing={{0}: (3, {}), {1}: (4, {})} | custom-call | flops 10000000000 | tf_op jit(solution)/shard_map/outer/pallas_call | solution.py:164
  98.3 2.6 %all-to-all-done.3 = f32[16,9,8,128]{3,2,1,0:T(8,128)S(1)} async-done(((f32[16,9,8,128]{3,2,1,0:T(8,128)}), f32[16,9,8,128]{3,2,1,0:T(8,128)S(1)}, u32[]{:S(2)}, u32[]{:S(2)}) %all-to-all-start.3) | async-done | bytes 589856 | tf_op jit(solution)/shard_map/all_to_all | solution.py:153
  100.8 1.1 %join.3 = f32[8,3,48,128]{3,2,1,0:T(8,128)} custom-call(f32[8,3,48,128]{3,2,1,0:T(8,128)S(1)} %get-tuple-element.23.base_ref, f32[8,3,48,128]{3,2,1,0:T(8,128)S(1)} %get-tuple-element.24.noise_ref, f32[3,48,128]{2,1,0:T(8,128)S(1)} %copy-done.1, f32[8,3,48,128]{3,2,1,0:T(8,128)S(1)} %bitcast.13, f32[8,3,48,128]{3,2,1,0:T(8,128)S(1)} %bitcast.12), custom_call_target="tpu_custom_call" | custom-call | tf_op jit(solution)/shard_map/join/pallas_call | solution.py:174
  (3 shorter events, 0.1 us)
Async XLA Ops:
  0.0 4.4 %copy-start = (f32[1,8,3,48,128]{4,3,2,1,0:T(8,128)S(1)}, f32[1,8,3,48,128]{4,3,2,1,0:T(8,128)}, u32[]{:S(2)}) copy-start(f32[1,8,3,48,128]{4,3,2,1,0:T(8,128)} %param.5) | copy-start | bytes 1769476
  0.0 15.5 %all-to-all-start = ((f32[8,3,48,128]{3,2,1,0:T(8,128)}), f32[8,3,48,128]{3,2,1,0:T(8,128)S(1)}, u32[]{:S(2)}, u32[]{:S(2)}) async-start(f32[8,3,48,128]{3,2,1,0:T(8,128)} %bitcast.9), calls=%async_computation | async-start | bytes 1179648 | tf_op jit(solution)/shard_map/all_to_all | solution.py:155
  4.5 40.0 %collective-permute-start = (f32[6,3,48,128]{3,2,1,0:T(8,128)S(1)}, f32[6,3,48,128]{3,2,1,0:T(8,128)S(1)}, u32[]{:S(2)}, u32[]{:S(2)}) collective-permute-start(f32[6,3,48,128]{3,2,1,0:T(8,128)S(1)} %slice_bitcast_fusion), channel_id=1, source_target_pairs={{0,16},{16,32},{32,48},{48,64},{64,80},{80,96},{96,112},{112,128},... | collective-permute-start | bytes 1327112 | tf_op jit(solution)/shard_map/ppermute | solution.py:179
  9.3 35.2 %collective-permute-start.1 = (f32[6,3,48,128]{3,2,1,0:T(8,128)S(1)}, f32[6,3,48,128]{3,2,1,0:T(8,128)S(1)}, u32[]{:S(2)}, u32[]{:S(2)}) collective-permute-start(f32[6,3,48,128]{3,2,1,0:T(8,128)S(1)} %slice_bitcast_fusion), channel_id=1, source_target_pairs={{16,0},{32,16},{48,32},{64,48},{80,64},{96,80},{112,96},{128,112},... | collective-permute-start | bytes 1327112 | tf_op jit(solution)/shard_map/ppermute | solution.py:180
  16.2 21.1 %copy-start.3 = (f32[1,3,3,48,128]{4,3,2,1,0:T(8,128)S(1)}, f32[1,3,3,48,128]{4,3,2,1,0:T(8,128)}, u32[]{:S(2)}) copy-start(f32[1,3,3,48,128]{4,3,2,1,0:T(8,128)} %param.7) | copy-start | bytes 663556
  16.2 10.7 %all-to-all-start.1 = ((f32[4,3,48,128]{3,2,1,0:T(8,128)}), f32[4,3,48,128]{3,2,1,0:T(8,128)S(1)}, u32[]{:S(2)}, u32[]{:S(2)}) async-start(f32[4,3,48,128]{3,2,1,0:T(8,128)} %spread.2), calls=%async_computation.1 | async-start | bytes 589824 | tf_op jit(solution)/shard_map/all_to_all | solution.py:157
  19.8 17.5 %copy-start.1 = (f32[3,48,128]{2,1,0:T(8,128)S(1)}, f32[3,48,128]{2,1,0:T(8,128)}, u32[]{:S(2)}) copy-start(f32[3,48,128]{2,1,0:T(8,128)} %dif_ref.7) | copy-start | bytes 221188
  19.8 17.5 %copy-start.2 = (f32[3,3,48,128]{3,2,1,0:T(8,128)S(1)}, f32[3,3,48,128]{3,2,1,0:T(8,128)}, u32[]{:S(2)}) copy-start(f32[3,3,48,128]{3,2,1,0:T(8,128)} %refs_5_.1) | copy-start | bytes 663556
  19.9 17.5 %copy-start.4 = (f32[8]{0:T(128)S(1)}, f32[8]{0:T(128)}, u32[]{:S(2)}) copy-start(f32[8]{0:T(128)} %stoich_ref.3) | copy-start | bytes 100
  26.9 15.6 %collective-permute-start.4 = (f32[4,3,48,128]{3,2,1,0:T(8,128)S(1)}, f32[4,3,48,128]{3,2,1,0:T(8,128)S(1)}, u32[]{:S(2)}, u32[]{:S(2)}) collective-permute-start(f32[4,3,48,128]{3,2,1,0:T(8,128)S(1)} %all-to-all-done.1.a_ref), channel_id=1, source_target_pairs={{0,8},{1,9},{2,10},{3,11},{4,12},{5,13},{6,14},{7,15},{8,0},{9,1},... | collective-permute-start | bytes 884744 | tf_op jit(solution)/shard_map/ppermute | solution.py:138
  29.5 15.0 %collective-permute-start.2 = (f32[2,3,48,128]{3,2,1,0:T(8,128)S(1)}, f32[2,3,48,128]{3,2,1,0:T(8,128)S(1)}, u32[]{:S(2)}, u32[]{:S(2)}) collective-permute-start(f32[2,3,48,128]{3,2,1,0:T(8,128)S(1)} %slice_bitcast_fusion.1), channel_id=1, source_target_pairs={{0,16},{16,32},{32,48},{48,64},{64,80},{80,96},{96,112},{112,128},... | collective-permute-start | bytes 442376 | tf_op jit(solution)/shard_map/ppermute | solution.py:179
  35.4 11.4 %collective-permute-start.3 = (f32[2,3,48,128]{3,2,1,0:T(8,128)S(1)}, f32[2,3,48,128]{3,2,1,0:T(8,128)S(1)}, u32[]{:S(2)}, u32[]{:S(2)}) collective-permute-start(f32[2,3,48,128]{3,2,1,0:T(8,128)S(1)} %slice_bitcast_fusion.1), channel_id=1, source_target_pairs={{16,0},{32,16},{48,32},{64,48},{80,64},{96,80},{112,96},{128,112},... | collective-permute-start | bytes 442376 | tf_op jit(solution)/shard_map/ppermute | solution.py:180
  42.6 5.5 %collective-permute-start.5 = (f32[4,3,48,128]{3,2,1,0:T(8,128)S(1)}, f32[4,3,48,128]{3,2,1,0:T(8,128)S(1)}, u32[]{:S(2)}, u32[]{:S(2)}) collective-permute-start(f32[4,3,48,128]{3,2,1,0:T(8,128)S(1)} %add.1.rest_0_), channel_id=1, source_target_pairs={{0,1},{1,0},{2,3},{3,2},{4,5},{5,4},{6,7},{7,6},{8,9},{9,8},{10,11... | collective-permute-start | bytes 884744 | tf_op jit(solution)/shard_map/ppermute | solution.py:138
  49.1 27.6 %all-to-all-start.2 = ((f32[16,9,8,128]{3,2,1,0:T(8,128)}), f32[16,9,8,128]{3,2,1,0:T(8,128)S(1)}, u32[]{:S(2)}, u32[]{:S(2)}) async-start(f32[16,9,8,128]{3,2,1,0:T(8,128)} %bitcast.4), calls=%async_computation.2 | async-start | bytes 1179648 | tf_op jit(solution)/shard_map/all_to_all | solution.py:151
  57.6 32.9 %collective-permute-start.6 = (f32[8,3,48,128]{3,2,1,0:T(8,128)}, f32[8,3,48,128]{3,2,1,0:T(8,128)S(1)}, u32[]{:S(2)}, u32[]{:S(2)}) collective-permute-start(f32[8,3,48,128]{3,2,1,0:T(8,128)} %join.2.q_ref.refs_2_), channel_id=1, source_target_pairs={{0,16},{16,32},{32,48},{48,64},{64,80},{80,96},{96,112},{112,128},... | collective-permute-start | bytes 1769480 | tf_op jit(solution)/shard_map/ppermute | solution.py:179
  61.2 34.5 %collective-permute-start.7 = (f32[8,3,48,128]{3,2,1,0:T(8,128)}, f32[8,3,48,128]{3,2,1,0:T(8,128)}, u32[]{:S(2)}, u32[]{:S(2)}) collective-permute-start(f32[8,3,48,128]{3,2,1,0:T(8,128)} %join.2.q_ref.refs_2_), channel_id=1, source_target_pairs={{16,0},{32,16},{48,32},{64,48},{80,64},{96,80},{112,96},{128,112},... | collective-permute-start | bytes 1769480 | tf_op jit(solution)/shard_map/ppermute | solution.py:180
  77.6 23.2 %all-to-all-start.3 = ((f32[16,9,8,128]{3,2,1,0:T(8,128)}), f32[16,9,8,128]{3,2,1,0:T(8,128)S(1)}, u32[]{:S(2)}, u32[]{:S(2)}) async-start(f32[16,9,8,128]{3,2,1,0:T(8,128)} %spread.3), calls=%async_computation.3 | async-start | bytes 1179648 | tf_op jit(solution)/shard_map/all_to_all | solution.py:153

commit v6 on v4

--- a/solution.py
+++ b/solution.py
@@ -15,9 +15,6 @@
 HBM = pl.BlockSpec(memory_space=pltpu.HBM)
 SMEM = pl.BlockSpec(memory_space=pltpu.SMEM)
 VMEM = pl.BlockSpec(memory_space=pltpu.VMEM)
-
-
-FIELD_ROWS = [[(y * 4 + x) * 2 + c for x in range(4) for c in range(2)] for y in range(2)]
 
 
 def call(kernel, out_shape, in_specs, scratch, flops, name, aliases={}):
@@ -64,10 +61,12 @@
     lax.fori_loop(0, scalars, one, 0)
 
 
-def outer_kernel(low_hbm, high_hbm, q_ref, base_ref, noise_ref, vel_ref, wie_ref, dif_ref, base_out, noise_out, low_ref, high_ref, sems):
+def outer_kernel(first_hbm, second_hbm, q_ref, base_ref, noise_ref, vel_ref, wie_ref, dif_ref, base_out, noise_out, halo_ref, sems):
     scalars, planes = q_ref.shape[:2]
     cuts = [pl.ds(0, scalars // 2), pl.ds(scalars // 2, scalars // 2)]
-    pairs = ((low_hbm, low_ref), (high_hbm, high_ref))
+    odd = lax.axis_index("space") % 2
+    low_ref, high_ref = halo_ref.at[0], halo_ref.at[1]
+    pairs = ((first_hbm, halo_ref.at[1 - odd]), (second_hbm, halo_ref.at[odd]))
     copies = [
         [pltpu.make_async_copy(a.at[cut], b.at[cut], sems.at[m, n]) for n, (a, b) in enumerate(pairs)]
         for m, cut in enumerate(cuts)
@@ -97,22 +96,16 @@
         lax.fori_loop(m * (scalars // 2), (m + 1) * (scalars // 2), one, 0)
 
 
-def join_kernel(fields, last, base_ref, noise_ref, dif_ref, own_ref, other_ref, *rest):
+def join_kernel(fields, last, base_ref, noise_ref, dif_ref, total_ref, *rest):
     out_ref = rest[-1]
     scalars, planes = base_ref.shape[:2]
-    half = scalars // 2
-    row = lax.axis_index("field") // 8
-
-    def total(s, i):
-        return jnp.where(row == s // half, own_ref[s % half, i], other_ref[s % half, i])
-
     for i in range(planes):
         dif = dif_ref[i]
-        theta_bar = 1.0 + 3.0 * sigmoid(total(scalars - 1, i) * (1.0 / fields))
+        theta_bar = 1.0 + 3.0 * sigmoid(total_ref[scalars - 1, i] * (1.0 / fields))
         amplitude = jnp.sqrt(2.0 * dif * theta_bar)
         pull = (time_step * mix_const / fields) * dif
         for s in range(scalars):
-            new = base_ref[s, i] + (amplitude * noise_ref[s, i] + pull * total(s, i))
+            new = base_ref[s, i] + (amplitude * noise_ref[s, i] + pull * total_ref[s, i])
             out_ref[s, i] = 0.5 * rest[0][s, i] + 0.5 * new if last else new
 
 
@@ -127,29 +120,27 @@
 def section(fields, stoich, q, velocity, wiener, diffusivity, phi=None):
     last = phi is not None
     like = jax.ShapeDtypeStruct(q.shape, q.dtype)
-    low, high = neighbours(q)
+    halo = neighbours(q)
     base, noise = call(
         inner_kernel, (like, like), [SMEM] + [VMEM] * 4, [pltpu.VMEM(q.shape[1:], jnp.float32)], 10**6, "inner"
     )(stoich, q, velocity, wiener, diffusivity)
     mark = q
     shares = mark.reshape(lax.axis_size("field"), -1, 8, q.shape[-1])
     received = lax.all_to_all(shares, "field", 0, 0)
-    spread = call(spread_kernel, jax.ShapeDtypeStruct((8,) + shares.shape[1:], q.dtype), [VMEM], [], 0, "spread")(received)
-    own = lax.all_to_all(spread, "field", 0, 0, axis_index_groups=FIELD_ROWS).reshape((-1,) + q.shape[1:])
-    other = lax.ppermute(own, "field", [(i, i ^ 8) for i in range(16)])
-    scratch = [pltpu.VMEM(q.shape, jnp.float32)] * 2 + [pltpu.SemaphoreType.DMA((2, 2))]
+    spread = call(spread_kernel, jax.ShapeDtypeStruct(shares.shape, q.dtype), [VMEM], [], 0, "spread")(received)
+    total = lax.all_to_all(spread, "field", 0, 0).reshape(q.shape)
+    scratch = [pltpu.VMEM((2,) + q.shape, jnp.float32)] + [pltpu.SemaphoreType.DMA((2, 2))]
     base, noise = call(outer_kernel, (like, like), [HBM] * 2 + [VMEM] * 6, scratch, 10**10, "outer", {3: 0, 4: 1})(
-        low, high, q, base, noise, velocity, wiener, diffusivity
+        *halo, q, base, noise, velocity, wiener, diffusivity
     )
-    args = (base, noise, diffusivity, own, other) + ((phi,) if last else ())
+    args = (base, noise, diffusivity, total) + ((phi,) if last else ())
     return call(functools.partial(join_kernel, fields, last), like, [VMEM] * len(args), [], 0, "join")(*args)
 
 
 def neighbours(q):
     count = lax.axis_size("space")
-    low = lax.ppermute(q, "space", [(i, i + 1) for i in range(count - 1)])
-    high = lax.ppermute(q, "space", [(i + 1, i) for i in range(count - 1)])
-    return low, high
+    swaps = [[(i, i + 1) for i in range(begin, count - 1, 2)] for begin in range(2)]
+    return tuple(lax.ppermute(q, "space", pairs + [(b, a) for a, b in pairs]) for pairs in swaps)
 
 
 def local(phi, velocity, wiener, diffusivity, stoich):

time: 107 us -> 99.5 us (0.930)
  waiting for transfers between devices: 63.7 us -> 50 us
  starting transfers between devices: 29.5 us -> 35.3 us
    all_to_all x2, waiting for transfers between devices: 41.2 us -> 18.8 us  [section(): received = lax.all_to_all(shares, 'field', 0, 0)]
    all_to_all x2, starting transfers between devices: 6.98 us -> 15 us  [section(): total = lax.all_to_all(spread, 'field', 0, 0).reshape(q.shape)]
    ppermute x6 -> x4, waiting for transfers between devices: 12.6 us -> 17 us  [neighbours(): lax.ppermute(q, 'space', pairs + [(b, a) for a, b in pairs])]
    all_to_all x2, waiting for transfers between devices: 9.98 us -> 14.1 us  [section(): total = lax.all_to_all(spread, 'field', 0, 0).reshape(q.shape)]
    ppermute x6 -> x4, starting transfers between devices: 9.19 us -> 7.21 us  [neighbours(): lax.ppermute(q, 'space', pairs + [(b, a) for a, b in pairs])]
  transfers between devices with their start and end apart: 10 -> 8, of which waited for: 6 -> 6; matrix products, arithmetic and copies ran while one was open for 0% -> 0% of each run, Pallas kernels for 10% -> 11%
where the time goes in v6:
time: 99.5 us; the launch traced here: 98.7 us
  waiting for transfers between devices  50 us (50%)
  starting transfers between devices  35.3 us (35%)
  Pallas kernels  12.7 us (13%)
    all_to_all x2, waiting for transfers between devices, section(): received = lax.all_to_all(shares, 'field', 0, 0)  18.8 us
    ppermute x4, waiting for transfers between devices, neighbours(): lax.ppermute(q, 'space', pairs + [(b, a) for a, b in pairs])  17 us
    all_to_all x2, starting transfers between devices, section(): total = lax.all_to_all(spread, 'field', 0, 0).reshape(q.shape)  15 us
    all_to_all x2, waiting for transfers between devices, section(): total = lax.all_to_all(spread, 'field', 0, 0).reshape(q.shape)  14.1 us
    all_to_all x2, starting transfers between devices, section(): received = lax.all_to_all(shares, 'field', 0, 0)  13.1 us
    ppermute x4, starting transfers between devices, neighbours(): lax.ppermute(q, 'space', pairs + [(b, a) for a, b in pairs])  7.21 us
    pallas_call x2, Pallas kernels, section(): call(inner_kernel, (like, like), [SMEM] + [VMEM] * 4, [pltpu.VMEM(q.shape...  4.96 us
    pallas_call x2, Pallas kernels, section(): call(outer_kernel, (like, like), [HBM] * 2 + [VMEM] * 6, scratch, 10 ** 1...  3.99 us
  transfers between devices with their start and end apart: 8, of which 6 were waited for; matrix products, arithmetic and copies ran while one was open for 0% of the time, Pallas kernels for 11%

profile of v6, /device:TPU:8, one launch (start us, length us, event | category | flops | bytes accessed | tf_op | source)
XLA Modules:
  0.0 98.7 jit_solution(7777061441940068353)
XLA Ops:
  0.0 0.0 copy-start
  0.0 9.4 %all-to-all-start = ((f32[16,9,8,128]{3,2,1,0:T(8,128)}), f32[16,9,8,128]{3,2,1,0:T(8,128)S(1)}, u32[]{:S(2)}, u32[]{:S(2)}) async-start(f32[16,9,8,128]{3,2,1,0:T(8,128)} %bitcast.7), calls=%async_computation | async-start | bytes 1179648 | tf_op jit(solution)/shard_map/all_to_all | solution.py:129
  9.4 0.0 copy-done
  9.4 1.9 %collective-permute-start = (f32[8,3,48,128]{3,2,1,0:T(8,128)S(1)}, f32[8,3,48,128]{3,2,1,0:T(8,128)S(1)}, u32[]{:S(2)}, u32[]{:S(2)}) collective-permute-start(f32[8,3,48,128]{3,2,1,0:T(8,128)S(1)} %bitcast.8), channel_id=1, source_target_pairs={{0,16},{32,48},{64,80},{96,112},{128,144},{160,176},{192,208},{224... | collective-permute-start | bytes 1769480 | tf_op jit(solution)/shard_map/ppermute | solution.py:143
  11.3 1.5 %collective-permute-start.1 = (f32[8,3,48,128]{3,2,1,0:T(8,128)S(1)}, f32[8,3,48,128]{3,2,1,0:T(8,128)}, u32[]{:S(2)}, u32[]{:S(2)}) collective-permute-start(f32[8,3,48,128]{3,2,1,0:T(8,128)S(1)} %bitcast.9), channel_id=1, source_target_pairs={{16,32},{48,64},{80,96},{112,128},{144,160},{176,192},{208,224},{2... | collective-permute-start | bytes 1769480 | tf_op jit(solution)/shard_map/ppermute | solution.py:143
  12.8 9.2 %all-to-all-done.parts_ref = f32[16,9,8,128]{3,2,1,0:T(8,128)S(1)} async-done(((f32[16,9,8,128]{3,2,1,0:T(8,128)}), f32[16,9,8,128]{3,2,1,0:T(8,128)S(1)}, u32[]{:S(2)}, u32[]{:S(2)}) %all-to-all-start) | async-done | bytes 589856 | tf_op jit(solution)/shard_map/all_to_all | solution.py:129
  22.0 0.9 spread.2
  22.9 0.0 copy-start.1
  22.9 0.0 copy-start.2
  22.9 0.0 copy-start.3
  22.9 7.4 %all-to-all-start.1 = ((f32[16,9,8,128]{3,2,1,0:T(8,128)}), f32[16,9,8,128]{3,2,1,0:T(8,128)S(1)}, u32[]{:S(2)}, u32[]{:S(2)}) async-start(f32[16,9,8,128]{3,2,1,0:T(8,128)} %spread.2), calls=%async_computation.1 | async-start | bytes 1179648 | tf_op jit(solution)/shard_map/all_to_all | solution.py:131
  30.3 0.0 copy-start.4
  30.3 0.0 copy-done.1
  30.3 0.0 copy-done.2
  30.3 0.0 copy-done.3
  30.4 0.6 copy-done.4
  31.0 2.2 %inner.2 = (f32[8,3,48,128]{3,2,1,0:T(8,128)S(1)}, f32[8,3,48,128]{3,2,1,0:T(8,128)S(1)}) custom-call(f32[8]{0:T(128)S(1)} %copy-done.4, f32[8,3,48,128]{3,2,1,0:T(8,128)S(1)} %bitcast.10, f32[3,3,48,128]{3,2,1,0:T(8,128)S(1)} %copy-done.2, f32[3,3,48,128]{3,2,1,0:T(8,128)S(1)} %bitcast.15, f32[3,48,128]{2,1,0:T(8,128)S(1)} %copy-done.1), custom_call_target="tpu_custom_call" | custom-call | flops 1000000 | tf_op jit(solution)/shard_map/inner/pallas_call | solution.py:124
  33.2 8.0 %collective-permute-done.first_hbm = f32[8,3,48,128]{3,2,1,0:T(8,128)S(1)} collective-permute-done((f32[8,3,48,128]{3,2,1,0:T(8,128)S(1)}, f32[8,3,48,128]{3,2,1,0:T(8,128)S(1)}, u32[]{:S(2)}, u32[]{:S(2)}) %collective-permute-start) | collective-permute-done | bytes 589856 | tf_op jit(solution)/shard_map/ppermute | solution.py:143
  41.2 0.0 collective-permute-done.1.second_hbm
  41.2 1.5 %outer.2 = (f32[8,3,48,128]{3,2,1,0:T(8,128)S(1)}, f32[8,3,48,128]{3,2,1,0:T(8,128)S(1)}) custom-call(f32[8,3,48,128]{3,2,1,0:T(8,128)S(1)} %collective-permute-done.first_hbm, f32[8,3,48,128]{3,2,1,0:T(8,128)} %collective-permute-done.1.second_hbm, f32[8,3,48,128]{3,2,1,0:T(8,128)S(1)} %bitcast.11, ...), custom_call_target="tpu_custom_call", output_to_operand_aliasing={{0}: (3, {}), {1}: (4, {})} | custom-call | flops 10000000000 | tf_op jit(solution)/shard_map/outer/pallas_call | solution.py:133
  42.7 8.5 %all-to-all-done.1 = f32[16,9,8,128]{3,2,1,0:T(8,128)S(1)} async-done(((f32[16,9,8,128]{3,2,1,0:T(8,128)}), f32[16,9,8,128]{3,2,1,0:T(8,128)S(1)}, u32[]{:S(2)}, u32[]{:S(2)}) %all-to-all-start.1) | async-done | bytes 589856 | tf_op jit(solution)/shard_map/all_to_all | solution.py:131
  51.2 1.0 join.2.q_ref
  52.1 3.7 %all-to-all-start.2 = ((f32[16,9,8,128]{3,2,1,0:T(8,128)}), f32[16,9,8,128]{3,2,1,0:T(8,128)S(1)}, u32[]{:S(2)}, u32[]{:S(2)}) async-start(f32[16,9,8,128]{3,2,1,0:T(8,128)} %bitcast.4), calls=%async_computation.2 | async-start | bytes 1179648 | tf_op jit(solution)/shard_map/all_to_all | solution.py:129
  55.8 2.3 %collective-permute-start.2 = (f32[8,3,48,128]{3,2,1,0:T(8,128)}, f32[8,3,48,128]{3,2,1,0:T(8,128)S(1)}, u32[]{:S(2)}, u32[]{:S(2)}) collective-permute-start(f32[8,3,48,128]{3,2,1,0:T(8,128)} %join.2.q_ref), channel_id=1, source_target_pairs={{0,16},{32,48},{64,80},{96,112},{128,144},{160,176},{192,208},{224... | collective-permute-start | bytes 1769480 | tf_op jit(solution)/shard_map/ppermute | solution.py:143
  58.1 1.5 %collective-permute-start.3 = (f32[8,3,48,128]{3,2,1,0:T(8,128)}, f32[8,3,48,128]{3,2,1,0:T(8,128)}, u32[]{:S(2)}, u32[]{:S(2)}) collective-permute-start(f32[8,3,48,128]{3,2,1,0:T(8,128)} %join.2.q_ref), channel_id=1, source_target_pairs={{16,32},{48,64},{80,96},{112,128},{144,160},{176,192},{208,224},{2... | collective-permute-start | bytes 1769480 | tf_op jit(solution)/shard_map/ppermute | solution.py:143
  59.6 9.6 %all-to-all-done.2.parts_ref = f32[16,9,8,128]{3,2,1,0:T(8,128)S(1)} async-done(((f32[16,9,8,128]{3,2,1,0:T(8,128)}), f32[16,9,8,128]{3,2,1,0:T(8,128)S(1)}, u32[]{:S(2)}, u32[]{:S(2)}) %all-to-all-start.2) | async-done | bytes 589856 | tf_op jit(solution)/shard_map/all_to_all | solution.py:129
  69.3 0.9 spread.3
  70.2 7.6 %all-to-all-start.3 = ((f32[16,9,8,128]{3,2,1,0:T(8,128)}), f32[16,9,8,128]{3,2,1,0:T(8,128)S(1)}, u32[]{:S(2)}, u32[]{:S(2)}) async-start(f32[16,9,8,128]{3,2,1,0:T(8,128)} %spread.3), calls=%async_computation.3 | async-start | bytes 1179648 | tf_op jit(solution)/shard_map/all_to_all | solution.py:131
  77.8 2.7 %inner.3 = (f32[8,3,48,128]{3,2,1,0:T(8,128)S(1)}, f32[8,3,48,128]{3,2,1,0:T(8,128)S(1)}) custom-call(f32[8]{0:T(128)S(1)} %copy-done.4, f32[8,3,48,128]{3,2,1,0:T(8,128)} %join.2.q_ref, f32[3,3,48,128]{3,2,1,0:T(8,128)S(1)} %copy-done.2, f32[3,3,48,128]{3,2,1,0:T(8,128)S(1)} %bitcast.17, f32[3,48,128]{2,1,0:T(8,128)S(1)} %copy-done.1), custom_call_target="tpu_custom_call" | custom-call | flops 1000000 | tf_op jit(solution)/shard_map/inner/pallas_call | solution.py:124
  80.5 9.0 %collective-permute-done.2.first_hbm = f32[8,3,48,128]{3,2,1,0:T(8,128)S(1)} collective-permute-done((f32[8,3,48,128]{3,2,1,0:T(8,128)}, f32[8,3,48,128]{3,2,1,0:T(8,128)S(1)}, u32[]{:S(2)}, u32[]{:S(2)}) %collective-permute-start.2) | collective-permute-done | bytes 589856 | tf_op jit(solution)/shard_map/ppermute | solution.py:143
  89.6 0.0 collective-permute-done.3.second_hbm
  89.6 2.5 %outer.3 = (f32[8,3,48,128]{3,2,1,0:T(8,128)S(1)}, f32[8,3,48,128]{3,2,1,0:T(8,128)S(1)}) custom-call(f32[8,3,48,128]{3,2,1,0:T(8,128)S(1)} %collective-permute-done.2.first_hbm, f32[8,3,48,128]{3,2,1,0:T(8,128)} %collective-permute-done.3.second_hbm, f32[8,3,48,128]{3,2,1,0:T(8,128)} %join.2.q_ref, ...), custom_call_target="tpu_custom_call", output_to_operand_aliasing={{0}: (3, {}), {1}: (4, {})} | custom-call | flops 10000000000 | tf_op jit(solution)/shard_map/outer/pallas_call | solution.py:133
  92.1 5.6 %all-to-all-done.3 = f32[16,9,8,128]{3,2,1,0:T(8,128)S(1)} async-done(((f32[16,9,8,128]{3,2,1,0:T(8,128)}), f32[16,9,8,128]{3,2,1,0:T(8,128)S(1)}, u32[]{:S(2)}, u32[]{:S(2)}) %all-to-all-start.3) | async-done | bytes 589856 | tf_op jit(solution)/shard_map/all_to_all | solution.py:131
  97.7 1.1 %join.3 = f32[8,3,48,128]{3,2,1,0:T(8,128)} custom-call(f32[8,3,48,128]{3,2,1,0:T(8,128)S(1)} %get-tuple-element.19.base_ref, f32[8,3,48,128]{3,2,1,0:T(8,128)S(1)} %get-tuple-element.20.noise_ref, f32[3,48,128]{2,1,0:T(8,128)S(1)} %copy-done.1, f32[8,3,48,128]{3,2,1,0:T(8,128)S(1)} %bitcast.13, f32[8,3,48,128]{3,2,1,0:T(8,128)S(1)} %bitcast.12), custom_call_target="tpu_custom_call" | custom-call | tf_op jit(solution)/shard_map/join/pallas_call | solution.py:137
Async XLA Ops:
  0.0 9.4 %copy-start = (f32[1,8,3,48,128]{4,3,2,1,0:T(8,128)S(1)}, f32[1,8,3,48,128]{4,3,2,1,0:T(8,128)}, u32[]{:S(2)}) copy-start(f32[1,8,3,48,128]{4,3,2,1,0:T(8,128)} %param.5) | copy-start | bytes 1769476
  0.0 22.0 %all-to-all-start = ((f32[16,9,8,128]{3,2,1,0:T(8,128)}), f32[16,9,8,128]{3,2,1,0:T(8,128)S(1)}, u32[]{:S(2)}, u32[]{:S(2)}) async-start(f32[16,9,8,128]{3,2,1,0:T(8,128)} %bitcast.7), calls=%async_computation | async-start | bytes 1179648 | tf_op jit(solution)/shard_map/all_to_all | solution.py:129
  9.4 31.8 %collective-permute-start = (f32[8,3,48,128]{3,2,1,0:T(8,128)S(1)}, f32[8,3,48,128]{3,2,1,0:T(8,128)S(1)}, u32[]{:S(2)}, u32[]{:S(2)}) collective-permute-start(f32[8,3,48,128]{3,2,1,0:T(8,128)S(1)} %bitcast.8), channel_id=1, source_target_pairs={{0,16},{32,48},{64,80},{96,112},{128,144},{160,176},{192,208},{224... | collective-permute-start | bytes 1769480 | tf_op jit(solution)/shard_map/ppermute | solution.py:143
  11.3 29.9 %collective-permute-start.1 = (f32[8,3,48,128]{3,2,1,0:T(8,128)S(1)}, f32[8,3,48,128]{3,2,1,0:T(8,128)}, u32[]{:S(2)}, u32[]{:S(2)}) collective-permute-start(f32[8,3,48,128]{3,2,1,0:T(8,128)S(1)} %bitcast.9), channel_id=1, source_target_pairs={{16,32},{48,64},{80,96},{112,128},{144,160},{176,192},{208,224},{2... | collective-permute-start | bytes 1769480 | tf_op jit(solution)/shard_map/ppermute | solution.py:143
  22.9 7.4 %copy-start.1 = (f32[3,48,128]{2,1,0:T(8,128)S(1)}, f32[3,48,128]{2,1,0:T(8,128)}, u32[]{:S(2)}) copy-start(f32[3,48,128]{2,1,0:T(8,128)} %dif_ref.11) | copy-start | bytes 221188
  22.9 7.4 %copy-start.2 = (f32[3,3,48,128]{3,2,1,0:T(8,128)S(1)}, f32[3,3,48,128]{3,2,1,0:T(8,128)}, u32[]{:S(2)}) copy-start(f32[3,3,48,128]{3,2,1,0:T(8,128)} %vel_ref.7) | copy-start | bytes 663556
  22.9 7.4 %copy-start.3 = (f32[1,3,3,48,128]{4,3,2,1,0:T(8,128)S(1)}, f32[1,3,3,48,128]{4,3,2,1,0:T(8,128)}, u32[]{:S(2)}) copy-start(f32[1,3,3,48,128]{4,3,2,1,0:T(8,128)} %param.7) | copy-start | bytes 663556
  22.9 28.2 %all-to-all-start.1 = ((f32[16,9,8,128]{3,2,1,0:T(8,128)}), f32[16,9,8,128]{3,2,1,0:T(8,128)S(1)}, u32[]{:S(2)}, u32[]{:S(2)}) async-start(f32[16,9,8,128]{3,2,1,0:T(8,128)} %spread.2), calls=%async_computation.1 | async-start | bytes 1179648 | tf_op jit(solution)/shard_map/all_to_all | solution.py:131
  30.3 0.7 copy-start.4
  52.1 17.1 %all-to-all-start.2 = ((f32[16,9,8,128]{3,2,1,0:T(8,128)}), f32[16,9,8,128]{3,2,1,0:T(8,128)S(1)}, u32[]{:S(2)}, u32[]{:S(2)}) async-start(f32[16,9,8,128]{3,2,1,0:T(8,128)} %bitcast.4), calls=%async_computation.2 | async-start | bytes 1179648 | tf_op jit(solution)/shard_map/all_to_all | solution.py:129
  55.8 33.7 %collective-permute-start.2 = (f32[8,3,48,128]{3,2,1,0:T(8,128)}, f32[8,3,48,128]{3,2,1,0:T(8,128)S(1)}, u32[]{:S(2)}, u32[]{:S(2)}) collective-permute-start(f32[8,3,48,128]{3,2,1,0:T(8,128)} %join.2.q_ref), channel_id=1, source_target_pairs={{0,16},{32,48},{64,80},{96,112},{128,144},{160,176},{192,208},{224... | collective-permute-start | bytes 1769480 | tf_op jit(solution)/shard_map/ppermute | solution.py:143
  58.1 31.4 %collective-permute-start.3 = (f32[8,3,48,128]{3,2,1,0:T(8,128)}, f32[8,3,48,128]{3,2,1,0:T(8,128)}, u32[]{:S(2)}, u32[]{:S(2)}) collective-permute-start(f32[8,3,48,128]{3,2,1,0:T(8,128)} %join.2.q_ref), channel_id=1, source_target_pairs={{16,32},{48,64},{80,96},{112,128},{144,160},{176,192},{208,224},{2... | collective-permute-start | bytes 1769480 | tf_op jit(solution)/shard_map/ppermute | solution.py:143
  70.2 27.5 %all-to-all-start.3 = ((f32[16,9,8,128]{3,2,1,0:T(8,128)}), f32[16,9,8,128]{3,2,1,0:T(8,128)S(1)}, u32[]{:S(2)}, u32[]{:S(2)}) async-start(f32[16,9,8,128]{3,2,1,0:T(8,128)} %spread.3), calls=%async_computation.3 | async-start | bytes 1179648 | tf_op jit(solution)/shard_map/all_to_all | solution.py:131

commit v7 on v6

--- a/solution.py
+++ b/solution.py
@@ -64,7 +64,7 @@
 def outer_kernel(first_hbm, second_hbm, q_ref, base_ref, noise_ref, vel_ref, wie_ref, dif_ref, base_out, noise_out, halo_ref, sems):
     scalars, planes = q_ref.shape[:2]
     cuts = [pl.ds(0, scalars // 2), pl.ds(scalars // 2, scalars // 2)]
-    odd = lax.axis_index("space") % 2
+    odd = (lax.axis_index("space") + lax.axis_index("field")) % 2
     low_ref, high_ref = halo_ref.at[0], halo_ref.at[1]
     pairs = ((first_hbm, halo_ref.at[1 - odd]), (second_hbm, halo_ref.at[odd]))
     copies = [
@@ -138,9 +138,14 @@
 
 
 def neighbours(q):
-    count = lax.axis_size("space")
-    swaps = [[(i, i + 1) for i in range(begin, count - 1, 2)] for begin in range(2)]
-    return tuple(lax.ppermute(q, "space", pairs + [(b, a) for a, b in pairs]) for pairs in swaps)
+    count, fields = lax.axis_size("space"), lax.axis_size("field")
+
+    def swap(n):
+        ones = [(i, f) for f in range(fields) for i in range((n + f) % 2, count - 1, 2)]
+        pairs = [(i * fields + f, (i + 1) * fields + f) for i, f in ones]
+        return lax.ppermute(q, ("space", "field"), pairs + [(b, a) for a, b in pairs])
+
+    return swap(0), swap(1)
 
 
 def local(phi, velocity, wiener, diffusivity, stoich):

time: 99.5 us -> 99.4 us (level)
  starting transfers between devices: 35.3 us -> 27.7 us
  waiting for transfers between devices: 50 us -> 57.5 us
    all_to_all x2, waiting for transfers between devices: 18.8 us -> 39.4 us  [section(): received = lax.all_to_all(shares, 'field', 0, 0)]
    ppermute x4, waiting for transfers between devices: 17 us -> 4.77 us  [swap(): lax.ppermute(q, ('space', 'field'), pairs + [(b, a) for a, b in pairs])]
    all_to_all x2, starting transfers between devices: 15 us -> 7.39 us  [section(): total = lax.all_to_all(spread, 'field', 0, 0).reshape(q.shape)]
where the time goes in v7:
time: 99.4 us; the launch traced here: 98.7 us
  waiting for transfers between devices  57.5 us (58%)
  starting transfers between devices  27.7 us (28%)
  Pallas kernels  12.7 us (13%)
    all_to_all x2, waiting for transfers between devices, section(): received = lax.all_to_all(shares, 'field', 0, 0)  39.4 us
    all_to_all x2, waiting for transfers between devices, section(): total = lax.all_to_all(spread, 'field', 0, 0).reshape(q.shape)  13.4 us
    all_to_all x2, starting transfers between devices, section(): received = lax.all_to_all(shares, 'field', 0, 0)  13.1 us
    all_to_all x2, starting transfers between devices, section(): total = lax.all_to_all(spread, 'field', 0, 0).reshape(q.shape)  7.39 us
    ppermute x4, starting transfers between devices, swap(): lax.ppermute(q, ('space', 'field'), pairs + [(b, a) for a, b in pairs])  7.21 us
    pallas_call x2, Pallas kernels, section(): call(inner_kernel, (like, like), [SMEM] + [VMEM] * 4, [pltpu.VMEM(q.shape...  4.96 us
    ppermute x4, waiting for transfers between devices, swap(): lax.ppermute(q, ('space', 'field'), pairs + [(b, a) for a, b in pairs])  4.77 us
    pallas_call x2, Pallas kernels, section(): call(outer_kernel, (like, like), [HBM] * 2 + [VMEM] * 6, scratch, 10 ** 1...  3.99 us
  transfers between devices with their start and end apart: 8, of which 6 were waited for; matrix products, arithmetic and copies ran while one was open for 0% of the time, Pallas kernels for 11%

profile of v7, /device:TPU:8, one launch (start us, length us, event | category | flops | bytes accessed | tf_op | source)
XLA Modules:
  0.0 98.7 jit_solution(14332035028378650704)
XLA Ops:
  0.0 0.0 copy-start
  0.0 9.4 %all-to-all-start = ((f32[16,9,8,128]{3,2,1,0:T(8,128)}), f32[16,9,8,128]{3,2,1,0:T(8,128)S(1)}, u32[]{:S(2)}, u32[]{:S(2)}) async-start(f32[16,9,8,128]{3,2,1,0:T(8,128)} %bitcast.7), calls=%async_computation | async-start | bytes 1179648 | tf_op jit(solution)/shard_map/all_to_all | solution.py:129
  9.4 0.0 copy-done
  9.4 1.9 %collective-permute-start = (f32[8,3,48,128]{3,2,1,0:T(8,128)S(1)}, f32[8,3,48,128]{3,2,1,0:T(8,128)S(1)}, u32[]{:S(2)}, u32[]{:S(2)}) collective-permute-start(f32[8,3,48,128]{3,2,1,0:T(8,128)S(1)} %bitcast.8), channel_id=1, source_target_pairs={{0,16},{32,48},{64,80},{96,112},{128,144},{160,176},{192,208},{224... | collective-permute-start | bytes 1769480 | tf_op jit(solution)/shard_map/ppermute | solution.py:146
  11.3 1.5 %collective-permute-start.1 = (f32[8,3,48,128]{3,2,1,0:T(8,128)S(1)}, f32[8,3,48,128]{3,2,1,0:T(8,128)}, u32[]{:S(2)}, u32[]{:S(2)}) collective-permute-start(f32[8,3,48,128]{3,2,1,0:T(8,128)S(1)} %bitcast.9), channel_id=1, source_target_pairs={{16,32},{48,64},{80,96},{112,128},{144,160},{176,192},{208,224},{2... | collective-permute-start | bytes 1769480 | tf_op jit(solution)/shard_map/ppermute | solution.py:146
  12.8 19.9 %all-to-all-done.parts_ref = f32[16,9,8,128]{3,2,1,0:T(8,128)S(1)} async-done(((f32[16,9,8,128]{3,2,1,0:T(8,128)}), f32[16,9,8,128]{3,2,1,0:T(8,128)S(1)}, u32[]{:S(2)}, u32[]{:S(2)}) %all-to-all-start) | async-done | bytes 589856 | tf_op jit(solution)/shard_map/all_to_all | solution.py:129
  32.7 0.9 spread.2
  33.5 0.0 copy-start.1
  33.5 0.0 copy-start.2
  33.5 0.0 copy-start.3
  33.5 3.7 %all-to-all-start.1 = ((f32[16,9,8,128]{3,2,1,0:T(8,128)}), f32[16,9,8,128]{3,2,1,0:T(8,128)S(1)}, u32[]{:S(2)}, u32[]{:S(2)}) async-start(f32[16,9,8,128]{3,2,1,0:T(8,128)} %spread.2), calls=%async_computation.1 | async-start | bytes 1179648 | tf_op jit(solution)/shard_map/all_to_all | solution.py:131
  37.3 0.0 copy-start.4
  37.3 0.0 copy-done.1
  37.3 0.0 copy-done.2
  37.3 0.0 copy-done.3
  37.3 0.6 copy-done.4
  37.9 2.2 %inner.2 = (f32[8,3,48,128]{3,2,1,0:T(8,128)S(1)}, f32[8,3,48,128]{3,2,1,0:T(8,128)S(1)}) custom-call(f32[8]{0:T(128)S(1)} %copy-done.4, f32[8,3,48,128]{3,2,1,0:T(8,128)S(1)} %bitcast.10, f32[3,3,48,128]{3,2,1,0:T(8,128)S(1)} %copy-done.2, f32[3,3,48,128]{3,2,1,0:T(8,128)S(1)} %bitcast.15, f32[3,48,128]{2,1,0:T(8,128)S(1)} %copy-done.1), custom_call_target="tpu_custom_call" | custom-call | flops 1000000 | tf_op jit(solution)/shard_map/inner/pallas_call | solution.py:124
  40.2 1.7 %collective-permute-done.first_hbm = f32[8,3,48,128]{3,2,1,0:T(8,128)S(1)} collective-permute-done((f32[8,3,48,128]{3,2,1,0:T(8,128)S(1)}, f32[8,3,48,128]{3,2,1,0:T(8,128)S(1)}, u32[]{:S(2)}, u32[]{:S(2)}) %collective-permute-start) | collective-permute-done | bytes 589856 | tf_op jit(solution)/shard_map/ppermute | solution.py:146
  41.8 0.0 collective-permute-done.1.second_hbm
  41.8 1.5 %outer.2 = (f32[8,3,48,128]{3,2,1,0:T(8,128)S(1)}, f32[8,3,48,128]{3,2,1,0:T(8,128)S(1)}) custom-call(f32[8,3,48,128]{3,2,1,0:T(8,128)S(1)} %collective-permute-done.first_hbm, f32[8,3,48,128]{3,2,1,0:T(8,128)} %collective-permute-done.1.second_hbm, f32[8,3,48,128]{3,2,1,0:T(8,128)S(1)} %bitcast.11, ...), custom_call_target="tpu_custom_call", output_to_operand_aliasing={{0}: (3, {}), {1}: (4, {})} | custom-call | flops 10000000000 | tf_op jit(solution)/shard_map/outer/pallas_call | solution.py:133
  43.3 7.9 %all-to-all-done.1 = f32[16,9,8,128]{3,2,1,0:T(8,128)S(1)} async-done(((f32[16,9,8,128]{3,2,1,0:T(8,128)}), f32[16,9,8,128]{3,2,1,0:T(8,128)S(1)}, u32[]{:S(2)}, u32[]{:S(2)}) %all-to-all-start.1) | async-done | bytes 589856 | tf_op jit(solution)/shard_map/all_to_all | solution.py:131
  51.2 1.0 join.2.q_ref
  52.1 3.7 %all-to-all-start.2 = ((f32[16,9,8,128]{3,2,1,0:T(8,128)}), f32[16,9,8,128]{3,2,1,0:T(8,128)S(1)}, u32[]{:S(2)}, u32[]{:S(2)}) async-start(f32[16,9,8,128]{3,2,1,0:T(8,128)} %bitcast.4), calls=%async_computation.2 | async-start | bytes 1179648 | tf_op jit(solution)/shard_map/all_to_all | solution.py:129
  55.8 2.3 %collective-permute-start.2 = (f32[8,3,48,128]{3,2,1,0:T(8,128)}, f32[8,3,48,128]{3,2,1,0:T(8,128)S(1)}, u32[]{:S(2)}, u32[]{:S(2)}) collective-permute-start(f32[8,3,48,128]{3,2,1,0:T(8,128)} %join.2.q_ref), channel_id=1, source_target_pairs={{0,16},{32,48},{64,80},{96,112},{128,144},{160,176},{192,208},{224... | collective-permute-start | bytes 1769480 | tf_op jit(solution)/shard_map/ppermute | solution.py:146
  58.1 1.5 %collective-permute-start.3 = (f32[8,3,48,128]{3,2,1,0:T(8,128)}, f32[8,3,48,128]{3,2,1,0:T(8,128)}, u32[]{:S(2)}, u32[]{:S(2)}) collective-permute-start(f32[8,3,48,128]{3,2,1,0:T(8,128)} %join.2.q_ref), channel_id=1, source_target_pairs={{16,32},{48,64},{80,96},{112,128},{144,160},{176,192},{208,224},{2... | collective-permute-start | bytes 1769480 | tf_op jit(solution)/shard_map/ppermute | solution.py:146
  59.6 19.5 %all-to-all-done.2.parts_ref = f32[16,9,8,128]{3,2,1,0:T(8,128)S(1)} async-done(((f32[16,9,8,128]{3,2,1,0:T(8,128)}), f32[16,9,8,128]{3,2,1,0:T(8,128)S(1)}, u32[]{:S(2)}, u32[]{:S(2)}) %all-to-all-start.2) | async-done | bytes 589856 | tf_op jit(solution)/shard_map/all_to_all | solution.py:129
  79.1 0.9 spread.3
  80.0 3.6 %all-to-all-start.3 = ((f32[16,9,8,128]{3,2,1,0:T(8,128)}), f32[16,9,8,128]{3,2,1,0:T(8,128)S(1)}, u32[]{:S(2)}, u32[]{:S(2)}) async-start(f32[16,9,8,128]{3,2,1,0:T(8,128)} %spread.3), calls=%async_computation.3 | async-start | bytes 1179648 | tf_op jit(solution)/shard_map/all_to_all | solution.py:131
  83.7 2.7 %inner.3 = (f32[8,3,48,128]{3,2,1,0:T(8,128)S(1)}, f32[8,3,48,128]{3,2,1,0:T(8,128)S(1)}) custom-call(f32[8]{0:T(128)S(1)} %copy-done.4, f32[8,3,48,128]{3,2,1,0:T(8,128)} %join.2.q_ref, f32[3,3,48,128]{3,2,1,0:T(8,128)S(1)} %copy-done.2, f32[3,3,48,128]{3,2,1,0:T(8,128)S(1)} %bitcast.17, f32[3,48,128]{2,1,0:T(8,128)S(1)} %copy-done.1), custom_call_target="tpu_custom_call" | custom-call | flops 1000000 | tf_op jit(solution)/shard_map/inner/pallas_call | solution.py:124
  86.4 3.1 %collective-permute-done.2.first_hbm = f32[8,3,48,128]{3,2,1,0:T(8,128)S(1)} collective-permute-done((f32[8,3,48,128]{3,2,1,0:T(8,128)}, f32[8,3,48,128]{3,2,1,0:T(8,128)S(1)}, u32[]{:S(2)}, u32[]{:S(2)}) %collective-permute-start.2) | collective-permute-done | bytes 589856 | tf_op jit(solution)/shard_map/ppermute | solution.py:146
  89.6 0.0 collective-permute-done.3.second_hbm
  89.6 2.5 %outer.3 = (f32[8,3,48,128]{3,2,1,0:T(8,128)S(1)}, f32[8,3,48,128]{3,2,1,0:T(8,128)S(1)}) custom-call(f32[8,3,48,128]{3,2,1,0:T(8,128)S(1)} %collective-permute-done.2.first_hbm, f32[8,3,48,128]{3,2,1,0:T(8,128)} %collective-permute-done.3.second_hbm, f32[8,3,48,128]{3,2,1,0:T(8,128)} %join.2.q_ref, ...), custom_call_target="tpu_custom_call", output_to_operand_aliasing={{0}: (3, {}), {1}: (4, {})} | custom-call | flops 10000000000 | tf_op jit(solution)/shard_map/outer/pallas_call | solution.py:133
  92.1 5.5 %all-to-all-done.3 = f32[16,9,8,128]{3,2,1,0:T(8,128)S(1)} async-done(((f32[16,9,8,128]{3,2,1,0:T(8,128)}), f32[16,9,8,128]{3,2,1,0:T(8,128)S(1)}, u32[]{:S(2)}, u32[]{:S(2)}) %all-to-all-start.3) | async-done | bytes 589856 | tf_op jit(solution)/shard_map/all_to_all | solution.py:131
  97.6 1.1 %join.3 = f32[8,3,48,128]{3,2,1,0:T(8,128)} custom-call(f32[8,3,48,128]{3,2,1,0:T(8,128)S(1)} %get-tuple-element.19.base_ref, f32[8,3,48,128]{3,2,1,0:T(8,128)S(1)} %get-tuple-element.20.noise_ref, f32[3,48,128]{2,1,0:T(8,128)S(1)} %copy-done.1, f32[8,3,48,128]{3,2,1,0:T(8,128)S(1)} %bitcast.13, f32[8,3,48,128]{3,2,1,0:T(8,128)S(1)} %bitcast.12), custom_call_target="tpu_custom_call" | custom-call | tf_op jit(solution)/shard_map/join/pallas_call | solution.py:137
Async XLA Ops:
  0.0 9.4 %copy-start = (f32[1,8,3,48,128]{4,3,2,1,0:T(8,128)S(1)}, f32[1,8,3,48,128]{4,3,2,1,0:T(8,128)}, u32[]{:S(2)}) copy-start(f32[1,8,3,48,128]{4,3,2,1,0:T(8,128)} %param.5) | copy-start | bytes 1769476
  0.0 32.7 %all-to-all-start = ((f32[16,9,8,128]{3,2,1,0:T(8,128)}), f32[16,9,8,128]{3,2,1,0:T(8,128)S(1)}, u32[]{:S(2)}, u32[]{:S(2)}) async-start(f32[16,9,8,128]{3,2,1,0:T(8,128)} %bitcast.7), calls=%async_computation | async-start | bytes 1179648 | tf_op jit(solution)/shard_map/all_to_all | solution.py:129
  9.4 32.4 %collective-permute-start = (f32[8,3,48,128]{3,2,1,0:T(8,128)S(1)}, f32[8,3,48,128]{3,2,1,0:T(8,128)S(1)}, u32[]{:S(2)}, u32[]{:S(2)}) collective-permute-start(f32[8,3,48,128]{3,2,1,0:T(8,128)S(1)} %bitcast.8), channel_id=1, source_target_pairs={{0,16},{32,48},{64,80},{96,112},{128,144},{160,176},{192,208},{224... | collective-permute-start | bytes 1769480 | tf_op jit(solution)/shard_map/ppermute | solution.py:146
  11.3 30.5 %collective-permute-start.1 = (f32[8,3,48,128]{3,2,1,0:T(8,128)S(1)}, f32[8,3,48,128]{3,2,1,0:T(8,128)}, u32[]{:S(2)}, u32[]{:S(2)}) collective-permute-start(f32[8,3,48,128]{3,2,1,0:T(8,128)S(1)} %bitcast.9), channel_id=1, source_target_pairs={{16,32},{48,64},{80,96},{112,128},{144,160},{176,192},{208,224},{2... | collective-permute-start | bytes 1769480 | tf_op jit(solution)/shard_map/ppermute | solution.py:146
  33.5 3.8 %copy-start.1 = (f32[3,48,128]{2,1,0:T(8,128)S(1)}, f32[3,48,128]{2,1,0:T(8,128)}, u32[]{:S(2)}) copy-start(f32[3,48,128]{2,1,0:T(8,128)} %dif_ref.11) | copy-start | bytes 221188
  33.5 3.8 %copy-start.2 = (f32[3,3,48,128]{3,2,1,0:T(8,128)S(1)}, f32[3,3,48,128]{3,2,1,0:T(8,128)}, u32[]{:S(2)}) copy-start(f32[3,3,48,128]{3,2,1,0:T(8,128)} %vel_ref.7) | copy-start | bytes 663556
  33.5 3.8 %copy-start.3 = (f32[1,3,3,48,128]{4,3,2,1,0:T(8,128)S(1)}, f32[1,3,3,48,128]{4,3,2,1,0:T(8,128)}, u32[]{:S(2)}) copy-start(f32[1,3,3,48,128]{4,3,2,1,0:T(8,128)} %param.7) | copy-start | bytes 663556
  33.5 17.6 %all-to-all-start.1 = ((f32[16,9,8,128]{3,2,1,0:T(8,128)}), f32[16,9,8,128]{3,2,1,0:T(8,128)S(1)}, u32[]{:S(2)}, u32[]{:S(2)}) async-start(f32[16,9,8,128]{3,2,1,0:T(8,128)} %spread.2), calls=%async_computation.1 | async-start | bytes 1179648 | tf_op jit(solution)/shard_map/all_to_all | solution.py:131
  37.3 0.7 copy-start.4
  52.1 27.0 %all-to-all-start.2 = ((f32[16,9,8,128]{3,2,1,0:T(8,128)}), f32[16,9,8,128]{3,2,1,0:T(8,128)S(1)}, u32[]{:S(2)}, u32[]{:S(2)}) async-start(f32[16,9,8,128]{3,2,1,0:T(8,128)} %bitcast.4), calls=%async_computation.2 | async-start | bytes 1179648 | tf_op jit(solution)/shard_map/all_to_all | solution.py:129
  55.8 33.7 %collective-permute-start.2 = (f32[8,3,48,128]{3,2,1,0:T(8,128)}, f32[8,3,48,128]{3,2,1,0:T(8,128)S(1)}, u32[]{:S(2)}, u32[]{:S(2)}) collective-permute-start(f32[8,3,48,128]{3,2,1,0:T(8,128)} %join.2.q_ref), channel_id=1, source_target_pairs={{0,16},{32,48},{64,80},{96,112},{128,144},{160,176},{192,208},{224... | collective-permute-start | bytes 1769480 | tf_op jit(solution)/shard_map/ppermute | solution.py:146
  58.1 31.4 %collective-permute-start.3 = (f32[8,3,48,128]{3,2,1,0:T(8,128)}, f32[8,3,48,128]{3,2,1,0:T(8,128)}, u32[]{:S(2)}, u32[]{:S(2)}) collective-permute-start(f32[8,3,48,128]{3,2,1,0:T(8,128)} %join.2.q_ref), channel_id=1, source_target_pairs={{16,32},{48,64},{80,96},{112,128},{144,160},{176,192},{208,224},{2... | collective-permute-start | bytes 1769480 | tf_op jit(solution)/shard_map/ppermute | solution.py:146
  80.0 17.6 %all-to-all-start.3 = ((f32[16,9,8,128]{3,2,1,0:T(8,128)}), f32[16,9,8,128]{3,2,1,0:T(8,128)S(1)}, u32[]{:S(2)}, u32[]{:S(2)}) async-start(f32[16,9,8,128]{3,2,1,0:T(8,128)} %spread.3), calls=%async_computation.3 | async-start | bytes 1179648 | tf_op jit(solution)/shard_map/all_to_all | solution.py:131

commit v8 on v7

--- a/solution.py
+++ b/solution.py
@@ -130,7 +130,7 @@
     spread = call(spread_kernel, jax.ShapeDtypeStruct(shares.shape, q.dtype), [VMEM], [], 0, "spread")(received)
     total = lax.all_to_all(spread, "field", 0, 0).reshape(q.shape)
     scratch = [pltpu.VMEM((2,) + q.shape, jnp.float32)] + [pltpu.SemaphoreType.DMA((2, 2))]
-    base, noise = call(outer_kernel, (like, like), [HBM] * 2 + [VMEM] * 6, scratch, 10**10, "outer", {3: 0, 4: 1})(
+    base, noise = call(outer_kernel, (like, like), [HBM] * 2 + [VMEM] * 6, scratch, 2 * 10**10, "outer", {3: 0, 4: 1})(
         *halo, q, base, noise, velocity, wiener, diffusivity
     )
     args = (base, noise, diffusivity, total) + ((phi,) if last else ())

time: 99.4 us -> 99.4 us (level)
    ppermute x4, waiting for transfers between devices: 4.77 us -> 10.6 us  [swap(): lax.ppermute(q, ('space', 'field'), pairs + [(b, a) for a, b in pairs])]
    all_to_all x2, waiting for transfers between devices: 39.4 us -> 34.3 us  [section(): received = lax.all_to_all(shares, 'field', 0, 0)]
where the time goes in v8:
time: 99.4 us; the launch traced here: 98.7 us
  waiting for transfers between devices  58.3 us (59%)
  starting transfers between devices  27.6 us (28%)
  Pallas kernels  12.7 us (13%)
    all_to_all x2, waiting for transfers between devices, section(): received = lax.all_to_all(shares, 'field', 0, 0)  34.3 us
    all_to_all x2, waiting for transfers between devices, section(): total = lax.all_to_all(spread, 'field', 0, 0).reshape(q.shape)  13.4 us
    all_to_all x2, starting transfers between devices, section(): received = lax.all_to_all(shares, 'field', 0, 0)  13.1 us
    ppermute x4, waiting for transfers between devices, swap(): lax.ppermute(q, ('space', 'field'), pairs + [(b, a) for a, b in pairs])  10.6 us
    all_to_all x2, starting transfers between devices, section(): total = lax.all_to_all(spread, 'field', 0, 0).reshape(q.shape)  7.25 us
    ppermute x4, starting transfers between devices, swap(): lax.ppermute(q, ('space', 'field'), pairs + [(b, a) for a, b in pairs])  7.23 us
    pallas_call x2, Pallas kernels, section(): call(inner_kernel, (like, like), [SMEM] + [VMEM] * 4, [pltpu.VMEM(q.shape...  4.96 us
    pallas_call x2, Pallas kernels, section(): call(outer_kernel, (like, like), [HBM] * 2 + [VMEM] * 6, scratch, 2 * 10...  3.99 us
  transfers between devices with their start and end apart: 8, of which 6 were waited for; matrix products, arithmetic and copies ran while one was open for 0% of the time, Pallas kernels for 11%

profile of v8, /device:TPU:8, one launch (start us, length us, event | category | flops | bytes accessed | tf_op | source)
XLA Modules:
  0.0 98.7 jit_solution(1381467753118852197)
XLA Ops:
  0.0 0.0 copy-start
  0.0 0.0 copy-start.1
  0.0 0.0 copy-start.2
  0.0 0.0 copy-start.3
  0.0 9.4 %all-to-all-start = ((f32[16,9,8,128]{3,2,1,0:T(8,128)}), f32[16,9,8,128]{3,2,1,0:T(8,128)S(1)}, u32[]{:S(2)}, u32[]{:S(2)}) async-start(f32[16,9,8,128]{3,2,1,0:T(8,128)} %bitcast.7), calls=%async_computation | async-start | bytes 1179648 | tf_op jit(solution)/shard_map/all_to_all | solution.py:129
  9.4 0.0 copy-done
  9.4 0.0 copy-start.4
  9.4 1.9 %collective-permute-start = (f32[8,3,48,128]{3,2,1,0:T(8,128)S(1)}, f32[8,3,48,128]{3,2,1,0:T(8,128)S(1)}, u32[]{:S(2)}, u32[]{:S(2)}) collective-permute-start(f32[8,3,48,128]{3,2,1,0:T(8,128)S(1)} %bitcast.8), channel_id=1, source_target_pairs={{0,16},{32,48},{64,80},{96,112},{128,144},{160,176},{192,208},{224... | collective-permute-start | bytes 1769480 | tf_op jit(solution)/shard_map/ppermute | solution.py:146
  11.3 1.5 %collective-permute-start.1 = (f32[8,3,48,128]{3,2,1,0:T(8,128)S(1)}, f32[8,3,48,128]{3,2,1,0:T(8,128)}, u32[]{:S(2)}, u32[]{:S(2)}) collective-permute-start(f32[8,3,48,128]{3,2,1,0:T(8,128)S(1)} %bitcast.9), channel_id=1, source_target_pairs={{16,32},{48,64},{80,96},{112,128},{144,160},{176,192},{208,224},{2... | collective-permute-start | bytes 1769480 | tf_op jit(solution)/shard_map/ppermute | solution.py:146
  12.8 0.0 copy-done.1
  12.8 0.0 copy-done.2
  12.8 0.0 copy-done.3
  12.8 0.0 copy-done.4
  12.8 2.2 %inner.2 = (f32[8,3,48,128]{3,2,1,0:T(8,128)S(1)}, f32[8,3,48,128]{3,2,1,0:T(8,128)S(1)}) custom-call(f32[8]{0:T(128)S(1)} %copy-done.4, f32[8,3,48,128]{3,2,1,0:T(8,128)S(1)} %bitcast.10, f32[3,3,48,128]{3,2,1,0:T(8,128)S(1)} %copy-done.2, f32[3,3,48,128]{3,2,1,0:T(8,128)S(1)} %bitcast.15, f32[3,48,128]{2,1,0:T(8,128)S(1)} %copy-done.1), custom_call_target="tpu_custom_call" | custom-call | flops 1000000 | tf_op jit(solution)/shard_map/inner/pallas_call | solution.py:124
  15.1 17.6 %all-to-all-done.parts_ref = f32[16,9,8,128]{3,2,1,0:T(8,128)S(1)} async-done(((f32[16,9,8,128]{3,2,1,0:T(8,128)}), f32[16,9,8,128]{3,2,1,0:T(8,128)S(1)}, u32[]{:S(2)}, u32[]{:S(2)}) %all-to-all-start) | async-done | bytes 589856 | tf_op jit(solution)/shard_map/all_to_all | solution.py:129
  32.7 0.9 spread.2
  33.6 3.6 %all-to-all-start.1 = ((f32[16,9,8,128]{3,2,1,0:T(8,128)}), f32[16,9,8,128]{3,2,1,0:T(8,128)S(1)}, u32[]{:S(2)}, u32[]{:S(2)}) async-start(f32[16,9,8,128]{3,2,1,0:T(8,128)} %spread.2), calls=%async_computation.1 | async-start | bytes 1179648 | tf_op jit(solution)/shard_map/all_to_all | solution.py:131
  37.2 4.7 %collective-permute-done.first_hbm = f32[8,3,48,128]{3,2,1,0:T(8,128)S(1)} collective-permute-done((f32[8,3,48,128]{3,2,1,0:T(8,128)S(1)}, f32[8,3,48,128]{3,2,1,0:T(8,128)S(1)}, u32[]{:S(2)}, u32[]{:S(2)}) %collective-permute-start) | collective-permute-done | bytes 589856 | tf_op jit(solution)/shard_map/ppermute | solution.py:146
  41.8 0.0 collective-permute-done.1.second_hbm
  41.9 1.5 %outer.2 = (f32[8,3,48,128]{3,2,1,0:T(8,128)S(1)}, f32[8,3,48,128]{3,2,1,0:T(8,128)S(1)}) custom-call(f32[8,3,48,128]{3,2,1,0:T(8,128)S(1)} %collective-permute-done.first_hbm, f32[8,3,48,128]{3,2,1,0:T(8,128)} %collective-permute-done.1.second_hbm, f32[8,3,48,128]{3,2,1,0:T(8,128)S(1)} %bitcast.11, ...), custom_call_target="tpu_custom_call", output_to_operand_aliasing={{0}: (3, {}), {1}: (4, {})} | custom-call | flops 20000000000 | tf_op jit(solution)/shard_map/outer/pallas_call | solution.py:133
  43.3 7.8 %all-to-all-done.1 = f32[16,9,8,128]{3,2,1,0:T(8,128)S(1)} async-done(((f32[16,9,8,128]{3,2,1,0:T(8,128)}), f32[16,9,8,128]{3,2,1,0:T(8,128)S(1)}, u32[]{:S(2)}, u32[]{:S(2)}) %all-to-all-start.1) | async-done | bytes 589856 | tf_op jit(solution)/shard_map/all_to_all | solution.py:131
  51.2 1.0 join.2.q_ref
  52.1 3.7 %all-to-all-start.2 = ((f32[16,9,8,128]{3,2,1,0:T(8,128)}), f32[16,9,8,128]{3,2,1,0:T(8,128)S(1)}, u32[]{:S(2)}, u32[]{:S(2)}) async-start(f32[16,9,8,128]{3,2,1,0:T(8,128)} %bitcast.4), calls=%async_computation.2 | async-start | bytes 1179648 | tf_op jit(solution)/shard_map/all_to_all | solution.py:129
  55.9 2.3 %collective-permute-start.2 = (f32[8,3,48,128]{3,2,1,0:T(8,128)}, f32[8,3,48,128]{3,2,1,0:T(8,128)S(1)}, u32[]{:S(2)}, u32[]{:S(2)}) collective-permute-start(f32[8,3,48,128]{3,2,1,0:T(8,128)} %join.2.q_ref), channel_id=1, source_target_pairs={{0,16},{32,48},{64,80},{96,112},{128,144},{160,176},{192,208},{224... | collective-permute-start | bytes 1769480 | tf_op jit(solution)/shard_map/ppermute | solution.py:146
  58.2 1.5 %collective-permute-start.3 = (f32[8,3,48,128]{3,2,1,0:T(8,128)}, f32[8,3,48,128]{3,2,1,0:T(8,128)}, u32[]{:S(2)}, u32[]{:S(2)}) collective-permute-start(f32[8,3,48,128]{3,2,1,0:T(8,128)} %join.2.q_ref), channel_id=1, source_target_pairs={{16,32},{48,64},{80,96},{112,128},{144,160},{176,192},{208,224},{2... | collective-permute-start | bytes 1769480 | tf_op jit(solution)/shard_map/ppermute | solution.py:146
  59.7 2.7 %inner.3 = (f32[8,3,48,128]{3,2,1,0:T(8,128)S(1)}, f32[8,3,48,128]{3,2,1,0:T(8,128)S(1)}) custom-call(f32[8]{0:T(128)S(1)} %copy-done.4, f32[8,3,48,128]{3,2,1,0:T(8,128)} %join.2.q_ref, f32[3,3,48,128]{3,2,1,0:T(8,128)S(1)} %copy-done.2, f32[3,3,48,128]{3,2,1,0:T(8,128)S(1)} %bitcast.17, f32[3,48,128]{2,1,0:T(8,128)S(1)} %copy-done.1), custom_call_target="tpu_custom_call" | custom-call | flops 1000000 | tf_op jit(solution)/shard_map/inner/pallas_call | solution.py:124
  62.4 16.7 %all-to-all-done.2.parts_ref = f32[16,9,8,128]{3,2,1,0:T(8,128)S(1)} async-done(((f32[16,9,8,128]{3,2,1,0:T(8,128)}), f32[16,9,8,128]{3,2,1,0:T(8,128)S(1)}, u32[]{:S(2)}, u32[]{:S(2)}) %all-to-all-start.2) | async-done | bytes 589856 | tf_op jit(solution)/shard_map/all_to_all | solution.py:129
  79.2 0.9 spread.3
  80.1 3.6 %all-to-all-start.3 = ((f32[16,9,8,128]{3,2,1,0:T(8,128)}), f32[16,9,8,128]{3,2,1,0:T(8,128)S(1)}, u32[]{:S(2)}, u32[]{:S(2)}) async-start(f32[16,9,8,128]{3,2,1,0:T(8,128)} %spread.3), calls=%async_computation.3 | async-start | bytes 1179648 | tf_op jit(solution)/shard_map/all_to_all | solution.py:131
  83.7 5.9 %collective-permute-done.2.first_hbm = f32[8,3,48,128]{3,2,1,0:T(8,128)S(1)} collective-permute-done((f32[8,3,48,128]{3,2,1,0:T(8,128)}, f32[8,3,48,128]{3,2,1,0:T(8,128)S(1)}, u32[]{:S(2)}, u32[]{:S(2)}) %collective-permute-start.2) | collective-permute-done | bytes 589856 | tf_op jit(solution)/shard_map/ppermute | solution.py:146
  89.6 0.0 collective-permute-done.3.second_hbm
  89.6 2.5 %outer.3 = (f32[8,3,48,128]{3,2,1,0:T(8,128)S(1)}, f32[8,3,48,128]{3,2,1,0:T(8,128)S(1)}) custom-call(f32[8,3,48,128]{3,2,1,0:T(8,128)S(1)} %collective-permute-done.2.first_hbm, f32[8,3,48,128]{3,2,1,0:T(8,128)} %collective-permute-done.3.second_hbm, f32[8,3,48,128]{3,2,1,0:T(8,128)} %join.2.q_ref, ...), custom_call_target="tpu_custom_call", output_to_operand_aliasing={{0}: (3, {}), {1}: (4, {})} | custom-call | flops 20000000000 | tf_op jit(solution)/shard_map/outer/pallas_call | solution.py:133
  92.1 5.5 %all-to-all-done.3 = f32[16,9,8,128]{3,2,1,0:T(8,128)S(1)} async-done(((f32[16,9,8,128]{3,2,1,0:T(8,128)}), f32[16,9,8,128]{3,2,1,0:T(8,128)S(1)}, u32[]{:S(2)}, u32[]{:S(2)}) %all-to-all-start.3) | async-done | bytes 589856 | tf_op jit(solution)/shard_map/all_to_all | solution.py:131
  97.6 1.1 %join.3 = f32[8,3,48,128]{3,2,1,0:T(8,128)} custom-call(f32[8,3,48,128]{3,2,1,0:T(8,128)S(1)} %get-tuple-element.19.base_ref, f32[8,3,48,128]{3,2,1,0:T(8,128)S(1)} %get-tuple-element.20.noise_ref, f32[3,48,128]{2,1,0:T(8,128)S(1)} %copy-done.1, f32[8,3,48,128]{3,2,1,0:T(8,128)S(1)} %bitcast.13, f32[8,3,48,128]{3,2,1,0:T(8,128)S(1)} %bitcast.12), custom_call_target="tpu_custom_call" | custom-call | tf_op jit(solution)/shard_map/join/pallas_call | solution.py:137
Async XLA Ops:
  0.0 9.4 %copy-start = (f32[1,8,3,48,128]{4,3,2,1,0:T(8,128)S(1)}, f32[1,8,3,48,128]{4,3,2,1,0:T(8,128)}, u32[]{:S(2)}) copy-start(f32[1,8,3,48,128]{4,3,2,1,0:T(8,128)} %param.5) | copy-start | bytes 1769476
  0.0 12.8 %copy-start.1 = (f32[3,48,128]{2,1,0:T(8,128)S(1)}, f32[3,48,128]{2,1,0:T(8,128)}, u32[]{:S(2)}) copy-start(f32[3,48,128]{2,1,0:T(8,128)} %dif_ref.11) | copy-start | bytes 221188
  0.0 12.8 %copy-start.2 = (f32[3,3,48,128]{3,2,1,0:T(8,128)S(1)}, f32[3,3,48,128]{3,2,1,0:T(8,128)}, u32[]{:S(2)}) copy-start(f32[3,3,48,128]{3,2,1,0:T(8,128)} %vel_ref.7) | copy-start | bytes 663556
  0.0 12.8 %copy-start.3 = (f32[1,3,3,48,128]{4,3,2,1,0:T(8,128)S(1)}, f32[1,3,3,48,128]{4,3,2,1,0:T(8,128)}, u32[]{:S(2)}) copy-start(f32[1,3,3,48,128]{4,3,2,1,0:T(8,128)} %param.7) | copy-start | bytes 663556
  0.0 32.7 %all-to-all-start = ((f32[16,9,8,128]{3,2,1,0:T(8,128)}), f32[16,9,8,128]{3,2,1,0:T(8,128)S(1)}, u32[]{:S(2)}, u32[]{:S(2)}) async-start(f32[16,9,8,128]{3,2,1,0:T(8,128)} %bitcast.7), calls=%async_computation | async-start | bytes 1179648 | tf_op jit(solution)/shard_map/all_to_all | solution.py:129
  9.4 3.4 %copy-start.4 = (f32[8]{0:T(128)S(1)}, f32[8]{0:T(128)}, u32[]{:S(2)}) copy-start(f32[8]{0:T(128)} %stoich_ref.3) | copy-start | bytes 100
  9.4 32.4 %collective-permute-start = (f32[8,3,48,128]{3,2,1,0:T(8,128)S(1)}, f32[8,3,48,128]{3,2,1,0:T(8,128)S(1)}, u32[]{:S(2)}, u32[]{:S(2)}) collective-permute-start(f32[8,3,48,128]{3,2,1,0:T(8,128)S(1)} %bitcast.8), channel_id=1, source_target_pairs={{0,16},{32,48},{64,80},{96,112},{128,144},{160,176},{192,208},{224... | collective-permute-start | bytes 1769480 | tf_op jit(solution)/shard_map/ppermute | solution.py:146
  11.3 30.5 %collective-permute-start.1 = (f32[8,3,48,128]{3,2,1,0:T(8,128)S(1)}, f32[8,3,48,128]{3,2,1,0:T(8,128)}, u32[]{:S(2)}, u32[]{:S(2)}) collective-permute-start(f32[8,3,48,128]{3,2,1,0:T(8,128)S(1)} %bitcast.9), channel_id=1, source_target_pairs={{16,32},{48,64},{80,96},{112,128},{144,160},{176,192},{208,224},{2... | collective-permute-start | bytes 1769480 | tf_op jit(solution)/shard_map/ppermute | solution.py:146
  33.6 17.6 %all-to-all-start.1 = ((f32[16,9,8,128]{3,2,1,0:T(8,128)}), f32[16,9,8,128]{3,2,1,0:T(8,128)S(1)}, u32[]{:S(2)}, u32[]{:S(2)}) async-start(f32[16,9,8,128]{3,2,1,0:T(8,128)} %spread.2), calls=%async_computation.1 | async-start | bytes 1179648 | tf_op jit(solution)/shard_map/all_to_all | solution.py:131
  52.1 27.0 %all-to-all-start.2 = ((f32[16,9,8,128]{3,2,1,0:T(8,128)}), f32[16,9,8,128]{3,2,1,0:T(8,128)S(1)}, u32[]{:S(2)}, u32[]{:S(2)}) async-start(f32[16,9,8,128]{3,2,1,0:T(8,128)} %bitcast.4), calls=%async_computation.2 | async-start | bytes 1179648 | tf_op jit(solution)/shard_map/all_to_all | solution.py:129
  55.9 33.7 %collective-permute-start.2 = (f32[8,3,48,128]{3,2,1,0:T(8,128)}, f32[8,3,48,128]{3,2,1,0:T(8,128)S(1)}, u32[]{:S(2)}, u32[]{:S(2)}) collective-permute-start(f32[8,3,48,128]{3,2,1,0:T(8,128)} %join.2.q_ref), channel_id=1, source_target_pairs={{0,16},{32,48},{64,80},{96,112},{128,144},{160,176},{192,208},{224... | collective-permute-start | bytes 1769480 | tf_op jit(solution)/shard_map/ppermute | solution.py:146
  58.2 31.4 %collective-permute-start.3 = (f32[8,3,48,128]{3,2,1,0:T(8,128)}, f32[8,3,48,128]{3,2,1,0:T(8,128)}, u32[]{:S(2)}, u32[]{:S(2)}) collective-permute-start(f32[8,3,48,128]{3,2,1,0:T(8,128)} %join.2.q_ref), channel_id=1, source_target_pairs={{16,32},{48,64},{80,96},{112,128},{144,160},{176,192},{208,224},{2... | collective-permute-start | bytes 1769480 | tf_op jit(solution)/shard_map/ppermute | solution.py:146
  80.1 17.6 %all-to-all-start.3 = ((f32[16,9,8,128]{3,2,1,0:T(8,128)}), f32[16,9,8,128]{3,2,1,0:T(8,128)S(1)}, u32[]{:S(2)}, u32[]{:S(2)}) async-start(f32[16,9,8,128]{3,2,1,0:T(8,128)} %spread.3), calls=%async_computation.3 | async-start | bytes 1179648 | tf_op jit(solution)/shard_map/all_to_all | solution.py:131
